TPU v7x, 256 devices: a whole 4x4x8 slice. The times are simulated.
256 devices in a mesh: band: 8 (over x, core), freq: 32 (over z, y).
Axes of the slice: x: 4, y: 4, z: 8, core: 2. Of those that a mesh axis runs over, the one named last changes fastest.
Arguments:
- samples: float32 [4096, 16384], P('band', 'freq'), may hold values from -6 to 6
- channel_delay: int32 [4096, 64], P('band'), may hold values from 0 to 4095
- merge_slope: int32 [15], replicated, may hold values from 16 to 1023
- tap_offset: int32 [32, 16], replicated, may hold values from -32 to 32, as said below
- tap_weight: float32 [32, 16], replicated, may hold values from -1.5 to 1.5
Outputs:
- best_power: float32 [1024, 8192], P('band', 'freq')
Inputs may be any that keep to these rules, and one draw needn't show every extreme that they name: `tap_offset`: in every draw some template has a tap at offset -32 and some template has one at 32.
All inputs are finite; a program needn't handle non-finite values.
Results may differ from a plain program's by a relative error of at most 0.0003.
Values sent between devices are 32-bit elements; how exact they have to be, the bound alone decides.
No kernel may reach another device: no remote copies, remote signals or barrier semaphores. Data moves between devices by JAX's collectives and lax.ppermute only.
A program may use at most 128 MiB of HBM per device.

v0:
```python
import math

import jax
import jax.numpy as jnp
import numpy as np
from jax import lax
from jax.experimental import pallas as pl
from jax.experimental.pallas import tpu as pltpu
from jax.sharding import PartitionSpec as P

REACH = 32
LANES = 128
ROOT = 64
D_BLOCK = 32

two_pi = 2.0 * math.pi
top_precision = lax.Precision.HIGHEST
f32 = jnp.float32
bf16 = jnp.bfloat16


def turning(count, modulus):
    angle = (count % modulus).astype(f32) * (two_pi / modulus)
    return (jnp.cos(angle), jnp.sin(angle))


def rotate(real, imag, cosine, sine_part):
    return (real * cosine + imag * sine_part, imag * cosine - real * sine_part)


def pick_entry(table, index):
    return jnp.sum(jnp.where(lax.iota(jnp.int32, table.shape[0]) == index, table, 0))


def split_bf16(value):
    high = value.astype(bf16)
    return high, (value - high.astype(f32)).astype(bf16)


def transform(blocks, length):
    sources, rows, samp = blocks.shape
    inner = length // LANES
    grid = blocks.transpose(1, 0, 2).reshape(rows, inner, LANES)
    index = lax.iota(jnp.int32, LANES)
    cos_first, sin_first = turning(index[:, None] * index[None, :], inner)
    part_re = jnp.einsum("cab,ak->ckb", grid, cos_first, precision=top_precision)
    part_im = -jnp.einsum("cab,ak->ckb", grid, sin_first, precision=top_precision)
    cos_twist, sin_twist = turning(index[:, None] * index[None, :], length)
    part_re, part_im = rotate(part_re, part_im, cos_twist, sin_twist)
    column = lax.iota(jnp.int32, LANES)
    kept = column // 4 * 2 + column % 2
    imag_col = (column // 2 % 2 == 1)[None, :]
    cos_second, sin_second = turning(index[:, None] * kept[None, :], LANES)
    scale = 1.0 / math.sqrt(length) / 16.0 / 4.0
    from_re = jnp.where(imag_col, -sin_second, cos_second) * scale
    from_im = jnp.where(imag_col, cos_second, sin_second) * scale
    both = jnp.concatenate([part_re, part_im], axis=2)
    out = jnp.einsum(
        "ckb,bm->cmk", both, jnp.concatenate([from_re, from_im], axis=0), precision=top_precision
    )
    slabs = LANES // 4
    return out.reshape(rows, slabs, 4, LANES).transpose(1, 0, 2, 3).reshape(slabs, rows * 4, LANES)


def base_tiles(first_bin, length):
    row = np.arange(4 * ROOT * 8)
    kind, step, sub_row = row // (ROOT * 8), row % (ROOT * 8) // 8, row % 8
    q = length // 4
    turns = np.array([[0, 3 * q, q, 0], [q, 0, 2 * q, q], [0] * 4, [3 * q] * 4])
    offset = turns[kind, sub_row // 2].astype(np.int32)
    shift = np.where(kind < 2, ROOT * step, step).astype(np.int32)
    half = (sub_row % 2 * LANES).astype(np.int32)
    bins = first_bin + half[:, None] + lax.iota(jnp.int32, LANES)[None, :]
    return turning(bins * shift[:, None] + offset[:, None], length)[0]


def sub_kernel(delay_ref, spec_ref, base_ref, tw_ref, out_ref, table, sums):
    group = 8

    def fill(block, carry):
        first = [base_ref[pl.ds((block * group + i) * 8, 8), :] for i in range(group)]
        second = [base_ref[pl.ds((ROOT + block * group + i) * 8, 8), :] for i in range(group)]

        def inner(q, c):
            cos_q = base_ref[pl.ds((2 * ROOT + q) * 8, 8), :]
            sin_q = base_ref[pl.ds((3 * ROOT + q) * 8, 8), :]
            for i in range(group):
                table[(block * group + i) * ROOT + q] = first[i] * cos_q + second[i] * sin_q
            return c

        return lax.fori_loop(0, ROOT, inner, carry, unroll=4)

    lax.fori_loop(0, ROOT // group, fill, 0)

    channels = spec_ref.shape[0] // 4
    per_sub = channels // 2
    delays = delay_ref.shape[0] // channels
    low_rows = lax.broadcasted_iota(jnp.int32, (8, LANES), 0) < 4
    for sb in range(2):
        for db in range(delays // D_BLOCK):

            def body(pair, accs):
                accs = list(accs)
                chan = sb * per_sub + 2 * pair
                tile = spec_ref[pl.ds(pl.multiple_of(chan * 4, 8), 8), :]
                turned = pltpu.roll(tile, 4, 0)
                start = chan * delays + db * D_BLOCK
                for j, mine in enumerate(
                    (jnp.where(low_rows, tile, turned), jnp.where(low_rows, turned, tile))
                ):
                    for d in range(D_BLOCK):
                        accs[d] = accs[d] + mine * table[delay_ref[start + j * delays + d]]
                return tuple(accs)

            zero = jnp.zeros((8, LANES), f32)
            accs = lax.fori_loop(0, per_sub // 2, body, (zero,) * D_BLOCK)
            for d in range(D_BLOCK):
                whole = accs[d] + pltpu.roll(accs[d], 6, 0)
                at = sb * delays + db * D_BLOCK + d
                sums[0, at : at + 1, 0:LANES] = whole[0:1]
                sums[0, at : at + 1, LANES:] = whole[1:2]
                sums[1, at : at + 1, 0:LANES] = whole[4:5]
                sums[1, at : at + 1, LANES:] = whole[5:6]

    re = sums[0].T
    im = sums[1].T
    re_turn = pltpu.roll(re, delays, 1)
    im_turn = pltpu.roll(im, delays, 1)
    left = lax.broadcasted_iota(jnp.int32, re.shape, 1) < delays
    up_re, up_im = rotate(
        jnp.where(left, re_turn, re), jnp.where(left, im_turn, im), tw_ref[0], tw_ref[1]
    )
    out_ref[0] = jnp.where(left, re, re_turn) + up_re
    out_ref[1] = jnp.where(left, im, im_turn) + up_im


def toeplitz_kernel(profile_ref, high_ref, low_ref):
    def body(a, carry):
        row = profile_ref[pl.ds(a, 1), :]
        wide = jnp.broadcast_to(row, (LANES, row.shape[1]))
        band = pltpu.roll(wide, 0, 1, stride=1, stride_axis=0)
        high, low = split_bf16(band)
        at = pl.ds(pl.multiple_of(a * LANES, LANES), LANES)
        high_ref[at, :] = high
        low_ref[at, :] = low
        return carry

    lax.fori_loop(0, profile_ref.shape[0], body, 0)


def corr_kernel(left_ref, mid_ref, right_ref, high_ref, low_ref, out_ref, ext):
    bins = mid_ref.shape[1]
    for x in range(2):
        cols = slice(x * LANES, (x + 1) * LANES)
        ext[0:REACH, cols] = left_ref[x]
        ext[REACH : REACH + bins, cols] = mid_ref[x]
        ext[REACH + bins : bins + 2 * REACH, cols] = right_ref[x]
        ext[bins + 2 * REACH :, cols] = jnp.zeros((ext.shape[0] - bins - 2 * REACH, LANES), f32)
    per = 4
    templates = high_ref.shape[0] // LANES
    for kb in range(bins // LANES):
        win_high, win_low = split_bf16(ext[kb * LANES : kb * LANES + 2 * LANES, :])

        def body(step, best):
            at = pl.ds(pl.multiple_of(step * per * LANES, LANES), per * LANES)
            high = high_ref[at, :]
            low = low_ref[at, :]
            got = (
                jnp.dot(high, win_high, preferred_element_type=f32)
                + jnp.dot(high, win_low, preferred_element_type=f32)
                + jnp.dot(low, win_high, preferred_element_type=f32)
            )
            for i in range(per):
                re = got[i * LANES : (i + 1) * LANES, :LANES]
                im = got[i * LANES : (i + 1) * LANES, LANES:]
                best = jnp.maximum(best, re * re + im * im)
            return best

        best = lax.fori_loop(0, templates // per, body, jnp.zeros((LANES, LANES), f32))
        out_ref[:, kb * LANES : (kb + 1) * LANES] = best.T


def per_device(samples, channel_delay, merge_slope, tap_offset, tap_weight):
    freq_count = lax.axis_size("freq")
    band_count = lax.axis_size("band")
    band_pos = lax.axis_index("band")
    freq_pos = lax.axis_index("freq")
    chan_dev, samp_dev = samples.shape
    length = samp_dev * freq_count
    bins_dev = length // 2 // freq_count
    delays_sub = channel_delay.shape[1]
    block = 2 * delays_sub
    vmem = pl.BlockSpec(memory_space=pltpu.VMEM)
    smem = pl.BlockSpec(memory_space=pltpu.SMEM)

    first_bin = freq_pos * bins_dev
    base = base_tiles(first_bin, length)
    bins_index = first_bin + lax.iota(jnp.int32, bins_dev)
    sections = band_count.bit_length()
    shifts = []
    for s in range(sections):
        size = 1 << s
        slope = pick_entry(merge_slope, band_pos // size * (2 * size) + size - 1)
        out_index = band_pos % size * block + lax.iota(jnp.int32, block)
        shifts.append(out_index * slope // 16 % length)
    turn_cos, turn_sin = turning(
        jnp.stack(shifts)[:, None, :] * bins_index[None, :, None], length
    )
    turns = jnp.stack([turn_cos, turn_sin], axis=1)
    window = 2 * LANES
    matches = tap_offset[:, :, None] + REACH == lax.iota(jnp.int32, window)[None, None, :]
    profile = jnp.sum(jnp.where(matches, tap_weight[:, :, None], 0.0), axis=1)
    templates = profile.shape[0]
    band_shape = jax.ShapeDtypeStruct((templates * LANES, window), bf16)
    high, low = pl.pallas_call(
        toeplitz_kernel,
        out_shape=(band_shape, band_shape),
        in_specs=[vmem],
        out_specs=(vmem, vmem),
        name="toeplitz",
    )(profile)

    blocks = samples.reshape(freq_count, chan_dev // freq_count, samp_dev)
    blocks = lax.all_to_all(blocks, "freq", split_axis=0, concat_axis=0, tiled=True)
    spec = transform(blocks, length)
    spec = lax.all_to_all(spec, "freq", split_axis=0, concat_axis=0, tiled=True)
    spec = spec.reshape(chan_dev * 4, LANES)

    current = pl.pallas_call(
        sub_kernel,
        out_shape=jax.ShapeDtypeStruct((2, bins_dev, block), f32),
        in_specs=[smem, vmem, vmem, vmem],
        out_specs=vmem,
        scratch_shapes=[
            pltpu.VMEM((ROOT * ROOT, 8, LANES), f32),
            pltpu.VMEM((2, block, bins_dev), f32),
        ],
        compiler_params=pltpu.CompilerParams(vmem_limit_bytes=40 * 2**20),
        name="subband",
    )(channel_delay.reshape(-1), spec, base, turns[0])

    for s in range(1, sections):
        half = 1 << (s - 1)
        partner = lax.ppermute(current, "band", [(i, i ^ half) for i in range(band_count)])
        upper_side = band_pos % (2 * half) >= half
        lower = jnp.where(upper_side, partner, current)
        upper = jnp.where(upper_side, current, partner)
        up_re, up_im = rotate(upper[0], upper[1], turns[s, 0], turns[s, 1])
        current = jnp.stack([lower[0] + up_re, lower[1] + up_im])

    ends = freq_count - 1
    from_left = lax.ppermute(
        current[:, bins_dev - REACH :], "freq", [(i, i + 1) for i in range(ends)]
    )
    from_right = lax.ppermute(current[:, :REACH], "freq", [(i + 1, i) for i in range(ends)])
    return pl.pallas_call(
        corr_kernel,
        out_shape=jax.ShapeDtypeStruct((block, bins_dev), f32),
        in_specs=[vmem] * 5,
        out_specs=vmem,
        scratch_shapes=[pltpu.VMEM((bins_dev + LANES, 2 * LANES), f32)],
        compiler_params=pltpu.CompilerParams(vmem_limit_bytes=40 * 2**20),
        name="templates",
    )(from_left, current, from_right, high, low)


def solution(mesh):
    placed = (P("band", "freq"), P("band", None), P(), P(), P())
    return jax.shard_map(
        per_device, mesh=mesh, in_specs=placed, out_specs=P("band", "freq"), check_vma=False
    )
```

profile of v0, /device:TPU:32, one launch (start us, length us, event | category | flops | bytes accessed | tf_op | source)
XLA Modules:
  0.0 168.9 jit_solution(1472732187547374966)
XLA Ops:
  0.0 11.4 %all-to-all-start = ((f32[32,16,512]{2,1,0:T(8,128)}), f32[32,16,512]{2,1,0:T(8,128)S(1)}, u32[]{:S(2)}, u32[]{:S(2)}) async-start(f32[32,16,512]{2,1,0:T(8,128)} %bitcast.35), calls=%async_computation | async-start | bytes 2097152 | tf_op jit(solution)/shard_map/all_to_all | solution.py:224
  11.4 0.3 fusion.44
  11.7 0.3 select_multiply_fusion.1
  12.0 26.6 %all-to-all-done = f32[32,16,512]{2,1,0:T(8,128)S(1)} async-done(((f32[32,16,512]{2,1,0:T(8,128)}), f32[32,16,512]{2,1,0:T(8,128)S(1)}, u32[]{:S(2)}, u32[]{:S(2)}) %all-to-all-start) | async-done | bytes 1048608 | tf_op jit(solution)/shard_map/all_to_all | solution.py:224
  38.6 0.6 copy.36
  39.2 0.1 reshape.518
  39.3 0.3 copy.38
  39.7 1.2 fusion.30
  40.9 1.2 fusion.28
  42.2 0.3 add_bitcast_fusion
  42.5 1.2 fusion
  43.7 0.0 copy-start.2
  43.8 0.0 copy-start.8
  43.8 1.3 copy.42
  45.0 6.4 %all-to-all-start.1 = ((f32[32,64,128]{2,1,0:T(8,128)}), f32[32,64,128]{2,1,0:T(8,128)S(1)}, u32[]{:S(2)}, u32[]{:S(2)}) async-start(f32[32,64,128]{2,1,0:T(8,128)} %bitcast.14), calls=%async_computation.1 | async-start | bytes 2097152 | tf_op jit(solution)/shard_map/all_to_all | solution.py:226
  51.4 0.0 copy-start.7
  51.4 0.0 copy-start.3
  51.4 0.0 copy-start.4
  51.5 0.1 copy.35
  51.7 0.1 reshape.516.delay_ref
  51.8 0.7 fusion.53
  52.5 1.3 and_select_fusion.4
  53.8 1.2 and_select_fusion
  55.0 2.1 %fusion.18 = (f32[4,1,256,128]{3,2,1,0:T(8,128)S(1)}, f32[4,1,256,128]{3,2,1,0:T(8,128)S(1)}) fusion(s32[256]{0:T(256)S(1)} %iota_add_fusion, s32[4,128]{1,0:T(4,128)S(1)} %pad_add_fusion), kind=kLoop, calls=%fused_computation.43 | loop fusion | flops 1835008 | bytes 1051648 | tf_op jit(solution)/shard_map/cos | solution.py:24
  57.2 3.9 %fusion.7.base_ref = f32[2048,128]{1,0:T(8,128)S(1)} fusion(s32[2048]{0:T(1024)S(1)} %copy-done.4, s32[2048]{0:T(1024)S(1)} %copy-done.3, s32[2048]{0:T(1024)S(1)} %bitcast.36), kind=kLoop, calls=%fused_computation.10 | loop fusion | flops 4194304 | bytes 1073152 | tf_op jit(solution)/shard_map/cos | solution.py:24
  61.1 16.8 %all-to-all-done.1 = f32[32,64,128]{2,1,0:T(8,128)S(1)} async-done(((f32[32,64,128]{2,1,0:T(8,128)}), f32[32,64,128]{2,1,0:T(8,128)S(1)}, u32[]{:S(2)}, u32[]{:S(2)}) %all-to-all-start.1) | async-done | bytes 1048608 | tf_op jit(solution)/shard_map/all_to_all | solution.py:226
  77.9 51.1 %subband.1 = f32[2,256,128]{2,1,0:T(8,128)S(1)} custom-call(s32[32768]{0:T(1024)S(1)} %reshape.516.delay_ref, f32[2048,128]{1,0:T(8,128)S(1)} %bitcast.28, f32[2048,128]{1,0:T(8,128)S(1)} %fusion.7.base_ref, f32[2,256,128]{2,1,0:T(8,128)S(1)} %fusion.14.tw_ref), custom_call_target="tpu_custom_call" | custom-call | tf_op jit(solution)/shard_map/subband/pallas_call | solution.py:229
  129.0 0.1 collective-permute-start
  129.1 2.1 %fusion.16 = (f32[4,256,128]{2,1,0:T(8,128)S(1)}, f32[4,256,128]{2,1,0:T(8,128)S(1)}) fusion(s32[256]{0:T(256)S(1)} %iota_add_fusion, s32[4,128]{1,0:T(4,128)S(1)} %pad_add_fusion), kind=kLoop, calls=%fused_computation.41 | loop fusion | flops 1835008 | bytes 1051648 | tf_op jit(solution)/shard_map/cos | solution.py:24
  131.2 0.0 collective-permute-done
  131.3 0.0 copy-start.6
  131.3 0.0 copy-start.5
  131.3 0.1 slice_add_fusion.5
  131.4 1.6 collective-permute-start.1
  133.0 7.2 %collective-permute-done.1 = f32[2,256,128]{2,1,0:T(8,128)S(1)} collective-permute-done((f32[2,256,128]{2,1,0:T(8,128)S(1)}, f32[2,256,128]{2,1,0:T(8,128)S(1)}, u32[]{:S(2)}, u32[]{:S(2)}) %collective-permute-start.1) | collective-permute-done | bytes 262176 | tf_op jit(solution)/shard_map/ppermute | solution.py:244
  140.2 0.1 slice_add_fusion.3
  140.3 3.1 %collective-permute-start.2 = (f32[2,256,128]{2,1,0:T(8,128)S(1)}, f32[2,256,128]{2,1,0:T(8,128)S(1)}, u32[]{:S(2)}, u32[]{:S(2)}) collective-permute-start(f32[2,256,128]{2,1,0:T(8,128)S(1)} %pad_maximum_fusion.3), channel_id=1, source_target_pairs={{0,128},{32,160},{64,192},{96,224},{128,0},{160,32},{192,64},{224,... | collective-permute-start | bytes 786440 | tf_op jit(solution)/shard_map/ppermute | solution.py:244
  143.4 0.1 copy.43
  143.5 0.1 copy.44
  143.6 0.9 select_reduce_fusion.profile_ref
  144.5 6.1 %toeplitz.1 = (bf16[4096,256]{1,0:T(8,128)(2,1)}, bf16[4096,256]{1,0:T(8,128)(2,1)}) custom-call(f32[32,256]{1,0:T(8,128)} %select_reduce_fusion.profile_ref), custom_call_target="tpu_custom_call" | custom-call | tf_op jit(solution)/shard_map/toeplitz/pallas_call | solution.py:215
  150.6 0.0 collective-permute-done.2
  150.7 3.2 %collective-permute-start.3 = (f32[2,32,128]{2,1,0:T(8,128)S(1)}, f32[2,32,128]{2,1,0:T(8,128)S(1)}, u32[]{:S(2)}, u32[]{:S(2)}) collective-permute-start(f32[2,32,128]{2,1,0:T(8,128)S(1)} %get-tuple-element.28), channel_id=1, source_target_pairs={{0,1},{1,2},{2,3},{3,4},{4,5},{5,6},{6,7},{7,8},{8,9},{9,10},{10,1... | collective-permute-start | bytes 98312 | tf_op jit(solution)/shard_map/ppermute | solution.py:252
  153.9 4.9 %collective-permute-start.4 = (f32[2,32,128]{2,1,0:T(8,128)S(1)}, f32[2,32,128]{2,1,0:T(8,128)S(1)}, u32[]{:S(2)}, u32[]{:S(2)}) collective-permute-start(f32[2,32,128]{2,1,0:T(8,128)S(1)} %get-tuple-element.27), channel_id=1, source_target_pairs={{1,0},{2,1},{3,2},{4,3},{5,4},{6,5},{7,6},{8,7},{9,8},{10,9},{11,1... | collective-permute-start | bytes 98312 | tf_op jit(solution)/shard_map/ppermute | solution.py:255
  158.8 0.0 collective-permute-done.3.left_ref
  158.8 1.5 collective-permute-done.4.right_ref
  160.4 1.6 copy-done.1
  162.0 6.9 %templates.1 = f32[128,256]{1,0:T(8,128)} custom-call(f32[2,32,128]{2,1,0:T(8,128)S(1)} %collective-permute-done.3.left_ref, f32[2,256,128]{2,1,0:T(8,128)S(1)} %pad_maximum_fusion.mid_ref, f32[2,32,128]{2,1,0:T(8,128)S(1)} %collective-permute-done.4.right_ref, bf16[4096,256]{1,0:T(8,128)(2,1)S(1)} %copy-done, bf16[4096,256]{1,0:T(8,128)(2,1)S(1)} %copy-done.1), custom_call_target="tpu_custom_call" | custom-call | tf_op jit(solution)/shard_map/templates/pallas_call | solution.py:256
  (25 shorter events, 0.3 us)
Async XLA Ops:
  0.0 38.6 %all-to-all-start = ((f32[32,16,512]{2,1,0:T(8,128)}), f32[32,16,512]{2,1,0:T(8,128)S(1)}, u32[]{:S(2)}, u32[]{:S(2)}) async-start(f32[32,16,512]{2,1,0:T(8,128)} %bitcast.35), calls=%async_computation | async-start | bytes 2097152 | tf_op jit(solution)/shard_map/all_to_all | solution.py:224
  43.7 7.8 %copy-start.2 = (s32[512,64]{0,1:T(8,128)S(1)}, s32[512,64]{0,1:T(8,128)}, u32[]{:S(2)}) copy-start(s32[512,64]{0,1:T(8,128)} %param.9) | copy-start | bytes 393220
  43.8 8.0 %copy-start.8 = (s32[15]{0:T(128)S(1)}, s32[15]{0:T(128)}, u32[]{:S(2)}) copy-start(s32[15]{0:T(128)} %param.10) | copy-start | bytes 184
  45.0 32.8 %all-to-all-start.1 = ((f32[32,64,128]{2,1,0:T(8,128)}), f32[32,64,128]{2,1,0:T(8,128)S(1)}, u32[]{:S(2)}, u32[]{:S(2)}) async-start(f32[32,64,128]{2,1,0:T(8,128)} %bitcast.14), calls=%async_computation.1 | async-start | bytes 2097152 | tf_op jit(solution)/shard_map/all_to_all | solution.py:226
  51.4 5.8 %copy-start.7 = (s32[2048,1]{0,1:T(1,128)S(1)}, s32[2048,1]{0,1:T(1,128)}, u32[]{:S(2)}) copy-start(s32[2048,1]{0,1:T(1,128)} %constant.256.clone) | copy-start | bytes 24580
  51.4 5.8 %copy-start.3 = (s32[2048]{0:T(1024)S(1)}, s32[2048]{0:T(1024)}, u32[]{:S(2)}) copy-start(s32[2048]{0:T(1024)} %constant.259) | copy-start | bytes 24580
  51.4 5.8 %copy-start.4 = (s32[2048]{0:T(1024)S(1)}, s32[2048]{0:T(1024)}, u32[]{:S(2)}) copy-start(s32[2048]{0:T(1024)} %constant.260) | copy-start | bytes 24580
  129.0 2.2 %collective-permute-start = (f32[2,256,128]{2,1,0:T(8,128)S(1)}, f32[2,256,128]{2,1,0:T(8,128)S(1)}, u32[]{:S(2)}, u32[]{:S(2)}) collective-permute-start(f32[2,256,128]{2,1,0:T(8,128)S(1)} %subband.1), channel_id=1, source_target_pairs={{0,32},{32,0},{64,96},{96,64},{128,160},{160,128},{192,224},{224,1... | collective-permute-start | bytes 786440 | tf_op jit(solution)/shard_map/ppermute | solution.py:244
  131.3 12.1 %copy-start.6 = (s32[32,16]{0,1:T(8,128)S(1)}, s32[32,16]{0,1:T(8,128)}, u32[]{:S(2)}) copy-start(s32[32,16]{0,1:T(8,128)} %param.11) | copy-start | bytes 6148
  131.3 12.2 %copy-start.5 = (f32[32,16]{0,1:T(8,128)S(1)}, f32[32,16]{0,1:T(8,128)}, u32[]{:S(2)}) copy-start(f32[32,16]{0,1:T(8,128)} %param.12) | copy-start | bytes 6148
  131.4 8.8 %collective-permute-start.1 = (f32[2,256,128]{2,1,0:T(8,128)S(1)}, f32[2,256,128]{2,1,0:T(8,128)S(1)}, u32[]{:S(2)}, u32[]{:S(2)}) collective-permute-start(f32[2,256,128]{2,1,0:T(8,128)S(1)} %pad_maximum_fusion.2), channel_id=1, source_target_pairs={{0,64},{32,96},{64,0},{96,32},{128,192},{160,224},{192,128},{224,1... | collective-permute-start | bytes 786440 | tf_op jit(solution)/shard_map/ppermute | solution.py:244
  140.3 10.3 %collective-permute-start.2 = (f32[2,256,128]{2,1,0:T(8,128)S(1)}, f32[2,256,128]{2,1,0:T(8,128)S(1)}, u32[]{:S(2)}, u32[]{:S(2)}) collective-permute-start(f32[2,256,128]{2,1,0:T(8,128)S(1)} %pad_maximum_fusion.3), channel_id=1, source_target_pairs={{0,128},{32,160},{64,192},{96,224},{128,0},{160,32},{192,64},{224,... | collective-permute-start | bytes 786440 | tf_op jit(solution)/shard_map/ppermute | solution.py:244
  150.6 9.8 %copy-start = (bf16[4096,256]{1,0:T(8,128)(2,1)S(1)}, bf16[4096,256]{1,0:T(8,128)(2,1)}, u32[]{:S(2)}) copy-start(bf16[4096,256]{1,0:T(8,128)(2,1)} %get-tuple-element.7.high_ref) | copy-start | bytes 6291460
  150.7 8.1 %collective-permute-start.3 = (f32[2,32,128]{2,1,0:T(8,128)S(1)}, f32[2,32,128]{2,1,0:T(8,128)S(1)}, u32[]{:S(2)}, u32[]{:S(2)}) collective-permute-start(f32[2,32,128]{2,1,0:T(8,128)S(1)} %get-tuple-element.28), channel_id=1, source_target_pairs={{0,1},{1,2},{2,3},{3,4},{4,5},{5,6},{6,7},{7,8},{8,9},{9,10},{10,1... | collective-permute-start | bytes 98312 | tf_op jit(solution)/shard_map/ppermute | solution.py:252
  153.9 6.5 %collective-permute-start.4 = (f32[2,32,128]{2,1,0:T(8,128)S(1)}, f32[2,32,128]{2,1,0:T(8,128)S(1)}, u32[]{:S(2)}, u32[]{:S(2)}) collective-permute-start(f32[2,32,128]{2,1,0:T(8,128)S(1)} %get-tuple-element.27), channel_id=1, source_target_pairs={{1,0},{2,1},{3,2},{4,3},{5,4},{6,5},{7,6},{8,7},{9,8},{10,9},{11,1... | collective-permute-start | bytes 98312 | tf_op jit(solution)/shard_map/ppermute | solution.py:255
  160.4 1.6 copy-start.1
where the time goes:
time: 171 us; the launch traced here: 169 us
  Pallas kernels  64.1 us (37%)
  waiting for transfers between devices  52.1 us (30%)
  starting transfers between devices  30.6 us (18%)
  other arithmetic  13.6 us (8%)
  local copies, waits for them, and re-layouts  4.3 us (3%)
  matrix products  3.72 us (2%)
    pallas_call x1, Pallas kernels, per_device(): pl.pallas_call(sub_kernel, out_shape=jax.ShapeDtypeStruct((2, bins_dev, b...  51.1 us
    all_to_all x1, waiting for transfers between devices, per_device(): lax.all_to_all(blocks, 'freq', split_axis=0, concat_axis=0, tiled=True)  26.6 us
    all_to_all x1, waiting for transfers between devices, per_device(): spec = lax.all_to_all(spec, 'freq', split_axis=0, concat_axis=0, tiled=True)  16.8 us
    all_to_all x1, starting transfers between devices, per_device(): lax.all_to_all(blocks, 'freq', split_axis=0, concat_axis=0, tiled=True)  11.4 us
    cos x3, other arithmetic, turning(): return (jnp.cos(angle), jnp.sin(angle))  8.11 us
    ppermute x3, waiting for transfers between devices, per_device(): lax.ppermute(current, 'band', [(i, i ^ half) for i in range(band_count)])  7.21 us
    pallas_call x1, Pallas kernels, per_device(): pl.pallas_call(corr_kernel, out_shape=jax.ShapeDtypeStruct((block, bins_d...  6.88 us
    all_to_all x1, starting transfers between devices, per_device(): spec = lax.all_to_all(spec, 'freq', split_axis=0, concat_axis=0, tiled=True)  6.37 us
  transfers between devices with their start and end apart: 7, of which 4 were waited for; matrix products, arithmetic and copies ran while one was open for 8% of the time, Pallas kernels for 4%

commit v1 on v0

v1 whole, which is shorter than its diff:
```python
import math

import jax
import jax.numpy as jnp
from jax import lax
from jax.experimental import pallas as pl
from jax.experimental.pallas import tpu as pltpu
from jax.sharding import PartitionSpec as P

REACH = 32
LANES = 128
GROUP = 8

two_pi = 2.0 * math.pi
top_precision = lax.Precision.HIGHEST
f32 = jnp.float32
bf16 = jnp.bfloat16


def turning(count, modulus):
    angle = (count % modulus).astype(f32) * (two_pi / modulus)
    return (jnp.cos(angle), jnp.sin(angle))


def rotate(real, imag, cosine, sine_part):
    return (real * cosine + imag * sine_part, imag * cosine - real * sine_part)


def pick_entry(table, index):
    return jnp.sum(jnp.where(lax.iota(jnp.int32, table.shape[0]) == index, table, 0))


def split_bf16(value):
    high = value.astype(bf16)
    return high, (value - high.astype(f32)).astype(bf16)


def transform(blocks, length):
    sources, rows, samp = blocks.shape
    inner = length // LANES
    grid = blocks.transpose(1, 0, 2).reshape(rows, inner, LANES)
    index = lax.iota(jnp.int32, LANES)
    cos_first, sin_first = turning(index[:, None] * index[None, :], inner)
    part_re = jnp.einsum("cab,ak->ckb", grid, cos_first, precision=top_precision)
    part_im = -jnp.einsum("cab,ak->ckb", grid, sin_first, precision=top_precision)
    cos_twist, sin_twist = turning(index[:, None] * index[None, :], length)
    part_re, part_im = rotate(part_re, part_im, cos_twist, sin_twist)
    column = lax.iota(jnp.int32, LANES)
    kept = column // 4 * 2 + column % 2
    imag_col = (column // 2 % 2 == 1)[None, :]
    cos_second, sin_second = turning(index[:, None] * kept[None, :], LANES)
    scale = 1.0 / math.sqrt(length) / 16.0 / 4.0
    from_re = jnp.where(imag_col, -sin_second, cos_second) * scale
    from_im = jnp.where(imag_col, cos_second, sin_second) * scale
    both = jnp.concatenate([part_re, part_im], axis=2)
    out = jnp.einsum(
        "ckb,bm->mck", both, jnp.concatenate([from_re, from_im], axis=0), precision=top_precision
    )
    return out.reshape(LANES // 4, 4, rows, LANES)


def delay_turns(channel_delay, first_bin, length):
    per_sub = channel_delay.shape[0] // 2
    both = jnp.concatenate([channel_delay[:per_sub], channel_delay[per_sub:]], axis=1)
    halves = [2 * first_bin + GROUP - 1, 2 * GROUP] + [2 * b + 1 for b in range(GROUP // 2)]
    count = both[None] * jnp.stack([jnp.int32(h) for h in halves])[:, None, None]
    return jnp.stack(turning(count, 2 * length), axis=1)


def spreading():
    shape = (LANES // 2 // GROUP, GROUP // 2, 2 * LANES, 2 * LANES)
    i = [lax.broadcasted_iota(jnp.int32, shape, d) for d in range(4)]
    half = LANES // 2
    source = i[0] * GROUP + i[1] * 2 + i[3] // LANES + i[3] % LANES // half * half
    return (i[2] % LANES == source).astype(bf16)


def sub_kernel(spec_ref, tab_ref, spread_ref, tw_ref, out_ref, parts, centre, wide):
    half = LANES // 2
    per_sub = centre.shape[1]
    sources = spec_ref.shape[0] // 2
    rows = spec_ref.shape[2]
    left = lax.broadcasted_iota(jnp.int32, (rows, LANES), 1) < half

    def arrange(g, carry):
        at = pl.ds(pl.multiple_of(rows * g, rows), rows)
        for x in range(2):
            centre[x, at, :] = tab_ref[0, x, at, :]
            to = pl.ds(pl.multiple_of(per_sub * x + rows * g, rows), rows)
            for h in range(2):
                first = spec_ref[g, 2 * x + h]
                second = spec_ref[sources + g, 2 * x + h]
                pair = (
                    jnp.where(left, first, pltpu.roll(second, half, 1)),
                    jnp.where(left, pltpu.roll(first, half, 1), second),
                )
                for o in range(2):
                    high, low = split_bf16(pair[o])
                    parts[2 * h + o, to, 0:LANES] = high
                    parts[2 * h + o, to, LANES:] = low
        return carry

    lax.fori_loop(0, sources, arrange, 0, unroll=2)
    quarter = spread_ref.shape[0]

    def bins(step, carry):
        for n in range(GROUP // 2):
            for r in range(2):
                at = slice(r * per_sub, (r + 1) * per_sub)
                wide[n, at, :] = jnp.dot(
                    parts[step // quarter, at, :],
                    spread_ref[step % quarter, n],
                    preferred_element_type=f32,
                )

        def channels(g, sums):
            re = list(sums[:GROUP])
            im = list(sums[GROUP:])
            at = pl.ds(pl.multiple_of(8 * g, 8), 8)
            at_im = pl.ds(pl.multiple_of(per_sub + 8 * g, 8), 8)
            mid_cos = centre[0, at, :]
            mid_sin = centre[1, at, :]
            for b in range(GROUP // 2):
                off_cos = tab_ref[2 + b, 0, at, :]
                off_sin = tab_ref[2 + b, 1, at, :]
                cc, ss = mid_cos * off_cos, mid_sin * off_sin
                sc, cs = mid_sin * off_cos, mid_cos * off_sin
                for j, cosine, sine in (
                    (GROUP // 2 + b, cc - ss, sc + cs),
                    (GROUP // 2 - 1 - b, cc + ss, sc - cs),
                ):
                    lanes = slice(j % 2 * LANES, j % 2 * LANES + LANES)
                    real = wide[j // 2, at, lanes]
                    imag = wide[j // 2, at_im, lanes]
                    re[j] = re[j] + (real * cosine + imag * sine)
                    im[j] = im[j] + (imag * cosine - real * sine)
            step_cos = tab_ref[1, 0, at, :]
            step_sin = tab_ref[1, 1, at, :]
            centre[0, at, :] = mid_cos * step_cos - mid_sin * step_sin
            centre[1, at, :] = mid_sin * step_cos + mid_cos * step_sin
            return tuple(re) + tuple(im)

        zero = jnp.zeros((8, LANES), f32)
        sums = lax.fori_loop(0, per_sub // 8, channels, (zero,) * (2 * GROUP), unroll=per_sub // 8)
        at = pl.ds(pl.multiple_of(step * GROUP, GROUP), GROUP)
        re, im = (
            jnp.concatenate(
                [jnp.sum(v, axis=0, keepdims=True) for v in sums[x * GROUP : (x + 1) * GROUP]],
                axis=0,
            )
            for x in range(2)
        )
        lower = lax.broadcasted_iota(jnp.int32, re.shape, 1) < half
        re_turn = pltpu.roll(re, half, 1)
        im_turn = pltpu.roll(im, half, 1)
        up_re, up_im = rotate(
            jnp.where(lower, re_turn, re),
            jnp.where(lower, im_turn, im),
            tw_ref[0, at, :],
            tw_ref[1, at, :],
        )
        out_ref[0, at, :] = jnp.where(lower, re, re_turn) + up_re
        out_ref[1, at, :] = jnp.where(lower, im, im_turn) + up_im
        return carry

    lax.fori_loop(0, out_ref.shape[1] // GROUP, bins, 0)


def toeplitz_kernel(profile_ref, high_ref, low_ref, edge_high_ref, edge_low_ref):
    rows = high_ref.shape[0] // profile_ref.shape[0]

    def body(a, carry):
        row = profile_ref[pl.ds(a, 1), :]
        wide = jnp.broadcast_to(row, (rows, row.shape[1]))
        high, low = split_bf16(pltpu.roll(wide, 0, 1, stride=1, stride_axis=0))
        at = pl.ds(pl.multiple_of(a * rows, rows), rows)
        high_ref[at, :] = high
        low_ref[at, :] = low
        at = pl.ds(pl.multiple_of(a * REACH, REACH), REACH)
        edge_high_ref[at, :] = high[:REACH, :LANES]
        edge_low_ref[at, :] = low[:REACH, :LANES]
        return carry

    lax.fori_loop(0, profile_ref.shape[0], body, 0)


def products(high, low, win_high, win_low):
    return (
        jnp.dot(high, win_high, preferred_element_type=f32)
        + jnp.dot(high, win_low, preferred_element_type=f32)
        + jnp.dot(low, win_high, preferred_element_type=f32)
    )


def power(value):
    re, im = value[:, :LANES], value[:, LANES:]
    return re * re + im * im


def inner_kernel(mid_ref, high_ref, low_ref, out_ref):
    rows = out_ref.shape[0]
    per = 2
    win_high, win_low = split_bf16(jnp.concatenate([mid_ref[0], mid_ref[1]], axis=1))

    def body(step, best):
        at = pl.ds(pl.multiple_of(step * per * rows, rows), per * rows)
        got = products(high_ref[at, :], low_ref[at, :], win_high, win_low)
        for i in range(per):
            best = jnp.maximum(best, power(got[i * rows : (i + 1) * rows]))
        return best

    steps = high_ref.shape[0] // (per * rows)
    out_ref[...] = lax.fori_loop(0, steps, body, jnp.zeros(out_ref.shape, f32), unroll=4)


def edge_kernel(left_ref, mid_ref, right_ref, inner_ref, high_ref, low_ref, out_ref):
    bins = mid_ref.shape[1]
    pad = jnp.zeros((LANES - 3 * REACH, LANES), f32)
    columns = []
    for x in range(2):
        columns.append(jnp.concatenate([left_ref[x], mid_ref[x, : 2 * REACH], pad], axis=0))
    for x in range(2):
        columns.append(jnp.concatenate([mid_ref[x, bins - 2 * REACH :], right_ref[x], pad], axis=0))
    win_high, win_low = split_bf16(jnp.concatenate(columns, axis=1))
    per = 8
    best = [jnp.zeros((REACH, LANES), f32)] * 2
    for step in range(high_ref.shape[0] // (per * REACH)):
        at = slice(step * per * REACH, (step + 1) * per * REACH)
        got = products(high_ref[at, :], low_ref[at, :], win_high, win_low)
        for i in range(per):
            mine = got[i * REACH : (i + 1) * REACH]
            for side in range(2):
                lanes = slice(side * 2 * LANES, (side + 1) * 2 * LANES)
                best[side] = jnp.maximum(best[side], power(mine[:, lanes]))
    out_ref[...] = jnp.concatenate([best[0], inner_ref[...], best[1]], axis=0).T


def per_device(samples, channel_delay, merge_slope, tap_offset, tap_weight):
    freq_count = lax.axis_size("freq")
    band_count = lax.axis_size("band")
    band_pos = lax.axis_index("band")
    freq_pos = lax.axis_index("freq")
    chan_dev, samp_dev = samples.shape
    length = samp_dev * freq_count
    bins_dev = length // 2 // freq_count
    delays_sub = channel_delay.shape[1]
    block = 2 * delays_sub
    vmem = pl.BlockSpec(memory_space=pltpu.VMEM)

    first_bin = freq_pos * bins_dev
    tabs = delay_turns(channel_delay, first_bin, length)
    spread = spreading()
    bins_index = first_bin + lax.iota(jnp.int32, bins_dev)
    sections = band_count.bit_length()
    shifts = []
    for s in range(sections):
        size = 1 << s
        slope = pick_entry(merge_slope, band_pos // size * (2 * size) + size - 1)
        out_index = band_pos % size * block + lax.iota(jnp.int32, block)
        shifts.append(out_index * slope // 16 % length)
    turns = jnp.stack(
        turning(jnp.stack(shifts)[:, None, :] * bins_index[None, :, None], length), axis=1
    )
    matches = tap_offset[:, :, None] + REACH == lax.iota(jnp.int32, bins_dev)[None, None, :]
    profile = jnp.sum(jnp.where(matches, tap_weight[:, :, None], 0.0), axis=1)
    templates = profile.shape[0]
    inner_bins = bins_dev - 2 * REACH
    band_shape = jax.ShapeDtypeStruct((templates * inner_bins, bins_dev), bf16)
    edge_shape = jax.ShapeDtypeStruct((templates * REACH, LANES), bf16)
    bands = pl.pallas_call(
        toeplitz_kernel,
        out_shape=(band_shape, band_shape, edge_shape, edge_shape),
        in_specs=[vmem],
        out_specs=(vmem,) * 4,
        compiler_params=pltpu.CompilerParams(vmem_limit_bytes=40 * 2**20),
        name="toeplitz",
    )(profile)

    blocks = samples.reshape(freq_count, chan_dev // freq_count, samp_dev)
    blocks = lax.all_to_all(blocks, "freq", split_axis=0, concat_axis=0, tiled=True)
    blocks, tabs, spread, bands = lax.optimization_barrier((blocks, tabs, spread, bands))
    spec = transform(blocks, length)
    spec = lax.all_to_all(spec, "freq", split_axis=0, concat_axis=0, tiled=True)
    spec, turns = lax.optimization_barrier((spec, turns))

    current = pl.pallas_call(
        sub_kernel,
        out_shape=jax.ShapeDtypeStruct((2, bins_dev, block), f32),
        in_specs=[vmem] * 4,
        out_specs=vmem,
        scratch_shapes=[
            pltpu.VMEM((4, chan_dev, 2 * LANES), bf16),
            pltpu.VMEM((2, chan_dev // 2, LANES), f32),
            pltpu.VMEM((GROUP // 2, chan_dev, 2 * LANES), f32),
        ],
        compiler_params=pltpu.CompilerParams(vmem_limit_bytes=40 * 2**20),
        name="subband",
    )(spec, tabs, spread, turns[0])

    for s in range(1, sections):
        half = 1 << (s - 1)
        partner = lax.ppermute(current, "band", [(i, i ^ half) for i in range(band_count)])
        upper_side = band_pos % (2 * half) >= half
        lower = jnp.where(upper_side, partner, current)
        upper = jnp.where(upper_side, current, partner)
        up_re, up_im = rotate(upper[0], upper[1], turns[s, 0], turns[s, 1])
        current = jnp.stack([lower[0] + up_re, lower[1] + up_im])

    ends = freq_count - 1
    from_left = lax.ppermute(
        current[:, bins_dev - REACH :], "freq", [(i, i + 1) for i in range(ends)]
    )
    from_right = lax.ppermute(current[:, :REACH], "freq", [(i + 1, i) for i in range(ends)])
    inner = pl.pallas_call(
        inner_kernel,
        out_shape=jax.ShapeDtypeStruct((inner_bins, block), f32),
        in_specs=[vmem] * 3,
        out_specs=vmem,
        cost_estimate=pl.CostEstimate(
            flops=6 * templates * inner_bins * bins_dev * 2 * block,
            bytes_accessed=4 * templates * inner_bins * bins_dev,
            transcendentals=0,
        ),
        compiler_params=pltpu.CompilerParams(vmem_limit_bytes=40 * 2**20),
        name="inner_bins",
    )(current, bands[0], bands[1])
    return pl.pallas_call(
        edge_kernel,
        out_shape=jax.ShapeDtypeStruct((block, bins_dev), f32),
        in_specs=[vmem] * 6,
        out_specs=vmem,
        compiler_params=pltpu.CompilerParams(vmem_limit_bytes=40 * 2**20),
        name="edge_bins",
    )(from_left, current, from_right, inner, bands[2], bands[3])


def solution(mesh):
    placed = (P("band", "freq"), P("band", None), P(), P(), P())
    return jax.shard_map(
        per_device, mesh=mesh, in_specs=placed, out_specs=P("band", "freq"), check_vma=False
    )
```

time: 171 us -> 149 us (0.87)
  Pallas kernels: 64.1 us -> 31.1 us
  local copies, waits for them, and re-layouts: 4.3 us -> 19.3 us
  waiting for transfers between devices: 52.1 us -> 45 us
  other arithmetic: 13.6 us -> 17.7 us
    pallas_call x1, Pallas kernels: 51.1 us -> 22.8 us  [per_device(): pl.pallas_call(sub_kernel, out_shape=jax.ShapeDtypeStruct((2, bins_dev, b...]
    all_to_all x1, waiting for transfers between devices: 26.6 us -> 10.6 us  [per_device(): lax.all_to_all(blocks, 'freq', split_axis=0, concat_axis=0, tiled=True)]
    unnamed x20 -> x13, local copies, waits for them, and re-layouts: 1.84 us -> 10.1 us
    ppermute x3, waiting for transfers between devices: 7.21 us -> 14.4 us  [per_device(): lax.ppermute(current, 'band', [(i, i ^ half) for i in range(band_count)])]
    pallas_call x2 -> x3, Pallas kernels: 13 us -> 8.33 us  [the longest x1 3.42 us: per_device(): pl.pallas_call(toeplitz_kernel, out_shape=(band_shape, band_shape, edge_s...]
    reshape x2, local copies, waits for them, and re-layouts: 0.4 us -> 3.85 us  [transform(): grid = blocks.transpose(1, 0, 2).reshape(rows, inner, LANES)]
    all_to_all x1, waiting for transfers between devices: 16.8 us -> 20 us  [per_device(): spec = lax.all_to_all(spec, 'freq', split_axis=0, concat_axis=0, tiled=True)]
    convert_element_type x0 -> x1, other arithmetic: none -> 2.95 us  [spreading(): return (i[2] % LANES == source).astype(bf16)]
  transfers between devices with their start and end apart: 7 -> 7, of which waited for: 4 -> 5; matrix products, arithmetic and copies ran while one was open for 8% -> 11% of each run, Pallas kernels for 4% -> 4%
where the time goes in v1:
time: 149 us; the launch traced here: 148 us
  waiting for transfers between devices  45 us (30%)
  Pallas kernels  31.1 us (21%)
  starting transfers between devices  30.4 us (20%)
  local copies, waits for them, and re-layouts  19.3 us (13%)
  other arithmetic  17.7 us (12%)
  matrix products  3.72 us (2%)
    pallas_call x1, Pallas kernels, per_device(): pl.pallas_call(sub_kernel, out_shape=jax.ShapeDtypeStruct((2, bins_dev, b...  22.8 us
    all_to_all x1, waiting for transfers between devices, per_device(): spec = lax.all_to_all(spec, 'freq', split_axis=0, concat_axis=0, tiled=True)  20 us
    ppermute x3, waiting for transfers between devices, per_device(): lax.ppermute(current, 'band', [(i, i ^ half) for i in range(band_count)])  14.4 us
    all_to_all x1, starting transfers between devices, per_device(): lax.all_to_all(blocks, 'freq', split_axis=0, concat_axis=0, tiled=True)  11.4 us
    all_to_all x1, waiting for transfers between devices, per_device(): lax.all_to_all(blocks, 'freq', split_axis=0, concat_axis=0, tiled=True)  10.6 us
    unnamed x13, local copies, waits for them, and re-layouts  10.1 us
    all_to_all x1, starting transfers between devices, per_device(): spec = lax.all_to_all(spec, 'freq', split_axis=0, concat_axis=0, tiled=True)  6.37 us
    cos x2, other arithmetic, turning(): return (jnp.cos(angle), jnp.sin(angle))  5.23 us
  transfers between devices with their start and end apart: 7, of which 5 were waited for; matrix products, arithmetic and copies ran while one was open for 11% of the time, Pallas kernels for 4%

profile of v1, /device:TPU:32, one launch (start us, length us, event | category | flops | bytes accessed | tf_op | source)
XLA Modules:
  0.0 147.6 jit_solution(17078304886406236424)
XLA Ops:
  0.0 11.4 %all-to-all-start = ((f32[32,16,512]{2,1,0:T(8,128)}), f32[32,16,512]{2,1,0:T(8,128)S(1)}, u32[]{:S(2)}, u32[]{:S(2)}) async-start(f32[32,16,512]{2,1,0:T(8,128)} %bitcast.82), calls=%async_computation | async-start | bytes 2097152 | tf_op jit(solution)/shard_map/all_to_all | solution.py:280
  11.4 0.3 fusion.54
  11.7 0.9 fusion.83
  12.6 0.1 copy.33
  12.7 0.8 copy.35
  13.5 0.7 broadcast_add_fusion
  14.3 0.1 stack.17
  14.4 3.1 %fusion.20 = (f32[6,1,256,128]{3,2,1,0:T(8,128)S(1)}, f32[6,1,256,128]{3,2,1,0:T(8,128)S(1)}) fusion(s32[6]{0:T(128)S(1)} %stack.17, s32[256,128]{1,0:T(8,128)S(1)} %copy.33), kind=kLoop, calls=%fused_computation.43 | loop fusion | flops 2752512 | bytes 1703960 | tf_op jit(solution)/shard_map/cos | solution.py:22
  17.5 0.3 select_reduce_fusion.profile_ref
  17.8 3.4 %toeplitz.1 = (bf16[6144,256]{1,0:T(8,128)(2,1)S(1)}, bf16[6144,256]{1,0:T(8,128)(2,1)S(1)}, bf16[1024,128]{1,0:T(8,128)(2,1)S(1)}, bf16[1024,128]{1,0:T(8,128)(2,1)S(1)}) custom-call(f32[32,256]{1,0:T(8,128)S(1)} %select_reduce_fusion.profile_ref), custom_call_target="tpu_custom_call" | custom-call | tf_op jit(solution)/shard_map/toeplitz/pallas_call | solution.py:270
  21.2 1.7 %copy-done.1 = bf16[6144,256]{1,0:T(8,128)(2,1)} copy-done((bf16[6144,256]{1,0:T(8,128)(2,1)}, bf16[6144,256]{1,0:T(8,128)(2,1)S(1)}, u32[]{:S(2)}) %copy-start.1) | copy-done | bytes 3145752
  22.9 1.7 %copy-done.3 = bf16[6144,256]{1,0:T(8,128)(2,1)} copy-done((bf16[6144,256]{1,0:T(8,128)(2,1)}, bf16[6144,256]{1,0:T(8,128)(2,1)S(1)}, u32[]{:S(2)}) %copy-start.3) | copy-done | bytes 3145752
  24.6 0.1 pad_maximum_fusion.tab_ref
  24.7 0.3 select_multiply_fusion.1
  25.1 3.0 %fusion.8.spread_ref = bf16[8,4,256,256]{3,2,1,0:T(8,128)(2,1)} fusion(s32[256]{0:T(256)S(1)} %get-tuple-element.62, s32[256]{0:T(256)S(1)} %get-tuple-element.63, s32[256]{0:T(256)S(1)} %get-tuple-element.61, s32[256]{0:T(256)S(1)} %get-tuple-element.64, s32[4]{0:T(128)S(1)} %iota_multiply_fusion.1, s32[8]{0:T(128)S(1)} %iota_multiply_fusion.2, ...), kind=kLoop, calls=%fused_computation.15 | loop fusion | flops 50331648 | bytes 4198960 | tf_op jit(solution)/shard_map/convert_element_type | solution.py:75
  28.0 10.6 %all-to-all-done = f32[32,16,512]{2,1,0:T(8,128)S(1)} async-done(((f32[32,16,512]{2,1,0:T(8,128)}), f32[32,16,512]{2,1,0:T(8,128)S(1)}, u32[]{:S(2)}, u32[]{:S(2)}) %all-to-all-start) | async-done | bytes 1048608 | tf_op jit(solution)/shard_map/all_to_all | solution.py:280
  38.6 1.6 %copy.36 = f32[16,32,512]{2,1,0:T(8,128)} copy(f32[16,32,512]{2,0,1:T(8,128)S(1)} %bitcast.79) | data formatting | bytes 2097152 | tf_op jit(solution)/shard_map/transpose | solution.py:41
  40.2 2.3 %reshape.558 = f32[16,128,128]{2,1,0:T(8,128)} reshape(f32[16,32,512]{2,1,0:T(8,128)} %copy.36) | data formatting | bytes 2097152 | tf_op jit(solution)/shard_map/reshape | solution.py:41
  42.5 1.6 %copy.38 = f32[16,128,128]{1,2,0:T(8,128)S(1)} copy(f32[16,128,128]{2,1,0:T(8,128)} %reshape.558) | data formatting | bytes 2097152 | tf_op jit(solution)/shard_map/reshape | solution.py:41
  44.1 1.2 fusion.40
  45.3 1.2 fusion.38
  46.6 0.3 add_bitcast_fusion
  46.9 1.2 fusion.9
  48.2 1.6 %copy.42 = f32[128,16,128]{2,1,0:T(8,128)} copy(f32[128,16,128]{2,0,1:T(8,128)S(1)} %fusion.9) | data formatting | bytes 2097152 | tf_op jit(solution)/shard_map/ckb,bm->mck/dot_general | solution.py:56
  49.8 6.4 %all-to-all-start.1 = ((f32[32,4,16,128]{3,2,1,0:T(8,128)}), f32[32,4,16,128]{3,2,1,0:T(8,128)S(1)}, u32[]{:S(2)}, u32[]{:S(2)}) async-start(f32[32,4,16,128]{3,2,1,0:T(8,128)} %bitcast.78), calls=%async_computation.1 | async-start | bytes 2097152 | tf_op jit(solution)/shard_map/all_to_all | solution.py:283
  56.2 0.7 fusion.65
  56.9 1.2 and_select_fusion.4
  58.2 1.2 and_select_fusion
  59.4 2.1 %fusion.22 = (f32[4,1,256,128]{3,2,1,0:T(8,128)S(1)}, f32[4,1,256,128]{3,2,1,0:T(8,128)S(1)}) fusion(s32[256]{0:T(256)S(1)} %iota_add_fusion, s32[4,128]{1,0:T(4,128)S(1)} %pad_add_fusion.1), kind=kLoop, calls=%fused_computation.53 | loop fusion | flops 1835008 | bytes 1051648 | tf_op jit(solution)/shard_map/cos | solution.py:22
  61.5 1.1 pad_maximum_fusion.1
  62.6 20.0 %all-to-all-done.1.spec_ref = f32[32,4,16,128]{3,2,1,0:T(8,128)S(1)} async-done(((f32[32,4,16,128]{3,2,1,0:T(8,128)}), f32[32,4,16,128]{3,2,1,0:T(8,128)S(1)}, u32[]{:S(2)}, u32[]{:S(2)}) %all-to-all-start.1) | async-done | bytes 1048608 | tf_op jit(solution)/shard_map/all_to_all | solution.py:283
  82.6 1.0 slice_bitcast_fusion.tw_ref
  83.6 2.2 %copy-done = bf16[8,4,256,256]{3,2,1,0:T(8,128)(2,1)S(1)} copy-done((bf16[8,4,256,256]{3,2,1,0:T(8,128)(2,1)S(1)}, bf16[8,4,256,256]{3,2,1,0:T(8,128)(2,1)}, u32[]{:S(2)}) %copy-start) | copy-done | bytes 4194328
  85.8 22.8 %subband.1 = f32[2,256,128]{2,1,0:T(8,128)S(1)} custom-call(f32[32,4,16,128]{3,2,1,0:T(8,128)S(1)} %all-to-all-done.1.spec_ref, f32[6,2,256,128]{3,2,1,0:T(8,128)S(1)} %pad_maximum_fusion.tab_ref, bf16[8,4,256,256]{3,2,1,0:T(8,128)(2,1)S(1)} %copy-done, f32[2,256,128]{2,1,0:T(8,128)S(1)} %slice_bitcast_fusion.tw_ref), custom_call_target="tpu_custom_call" | custom-call | tf_op jit(solution)/shard_map/subband/pallas_call | solution.py:286
  108.6 1.5 %collective-permute-done = f32[2,256,128]{2,1,0:T(8,128)S(1)} collective-permute-done((f32[2,256,128]{2,1,0:T(8,128)S(1)}, f32[2,256,128]{2,1,0:T(8,128)S(1)}, u32[]{:S(2)}, u32[]{:S(2)}) %collective-permute-start) | collective-permute-done | bytes 262176 | tf_op jit(solution)/shard_map/ppermute | solution.py:302
  110.2 1.0 slice_add_fusion.5
  111.2 1.6 %collective-permute-start.1 = (f32[2,256,128]{2,1,0:T(8,128)S(1)}, f32[2,256,128]{2,1,0:T(8,128)S(1)}, u32[]{:S(2)}, u32[]{:S(2)}) collective-permute-start(f32[2,256,128]{2,1,0:T(8,128)S(1)} %pad_maximum_fusion.3), channel_id=1, source_target_pairs={{0,64},{32,96},{64,0},{96,32},{128,192},{160,224},{192,128},{224,1... | collective-permute-start | bytes 786440 | tf_op jit(solution)/shard_map/ppermute | solution.py:302
  112.8 6.9 %collective-permute-done.1 = f32[2,256,128]{2,1,0:T(8,128)S(1)} collective-permute-done((f32[2,256,128]{2,1,0:T(8,128)S(1)}, f32[2,256,128]{2,1,0:T(8,128)S(1)}, u32[]{:S(2)}, u32[]{:S(2)}) %collective-permute-start.1) | collective-permute-done | bytes 262176 | tf_op jit(solution)/shard_map/ppermute | solution.py:302
  119.7 1.0 slice_add_fusion.3
  120.7 3.1 %collective-permute-start.2 = (f32[2,256,128]{2,1,0:T(8,128)S(1)}, f32[2,256,128]{2,1,0:T(8,128)S(1)}, u32[]{:S(2)}, u32[]{:S(2)}) collective-permute-start(f32[2,256,128]{2,1,0:T(8,128)S(1)} %pad_maximum_fusion.4), channel_id=1, source_target_pairs={{0,128},{32,160},{64,192},{96,224},{128,0},{160,32},{192,64},{224,... | collective-permute-start | bytes 786440 | tf_op jit(solution)/shard_map/ppermute | solution.py:302
  123.9 6.0 %collective-permute-done.2 = f32[2,256,128]{2,1,0:T(8,128)S(1)} collective-permute-done((f32[2,256,128]{2,1,0:T(8,128)S(1)}, f32[2,256,128]{2,1,0:T(8,128)S(1)}, u32[]{:S(2)}, u32[]{:S(2)}) %collective-permute-start.2) | collective-permute-done | bytes 262176 | tf_op jit(solution)/shard_map/ppermute | solution.py:302
  129.9 1.0 slice_add_fusion
  131.0 3.0 %collective-permute-start.3 = (f32[2,32,128]{2,1,0:T(8,128)S(1)}, f32[2,32,128]{2,1,0:T(8,128)S(1)}, u32[]{:S(2)}, u32[]{:S(2)}) collective-permute-start(f32[2,32,128]{2,1,0:T(8,128)S(1)} %get-tuple-element.50), channel_id=1, source_target_pairs={{0,1},{1,2},{2,3},{3,4},{4,5},{5,6},{6,7},{7,8},{8,9},{9,10},{10,1... | collective-permute-start | bytes 98312 | tf_op jit(solution)/shard_map/ppermute | solution.py:310
  134.0 4.9 %collective-permute-start.4 = (f32[2,32,128]{2,1,0:T(8,128)S(1)}, f32[2,32,128]{2,1,0:T(8,128)S(1)}, u32[]{:S(2)}, u32[]{:S(2)}) collective-permute-start(f32[2,32,128]{2,1,0:T(8,128)S(1)} %get-tuple-element.49), channel_id=1, source_target_pairs={{1,0},{2,1},{3,2},{4,3},{5,4},{6,5},{7,6},{8,7},{9,8},{10,9},{11,1... | collective-permute-start | bytes 98312 | tf_op jit(solution)/shard_map/ppermute | solution.py:313
  138.9 1.9 %copy-done.2 = bf16[6144,256]{1,0:T(8,128)(2,1)S(1)} copy-done((bf16[6144,256]{1,0:T(8,128)(2,1)S(1)}, bf16[6144,256]{1,0:T(8,128)(2,1)}, u32[]{:S(2)}) %copy-start.2) | copy-done | bytes 3145752
  140.8 1.9 %copy-done.4 = bf16[6144,256]{1,0:T(8,128)(2,1)S(1)} copy-done((bf16[6144,256]{1,0:T(8,128)(2,1)S(1)}, bf16[6144,256]{1,0:T(8,128)(2,1)}, u32[]{:S(2)}) %copy-start.4) | copy-done | bytes 3145752
  142.7 3.2 %inner_bins.1.inner_ref = f32[192,128]{1,0:T(8,128)S(1)} custom-call(f32[2,256,128]{2,1,0:T(8,128)S(1)} %pad_maximum_fusion.2.mid_ref, bf16[6144,256]{1,0:T(8,128)(2,1)S(1)} %copy-done.2, bf16[6144,256]{1,0:T(8,128)(2,1)S(1)} %copy-done.4), custom_call_target="tpu_custom_call" | custom-call | flops 2415919104 | bytes 6291456 | tf_op jit(solution)/shard_map/inner_bins/pallas_call | solution.py:314
  145.9 1.7 %edge_bins.1 = f32[128,256]{1,0:T(8,128)} custom-call(f32[2,32,128]{2,1,0:T(8,128)S(1)} %collective-permute-done.3.left_ref, f32[2,256,128]{2,1,0:T(8,128)S(1)} %pad_maximum_fusion.2.mid_ref, f32[2,32,128]{2,1,0:T(8,128)S(1)} %collective-permute-done.4.right_ref, f32[192,128]{1,0:T(8,128)S(1)} %inner_bins.1.inner_ref, ...), custom_call_target="tpu_custom_call" | custom-call | tf_op jit(solution)/shard_map/edge_bins/pallas_call | solution.py:327
  (28 shorter events, 0.4 us)
Async XLA Ops:
  0.0 38.6 %all-to-all-start = ((f32[32,16,512]{2,1,0:T(8,128)}), f32[32,16,512]{2,1,0:T(8,128)S(1)}, u32[]{:S(2)}, u32[]{:S(2)}) async-start(f32[32,16,512]{2,1,0:T(8,128)} %bitcast.82), calls=%async_computation | async-start | bytes 2097152 | tf_op jit(solution)/shard_map/all_to_all | solution.py:280
  21.2 1.7 %copy-start.1 = (bf16[6144,256]{1,0:T(8,128)(2,1)}, bf16[6144,256]{1,0:T(8,128)(2,1)S(1)}, u32[]{:S(2)}) copy-start(bf16[6144,256]{1,0:T(8,128)(2,1)S(1)} %get-tuple-element.27.high_ref) | copy-start | bytes 9437188
  22.9 1.7 %copy-start.3 = (bf16[6144,256]{1,0:T(8,128)(2,1)}, bf16[6144,256]{1,0:T(8,128)(2,1)S(1)}, u32[]{:S(2)}) copy-start(bf16[6144,256]{1,0:T(8,128)(2,1)S(1)} %get-tuple-element.28.low_ref) | copy-start | bytes 9437188
  46.9 9.3 %copy-start.5 = (s32[15]{0:T(128)S(1)}, s32[15]{0:T(128)}, u32[]{:S(2)}) copy-start(s32[15]{0:T(128)} %param.7) | copy-start | bytes 184
  49.8 32.8 %all-to-all-start.1 = ((f32[32,4,16,128]{3,2,1,0:T(8,128)}), f32[32,4,16,128]{3,2,1,0:T(8,128)S(1)}, u32[]{:S(2)}, u32[]{:S(2)}) async-start(f32[32,4,16,128]{3,2,1,0:T(8,128)} %bitcast.78), calls=%async_computation.1 | async-start | bytes 2097152 | tf_op jit(solution)/shard_map/all_to_all | solution.py:283
  83.6 2.2 %copy-start = (bf16[8,4,256,256]{3,2,1,0:T(8,128)(2,1)S(1)}, bf16[8,4,256,256]{3,2,1,0:T(8,128)(2,1)}, u32[]{:S(2)}) copy-start(bf16[8,4,256,256]{3,2,1,0:T(8,128)(2,1)} %fusion.8.spread_ref) | copy-start | bytes 12582916
  108.6 1.6 %collective-permute-start = (f32[2,256,128]{2,1,0:T(8,128)S(1)}, f32[2,256,128]{2,1,0:T(8,128)S(1)}, u32[]{:S(2)}, u32[]{:S(2)}) collective-permute-start(f32[2,256,128]{2,1,0:T(8,128)S(1)} %subband.1), channel_id=1, source_target_pairs={{0,32},{32,0},{64,96},{96,64},{128,160},{160,128},{192,224},{224,1... | collective-permute-start | bytes 786440 | tf_op jit(solution)/shard_map/ppermute | solution.py:302
  111.2 8.4 %collective-permute-start.1 = (f32[2,256,128]{2,1,0:T(8,128)S(1)}, f32[2,256,128]{2,1,0:T(8,128)S(1)}, u32[]{:S(2)}, u32[]{:S(2)}) collective-permute-start(f32[2,256,128]{2,1,0:T(8,128)S(1)} %pad_maximum_fusion.3), channel_id=1, source_target_pairs={{0,64},{32,96},{64,0},{96,32},{128,192},{160,224},{192,128},{224,1... | collective-permute-start | bytes 786440 | tf_op jit(solution)/shard_map/ppermute | solution.py:302
  120.7 9.1 %collective-permute-start.2 = (f32[2,256,128]{2,1,0:T(8,128)S(1)}, f32[2,256,128]{2,1,0:T(8,128)S(1)}, u32[]{:S(2)}, u32[]{:S(2)}) collective-permute-start(f32[2,256,128]{2,1,0:T(8,128)S(1)} %pad_maximum_fusion.4), channel_id=1, source_target_pairs={{0,128},{32,160},{64,192},{96,224},{128,0},{160,32},{192,64},{224,... | collective-permute-start | bytes 786440 | tf_op jit(solution)/shard_map/ppermute | solution.py:302
  131.0 15.0 %collective-permute-start.3 = (f32[2,32,128]{2,1,0:T(8,128)S(1)}, f32[2,32,128]{2,1,0:T(8,128)S(1)}, u32[]{:S(2)}, u32[]{:S(2)}) collective-permute-start(f32[2,32,128]{2,1,0:T(8,128)S(1)} %get-tuple-element.50), channel_id=1, source_target_pairs={{0,1},{1,2},{2,3},{3,4},{4,5},{5,6},{6,7},{7,8},{8,9},{9,10},{10,1... | collective-permute-start | bytes 98312 | tf_op jit(solution)/shard_map/ppermute | solution.py:310
  134.0 11.9 %collective-permute-start.4 = (f32[2,32,128]{2,1,0:T(8,128)S(1)}, f32[2,32,128]{2,1,0:T(8,128)S(1)}, u32[]{:S(2)}, u32[]{:S(2)}) collective-permute-start(f32[2,32,128]{2,1,0:T(8,128)S(1)} %get-tuple-element.49), channel_id=1, source_target_pairs={{1,0},{2,1},{3,2},{4,3},{5,4},{6,5},{7,6},{8,7},{9,8},{10,9},{11,1... | collective-permute-start | bytes 98312 | tf_op jit(solution)/shard_map/ppermute | solution.py:313
  138.9 1.9 %copy-start.2 = (bf16[6144,256]{1,0:T(8,128)(2,1)S(1)}, bf16[6144,256]{1,0:T(8,128)(2,1)}, u32[]{:S(2)}) copy-start(bf16[6144,256]{1,0:T(8,128)(2,1)} %copy-done.1) | copy-start | bytes 9437188
  140.8 1.9 %copy-start.4 = (bf16[6144,256]{1,0:T(8,128)(2,1)S(1)}, bf16[6144,256]{1,0:T(8,128)(2,1)}, u32[]{:S(2)}) copy-start(bf16[6144,256]{1,0:T(8,128)(2,1)} %copy-done.3) | copy-start | bytes 9437188

commit v2 on v1

--- a/solution.py
+++ b/solution.py
@@ -1,3 +1,4 @@
+import functools
 import math
 
 import jax
@@ -10,6 +11,8 @@
 REACH = 32
 LANES = 128
 GROUP = 8
+SUB_VMEM = 20 * 2**20
+FILTER_VMEM = 20 * 2**20
 
 two_pi = 2.0 * math.pi
 top_precision = lax.Precision.HIGHEST
@@ -62,7 +65,8 @@
 def delay_turns(channel_delay, first_bin, length):
     per_sub = channel_delay.shape[0] // 2
     both = jnp.concatenate([channel_delay[:per_sub], channel_delay[per_sub:]], axis=1)
-    halves = [2 * first_bin + GROUP - 1, 2 * GROUP] + [2 * b + 1 for b in range(GROUP // 2)]
+    halves = [2 * first_bin + LANES * q + GROUP - 1 for q in range(4)]
+    halves += [2 * GROUP] + [2 * b + 1 for b in range(GROUP // 2)]
     count = both[None] * jnp.stack([jnp.int32(h) for h in halves])[:, None, None]
     return jnp.stack(turning(count, 2 * length), axis=1)
 
@@ -75,9 +79,9 @@
     return (i[2] % LANES == source).astype(bf16)
 
 
-def sub_kernel(spec_ref, tab_ref, spread_ref, tw_ref, out_ref, parts, centre, wide):
+def sub_kernel(quarters, spec_ref, tab_ref, spread_ref, tw_ref, out_ref, parts, centre, wide):
     half = LANES // 2
-    per_sub = centre.shape[1]
+    per_sub = centre.shape[2]
     sources = spec_ref.shape[0] // 2
     rows = spec_ref.shape[2]
     left = lax.broadcasted_iota(jnp.int32, (rows, LANES), 1) < half
@@ -85,31 +89,31 @@
     def arrange(g, carry):
         at = pl.ds(pl.multiple_of(rows * g, rows), rows)
         for x in range(2):
-            centre[x, at, :] = tab_ref[0, x, at, :]
             to = pl.ds(pl.multiple_of(per_sub * x + rows * g, rows), rows)
-            for h in range(2):
-                first = spec_ref[g, 2 * x + h]
-                second = spec_ref[sources + g, 2 * x + h]
-                pair = (
-                    jnp.where(left, first, pltpu.roll(second, half, 1)),
-                    jnp.where(left, pltpu.roll(first, half, 1), second),
-                )
-                for o in range(2):
-                    high, low = split_bf16(pair[o])
-                    parts[2 * h + o, to, 0:LANES] = high
-                    parts[2 * h + o, to, LANES:] = low
+            for slot, q in enumerate(quarters):
+                first = spec_ref[g, 2 * x + q // 2]
+                second = spec_ref[sources + g, 2 * x + q // 2]
+                if q % 2 == 0:
+                    pair = jnp.where(left, first, pltpu.roll(second, half, 1))
+                else:
+                    pair = jnp.where(left, pltpu.roll(first, half, 1), second)
+                high, low = split_bf16(pair)
+                parts[slot, to, 0:LANES] = high
+                parts[slot, to, LANES:] = low
+                centre[slot, x, at, :] = tab_ref[q, x, at, :]
         return carry
 
     lax.fori_loop(0, sources, arrange, 0, unroll=2)
-    quarter = spread_ref.shape[0]
+    steps = spread_ref.shape[0]
 
     def bins(step, carry):
+        slot = step // steps
         for n in range(GROUP // 2):
             for r in range(2):
                 at = slice(r * per_sub, (r + 1) * per_sub)
                 wide[n, at, :] = jnp.dot(
-                    parts[step // quarter, at, :],
-                    spread_ref[step % quarter, n],
+                    parts[slot, at, :],
+                    spread_ref[step % steps, n],
                     preferred_element_type=f32,
                 )
 
@@ -118,11 +122,11 @@
             im = list(sums[GROUP:])
             at = pl.ds(pl.multiple_of(8 * g, 8), 8)
             at_im = pl.ds(pl.multiple_of(per_sub + 8 * g, 8), 8)
-            mid_cos = centre[0, at, :]
-            mid_sin = centre[1, at, :]
+            mid_cos = centre[slot, 0, at, :]
+            mid_sin = centre[slot, 1, at, :]
             for b in range(GROUP // 2):
-                off_cos = tab_ref[2 + b, 0, at, :]
-                off_sin = tab_ref[2 + b, 1, at, :]
+                off_cos = tab_ref[5 + b, 0, at, :]
+                off_sin = tab_ref[5 + b, 1, at, :]
                 cc, ss = mid_cos * off_cos, mid_sin * off_sin
                 sc, cs = mid_sin * off_cos, mid_cos * off_sin
                 for j, cosine, sine in (
@@ -134,10 +138,10 @@
                     imag = wide[j // 2, at_im, lanes]
                     re[j] = re[j] + (real * cosine + imag * sine)
                     im[j] = im[j] + (imag * cosine - real * sine)
-            step_cos = tab_ref[1, 0, at, :]
-            step_sin = tab_ref[1, 1, at, :]
-            centre[0, at, :] = mid_cos * step_cos - mid_sin * step_sin
-            centre[1, at, :] = mid_sin * step_cos + mid_cos * step_sin
+            step_cos = tab_ref[4, 0, at, :]
+            step_sin = tab_ref[4, 1, at, :]
+            centre[slot, 0, at, :] = mid_cos * step_cos - mid_sin * step_sin
+            centre[slot, 1, at, :] = mid_sin * step_cos + mid_cos * step_sin
             return tuple(re) + tuple(im)
 
         zero = jnp.zeros((8, LANES), f32)
@@ -197,30 +201,12 @@
     return re * re + im * im
 
 
-def inner_kernel(mid_ref, high_ref, low_ref, out_ref):
-    rows = out_ref.shape[0]
-    per = 2
-    win_high, win_low = split_bf16(jnp.concatenate([mid_ref[0], mid_ref[1]], axis=1))
-
-    def body(step, best):
-        at = pl.ds(pl.multiple_of(step * per * rows, rows), per * rows)
-        got = products(high_ref[at, :], low_ref[at, :], win_high, win_low)
-        for i in range(per):
-            best = jnp.maximum(best, power(got[i * rows : (i + 1) * rows]))
-        return best
-
-    steps = high_ref.shape[0] // (per * rows)
-    out_ref[...] = lax.fori_loop(0, steps, body, jnp.zeros(out_ref.shape, f32), unroll=4)
-
-
-def edge_kernel(left_ref, mid_ref, right_ref, inner_ref, high_ref, low_ref, out_ref):
-    bins = mid_ref.shape[1]
+def edge_kernel(left_ref, outer_ref, right_ref, high_ref, low_ref, out_ref):
+    near = 2 * REACH
     pad = jnp.zeros((LANES - 3 * REACH, LANES), f32)
-    columns = []
-    for x in range(2):
-        columns.append(jnp.concatenate([left_ref[x], mid_ref[x, : 2 * REACH], pad], axis=0))
-    for x in range(2):
-        columns.append(jnp.concatenate([mid_ref[x, bins - 2 * REACH :], right_ref[x], pad], axis=0))
+    columns = [
+        jnp.concatenate([left_ref[x], outer_ref[x, :near], pad], axis=0) for x in range(2)
+    ] + [jnp.concatenate([outer_ref[x, near:], right_ref[x], pad], axis=0) for x in range(2)]
     win_high, win_low = split_bf16(jnp.concatenate(columns, axis=1))
     per = 8
     best = [jnp.zeros((REACH, LANES), f32)] * 2
@@ -232,7 +218,30 @@
             for side in range(2):
                 lanes = slice(side * 2 * LANES, (side + 1) * 2 * LANES)
                 best[side] = jnp.maximum(best[side], power(mine[:, lanes]))
-    out_ref[...] = jnp.concatenate([best[0], inner_ref[...], best[1]], axis=0).T
+    out_ref[0] = best[0]
+    out_ref[1] = best[1]
+
+
+def inner_kernel(outer_ref, mid_ref, edge_ref, high_ref, low_ref, out_ref):
+    near = 2 * REACH
+    rows = out_ref.shape[1] - near
+    per = 2
+    columns = [
+        jnp.concatenate([outer_ref[x, :near], mid_ref[x], outer_ref[x, near:]], axis=0)
+        for x in range(2)
+    ]
+    win_high, win_low = split_bf16(jnp.concatenate(columns, axis=1))
+
+    def body(step, best):
+        at = pl.ds(pl.multiple_of(step * per * rows, rows), per * rows)
+        got = products(high_ref[at, :], low_ref[at, :], win_high, win_low)
+        for i in range(per):
+            best = jnp.maximum(best, power(got[i * rows : (i + 1) * rows]))
+        return best
+
+    steps = high_ref.shape[0] // (per * rows)
+    best = lax.fori_loop(0, steps, body, jnp.zeros((rows, LANES), f32), unroll=4)
+    out_ref[...] = jnp.concatenate([edge_ref[0], best, edge_ref[1]], axis=0).T
 
 
 def per_device(samples, channel_delay, merge_slope, tap_offset, tap_weight):
@@ -250,7 +259,6 @@
     first_bin = freq_pos * bins_dev
     tabs = delay_turns(channel_delay, first_bin, length)
     spread = spreading()
-    bins_index = first_bin + lax.iota(jnp.int32, bins_dev)
     sections = band_count.bit_length()
     shifts = []
     for s in range(sections):
@@ -258,9 +266,20 @@
         slope = pick_entry(merge_slope, band_pos // size * (2 * size) + size - 1)
         out_index = band_pos % size * block + lax.iota(jnp.int32, block)
         shifts.append(out_index * slope // 16 % length)
-    turns = jnp.stack(
-        turning(jnp.stack(shifts)[:, None, :] * bins_index[None, :, None], length), axis=1
-    )
+    shifts = jnp.stack(shifts)
+    chunks = ((0, 3), (1, 2))
+    quarter = bins_dev // 4
+    within = lax.iota(jnp.int32, quarter)
+    turns = []
+    for pair in chunks:
+        bins_index = jnp.concatenate([first_bin + q * quarter + within for q in pair])
+        count = shifts[:, None, :] * bins_index[None, :, None]
+        turns.append(
+            (
+                jnp.stack(turning(count[0], length)),
+                jnp.stack(turning(count[1:], length), axis=1),
+            )
+        )
     matches = tap_offset[:, :, None] + REACH == lax.iota(jnp.int32, bins_dev)[None, None, :]
     profile = jnp.sum(jnp.where(matches, tap_weight[:, :, None], 0.0), axis=1)
     templates = profile.shape[0]
@@ -272,66 +291,73 @@
         out_shape=(band_shape, band_shape, edge_shape, edge_shape),
         in_specs=[vmem],
         out_specs=(vmem,) * 4,
-        compiler_params=pltpu.CompilerParams(vmem_limit_bytes=40 * 2**20),
+        compiler_params=pltpu.CompilerParams(vmem_limit_bytes=FILTER_VMEM),
         name="toeplitz",
     )(profile)
 
     blocks = samples.reshape(freq_count, chan_dev // freq_count, samp_dev)
     blocks = lax.all_to_all(blocks, "freq", split_axis=0, concat_axis=0, tiled=True)
-    blocks, tabs, spread, bands = lax.optimization_barrier((blocks, tabs, spread, bands))
     spec = transform(blocks, length)
     spec = lax.all_to_all(spec, "freq", split_axis=0, concat_axis=0, tiled=True)
-    spec, turns = lax.optimization_barrier((spec, turns))
-
-    current = pl.pallas_call(
-        sub_kernel,
-        out_shape=jax.ShapeDtypeStruct((2, bins_dev, block), f32),
-        in_specs=[vmem] * 4,
-        out_specs=vmem,
-        scratch_shapes=[
-            pltpu.VMEM((4, chan_dev, 2 * LANES), bf16),
-            pltpu.VMEM((2, chan_dev // 2, LANES), f32),
-            pltpu.VMEM((GROUP // 2, chan_dev, 2 * LANES), f32),
-        ],
-        compiler_params=pltpu.CompilerParams(vmem_limit_bytes=40 * 2**20),
-        name="subband",
-    )(spec, tabs, spread, turns[0])
+    spec, turns, tabs, spread, bands = lax.optimization_barrier(
+        (spec, turns, tabs, spread, bands)
+    )
+
+    current = []
+    for pair, turn in zip(chunks, turns):
+        current.append(
+            pl.pallas_call(
+                functools.partial(sub_kernel, pair),
+                out_shape=jax.ShapeDtypeStruct((2, bins_dev // 2, block), f32),
+                in_specs=[vmem] * 4,
+                out_specs=vmem,
+                scratch_shapes=[
+                    pltpu.VMEM((2, chan_dev, 2 * LANES), bf16),
+                    pltpu.VMEM((2, 2, chan_dev // 2, LANES), f32),
+                    pltpu.VMEM((GROUP // 2, chan_dev, 2 * LANES), f32),
+                ],
+                cost_estimate=pl.CostEstimate(
+                    flops=10**10, bytes_accessed=2**23, transcendentals=0
+                ),
+                compiler_params=pltpu.CompilerParams(vmem_limit_bytes=SUB_VMEM),
+                name="subband",
+            )(spec, tabs, spread, turn[0])
+        )
 
     for s in range(1, sections):
         half = 1 << (s - 1)
-        partner = lax.ppermute(current, "band", [(i, i ^ half) for i in range(band_count)])
-        upper_side = band_pos % (2 * half) >= half
-        lower = jnp.where(upper_side, partner, current)
-        upper = jnp.where(upper_side, current, partner)
-        up_re, up_im = rotate(upper[0], upper[1], turns[s, 0], turns[s, 1])
-        current = jnp.stack([lower[0] + up_re, lower[1] + up_im])
-
+        for i in range(len(chunks)):
+            mine = current[i]
+            partner = lax.ppermute(mine, "band", [(j, j ^ half) for j in range(band_count)])
+            upper_side = band_pos % (2 * half) >= half
+            lower = jnp.where(upper_side, partner, mine)
+            upper = jnp.where(upper_side, mine, partner)
+            turn = turns[i][1][s - 1]
+            up_re, up_im = rotate(upper[0], upper[1], turn[0], turn[1])
+            current[i] = jnp.stack([lower[0] + up_re, lower[1] + up_im])
+
+    outer, middle = current
     ends = freq_count - 1
     from_left = lax.ppermute(
-        current[:, bins_dev - REACH :], "freq", [(i, i + 1) for i in range(ends)]
-    )
-    from_right = lax.ppermute(current[:, :REACH], "freq", [(i + 1, i) for i in range(ends)])
-    inner = pl.pallas_call(
+        outer[:, bins_dev // 2 - REACH :], "freq", [(i, i + 1) for i in range(ends)]
+    )
+    from_right = lax.ppermute(outer[:, :REACH], "freq", [(i + 1, i) for i in range(ends)])
+    edges = pl.pallas_call(
+        edge_kernel,
+        out_shape=jax.ShapeDtypeStruct((2, REACH, block), f32),
+        in_specs=[vmem] * 5,
+        out_specs=vmem,
+        compiler_params=pltpu.CompilerParams(vmem_limit_bytes=FILTER_VMEM),
+        name="edge_bins",
+    )(from_left, outer, from_right, bands[2], bands[3])
+    return pl.pallas_call(
         inner_kernel,
-        out_shape=jax.ShapeDtypeStruct((inner_bins, block), f32),
-        in_specs=[vmem] * 3,
+        out_shape=jax.ShapeDtypeStruct((block, bins_dev), f32),
+        in_specs=[vmem] * 5,
         out_specs=vmem,
-        cost_estimate=pl.CostEstimate(
-            flops=6 * templates * inner_bins * bins_dev * 2 * block,
-            bytes_accessed=4 * templates * inner_bins * bins_dev,
-            transcendentals=0,
-        ),
-        compiler_params=pltpu.CompilerParams(vmem_limit_bytes=40 * 2**20),
+        compiler_params=pltpu.CompilerParams(vmem_limit_bytes=FILTER_VMEM),
         name="inner_bins",
-    )(current, bands[0], bands[1])
-    return pl.pallas_call(
-        edge_kernel,
-        out_shape=jax.ShapeDtypeStruct((block, bins_dev), f32),
-        in_specs=[vmem] * 6,
-        out_specs=vmem,
-        compiler_params=pltpu.CompilerParams(vmem_limit_bytes=40 * 2**20),
-        name="edge_bins",
-    )(from_left, current, from_right, inner, bands[2], bands[3])
+    )(outer, middle, edges, bands[0], bands[1])
 
 
 def solution(mesh):

time: 149 us -> 152 us (1.020)
  waiting for transfers between devices: 45 us -> 33.8 us
  other arithmetic: 17.7 us -> 25 us
  Pallas kernels: 31.1 us -> 34.1 us
  starting transfers between devices: 30.4 us -> 33.1 us
    all_to_all x1, waiting for transfers between devices: 10.6 us -> 4.89 us  [per_device(): lax.all_to_all(blocks, 'freq', split_axis=0, concat_axis=0, tiled=True)]
    all_to_all x1, waiting for transfers between devices: 20 us -> 16.4 us  [per_device(): spec = lax.all_to_all(spec, 'freq', split_axis=0, concat_axis=0, tiled=True)]
    pallas_call x3 -> x4, Pallas kernels: 27.7 us -> 30.7 us  [the longest x2 25.8 us: per_device(): pl.pallas_call(functools.partial(sub_kernel, pair), out_shape=jax.ShapeDt...]
    add x4 -> x8, other arithmetic: 3.04 us -> 0.15 us  [the longest x6 0.15 us: per_device(): current[i] = jnp.stack([lower[0] + up_re, lower[1] + up_im])]
    another operation x6 -> x14, other arithmetic: 1.15 us -> 3.9 us  [the longest x4 3.15 us: per_device(): jnp.stack(turning(count[1:], length), axis=1)]
    ppermute x5 -> x8, starting transfers between devices: 12.7 us -> 15.2 us  [the longest x6 8.14 us: per_device(): lax.ppermute(mine, 'band', [(j, j ^ half) for j in range(band_count)])]
    ppermute x5 -> x8, waiting for transfers between devices: 14.4 us -> 12.6 us  [the longest x6 6.72 us: per_device(): lax.ppermute(mine, 'band', [(j, j ^ half) for j in range(band_count)])]
    unnamed x13 -> x41, local copies, waits for them, and re-layouts: 10.1 us -> 8.39 us
  transfers between devices with their start and end apart: 7 -> 10, of which waited for: 5 -> 5; matrix products, arithmetic and copies ran while one was open for 11% -> 18% of each run, Pallas kernels for 4% -> 11%
where the time goes in v2:
time: 152 us; the launch traced here: 151 us
  Pallas kernels  34.1 us (22%)
  waiting for transfers between devices  33.8 us (22%)
  starting transfers between devices  33.1 us (22%)
  other arithmetic  25 us (16%)
  local copies, waits for them, and re-layouts  19.2 us (13%)
  matrix products  5.03 us (3%)
    pallas_call x2, Pallas kernels, per_device(): pl.pallas_call(functools.partial(sub_kernel, pair), out_shape=jax.ShapeDt...  25.8 us
    all_to_all x1, waiting for transfers between devices, per_device(): spec = lax.all_to_all(spec, 'freq', split_axis=0, concat_axis=0, tiled=True)  16.4 us
    all_to_all x1, starting transfers between devices, per_device(): lax.all_to_all(blocks, 'freq', split_axis=0, concat_axis=0, tiled=True)  11.5 us
    unnamed x41, local copies, waits for them, and re-layouts  8.39 us
    ppermute x6, starting transfers between devices, per_device(): lax.ppermute(mine, 'band', [(j, j ^ half) for j in range(band_count)])  8.14 us
    ppermute x6, waiting for transfers between devices, per_device(): lax.ppermute(mine, 'band', [(j, j ^ half) for j in range(band_count)])  6.72 us
    all_to_all x1, starting transfers between devices, per_device(): spec = lax.all_to_all(spec, 'freq', split_axis=0, concat_axis=0, tiled=True)  6.43 us
    cos x3, other arithmetic, turning(): return (jnp.cos(angle), jnp.sin(angle))  6.08 us
  transfers between devices with their start and end apart: 10, of which 5 were waited for; matrix products, arithmetic and copies ran while one was open for 18% of the time, Pallas kernels for 11%

profile of v2, /device:TPU:32, one launch (start us, length us, event | category | flops | bytes accessed | tf_op | source)
XLA Modules:
  0.0 150.8 jit_solution(6695886978466686878)
XLA Ops:
  0.0 11.5 %all-to-all-start = ((f32[32,16,512]{2,1,0:T(8,128)}), f32[32,16,512]{2,1,0:T(8,128)}, u32[]{:S(2)}, u32[]{:S(2)}) async-start(f32[32,16,512]{2,1,0:T(8,128)} %bitcast.150), calls=%async_computation | async-start | bytes 2097152 | tf_op jit(solution)/shard_map/all_to_all | solution.py:299
  12.1 0.6 iota_multiply_fusion.1
  14.4 0.7 broadcast_add_fusion
  15.2 0.8 copy.54
  16.4 0.7 fusion.82
  17.1 1.3 and_select_fusion.4
  18.4 1.2 and_select_fusion
  19.7 0.8 copy.52
  20.5 3.4 %toeplitz.1 = (bf16[6144,256]{1,0:T(8,128)(2,1)S(1)}, bf16[6144,256]{1,0:T(8,128)(2,1)S(1)}, bf16[1024,128]{1,0:T(8,128)(2,1)S(1)}, bf16[1024,128]{1,0:T(8,128)(2,1)S(1)}) custom-call(f32[32,256]{1,0:T(8,128)S(1)} %select_reduce_fusion.profile_ref), custom_call_target="tpu_custom_call" | custom-call | tf_op jit(solution)/shard_map/toeplitz/pallas_call | solution.py:289
  23.9 1.6 %copy-done.1 = bf16[6144,256]{1,0:T(8,128)(2,1)} copy-done((bf16[6144,256]{1,0:T(8,128)(2,1)}, bf16[6144,256]{1,0:T(8,128)(2,1)S(1)}, u32[]{:S(2)}) %copy-start.1) | copy-done | bytes 3145752
  25.5 0.7 copy-done.4
  26.2 0.7 stack.98
  26.9 0.9 fusion.67
  28.5 0.7 pad_maximum_fusion.4.tw_ref
  29.1 0.8 cosine_bitcast_fusion
  29.9 0.8 pad_maximum_fusion.2
  30.7 0.8 cosine_bitcast_fusion.1
  31.5 0.8 pad_maximum_fusion.1
  32.3 1.7 %select_multiply_fusion.1 = (f32[128,128]{0,1:T(8,128)}, f32[128,128]{0,1:T(8,128)}) fusion(s32[128]{0:T(128)} %fusion.79, pred[128]{0:T(512)(128)(4,1)} %fusion.81), kind=kLoop, calls=%fused_computation.157 | loop fusion | flops 311296 | bytes 131712 | tf_op jit(solution)/shard_map/mul | solution.py:56
  34.0 4.9 %all-to-all-done = f32[32,16,512]{2,1,0:T(8,128)} async-done(((f32[32,16,512]{2,1,0:T(8,128)}), f32[32,16,512]{2,1,0:T(8,128)}, u32[]{:S(2)}, u32[]{:S(2)}) %all-to-all-start) | async-done | bytes 1048608 | tf_op jit(solution)/shard_map/all_to_all | solution.py:299
  38.9 2.8 %copy.42 = f32[16,32,512]{2,1,0:T(8,128)} copy(f32[16,32,512]{2,0,1:T(8,128)} %bitcast.2) | data formatting | bytes 2097152 | tf_op jit(solution)/shard_map/transpose | solution.py:44
  41.7 2.3 %reshape.544 = f32[16,128,128]{2,1,0:T(8,128)} reshape(f32[16,32,512]{2,1,0:T(8,128)} %copy.42) | data formatting | bytes 2097152 | tf_op jit(solution)/shard_map/reshape | solution.py:44
  44.0 2.6 %copy.44 = f32[16,128,128]{1,2,0:T(8,128)} copy(f32[16,128,128]{2,1,0:T(8,128)} %reshape.544) | data formatting | bytes 2097152 | tf_op jit(solution)/shard_map/reshape | solution.py:44
  46.6 2.6 %fusion.51 = f32[128,2048]{0,1:S(1)} fusion(f32[128,2048]{0,1:T(8,128)} %bitcast.145), kind=kOutput, calls=%fused_computation.146 | convolution fusion | flops 402882560 | bytes 2097152
  49.1 1.2 fusion.53
  51.3 1.2 fusion.9
  52.5 1.6 %copy.48 = f32[128,16,128]{2,1,0:T(8,128)} copy(f32[128,16,128]{2,0,1:T(8,128)S(1)} %fusion.9) | data formatting | bytes 2097152 | tf_op jit(solution)/shard_map/ckb,bm->mck/dot_general | solution.py:59
  54.1 6.4 %all-to-all-start.1 = ((f32[32,4,16,128]{3,2,1,0:T(8,128)}), f32[32,4,16,128]{3,2,1,0:T(8,128)}, u32[]{:S(2)}, u32[]{:S(2)}) async-start(f32[32,4,16,128]{3,2,1,0:T(8,128)} %bitcast.147), calls=%async_computation.1 | async-start | bytes 2097152 | tf_op jit(solution)/shard_map/all_to_all | solution.py:301
  60.5 5.5 %fusion.17 = (f32[9,1,256,128]{3,2,1,0:T(8,128)S(1)}, f32[9,1,256,128]{3,2,1,0:T(8,128)S(1)}) fusion(s32[9]{0:T(128)} %stack.98, s32[256,128]{1,0:T(8,128)} %copy.52), kind=kLoop, calls=%fused_computation.32 | loop fusion | flops 4128768 | bytes 2490404 | tf_op jit(solution)/shard_map/cos | solution.py:25
  66.1 1.6 %pad_maximum_fusion.tab_ref = f32[9,2,256,128]{3,2,1,0:T(8,128)} fusion(f32[9,1,256,128]{3,2,1,0:T(8,128)S(1)} %get-tuple-element.74, f32[9,1,256,128]{3,2,1,0:T(8,128)S(1)} %get-tuple-element.73), kind=kLoop, calls=%fused_computation.16 | loop fusion | flops 589824 | bytes 4718592 | tf_op jit(solution)/shard_map/stack | solution.py:71
  67.8 2.9 %fusion.8.spread_ref = bf16[8,4,256,256]{3,2,1,0:T(8,128)(2,1)} fusion(s32[256]{0:T(256)S(1)} %get-tuple-element.96, s32[256]{0:T(256)S(1)} %get-tuple-element.97, s32[256]{0:T(256)S(1)} %get-tuple-element.95, s32[256]{0:T(256)S(1)} %get-tuple-element.98, s32[4]{0:T(128)S(1)} %copy-done.17, s32[8]{0:T(128)S(1)} %copy-done.16, ...), kind=kLoop, calls=%fused_computation.15 | loop fusion | flops 50331648 | bytes 4198960 | tf_op jit(solution)/shard_map/convert_element_type | solution.py:79
  70.7 16.4 %all-to-all-done.1.spec_ref = f32[32,4,16,128]{3,2,1,0:T(8,128)} async-done(((f32[32,4,16,128]{3,2,1,0:T(8,128)}), f32[32,4,16,128]{3,2,1,0:T(8,128)}, u32[]{:S(2)}, u32[]{:S(2)}) %all-to-all-start.1) | async-done | bytes 1048608 | tf_op jit(solution)/shard_map/all_to_all | solution.py:301
  87.0 2.2 %copy-done = bf16[8,4,256,256]{3,2,1,0:T(8,128)(2,1)S(1)} copy-done((bf16[8,4,256,256]{3,2,1,0:T(8,128)(2,1)S(1)}, bf16[8,4,256,256]{3,2,1,0:T(8,128)(2,1)}, u32[]{:S(2)}) %copy-start) | copy-done | bytes 4194328
  89.2 1.7 %copy-done.3 = f32[9,2,256,128]{3,2,1,0:T(8,128)S(1)} copy-done((f32[9,2,256,128]{3,2,1,0:T(8,128)S(1)}, f32[9,2,256,128]{3,2,1,0:T(8,128)}, u32[]{:S(2)}) %copy-start.3) | copy-done | bytes 2359320
  90.9 0.9 copy-done.6
  91.8 12.9 %subband.2 = f32[2,128,128]{2,1,0:T(8,128)S(1)} custom-call(f32[32,4,16,128]{3,2,1,0:T(8,128)} %all-to-all-done.1.spec_ref, f32[9,2,256,128]{3,2,1,0:T(8,128)S(1)} %copy-done.3, bf16[8,4,256,256]{3,2,1,0:T(8,128)(2,1)S(1)} %copy-done, f32[2,128,128]{2,1,0:T(8,128)S(1)} %copy-done.6), custom_call_target="tpu_custom_call" | custom-call | flops 10000000000 | bytes 8388608 | tf_op jit(solution)/shard_map/subband/pallas_call | solution.py:309
  104.8 12.9 %subband.3 = f32[2,128,128]{2,1,0:T(8,128)S(1)} custom-call(f32[32,4,16,128]{3,2,1,0:T(8,128)} %all-to-all-done.1.spec_ref, f32[9,2,256,128]{3,2,1,0:T(8,128)S(1)} %copy-done.3, bf16[8,4,256,256]{3,2,1,0:T(8,128)(2,1)S(1)} %copy-done, f32[2,128,128]{2,1,0:T(8,128)S(1)} %pad_maximum_fusion.5.tw_ref), custom_call_target="tpu_custom_call" | custom-call | flops 10000000000 | bytes 8388608 | tf_op jit(solution)/shard_map/subband/pallas_call | solution.py:309
  118.2 1.6 %collective-permute-start.1 = (f32[2,128,128]{2,1,0:T(8,128)S(1)}, f32[2,128,128]{2,1,0:T(8,128)S(1)}, u32[]{:S(2)}, u32[]{:S(2)}) collective-permute-start(f32[2,128,128]{2,1,0:T(8,128)S(1)} %pad_maximum_fusion.6), channel_id=1, source_target_pairs={{0,64},{32,96},{64,0},{96,32},{128,192},{160,224},{192,128},{224,1... | collective-permute-start | bytes 393224 | tf_op jit(solution)/shard_map/ppermute | solution.py:331
  119.9 0.9 collective-permute-start.4
  120.8 3.9 %collective-permute-done.1 = f32[2,128,128]{2,1,0:T(8,128)S(1)} collective-permute-done((f32[2,128,128]{2,1,0:T(8,128)S(1)}, f32[2,128,128]{2,1,0:T(8,128)S(1)}, u32[]{:S(2)}, u32[]{:S(2)}) %collective-permute-start.1) | collective-permute-done | bytes 131104 | tf_op jit(solution)/shard_map/ppermute | solution.py:331
  124.8 3.1 %collective-permute-start.2 = (f32[2,128,128]{2,1,0:T(8,128)S(1)}, f32[2,128,128]{2,1,0:T(8,128)S(1)}, u32[]{:S(2)}, u32[]{:S(2)}) collective-permute-start(f32[2,128,128]{2,1,0:T(8,128)S(1)} %pad_maximum_fusion.7), channel_id=1, source_target_pairs={{0,128},{32,160},{64,192},{96,224},{128,0},{160,32},{192,64},{224,... | collective-permute-start | bytes 393224 | tf_op jit(solution)/shard_map/ppermute | solution.py:331
  128.0 2.0 %collective-permute-start.5 = (f32[2,128,128]{2,1,0:T(8,128)S(1)}, f32[2,128,128]{2,1,0:T(8,128)S(1)}, u32[]{:S(2)}, u32[]{:S(2)}) collective-permute-start(f32[2,128,128]{2,1,0:T(8,128)S(1)} %pad_maximum_fusion.9), channel_id=1, source_target_pairs={{0,128},{32,160},{64,192},{96,224},{128,0},{160,32},{192,64},{224,... | collective-permute-start | bytes 393224 | tf_op jit(solution)/shard_map/ppermute | solution.py:331
  129.9 2.9 %collective-permute-done.2 = f32[2,128,128]{2,1,0:T(8,128)S(1)} collective-permute-done((f32[2,128,128]{2,1,0:T(8,128)S(1)}, f32[2,128,128]{2,1,0:T(8,128)S(1)}, u32[]{:S(2)}, u32[]{:S(2)}) %collective-permute-start.2) | collective-permute-done | bytes 131104 | tf_op jit(solution)/shard_map/ppermute | solution.py:331
  132.9 5.1 %collective-permute-start.7 = (f32[2,32,128]{2,1,0:T(8,128)S(1)}, f32[2,32,128]{2,1,0:T(8,128)S(1)}, u32[]{:S(2)}, u32[]{:S(2)}) collective-permute-start(f32[2,32,128]{2,1,0:T(8,128)S(1)} %get-tuple-element.75), channel_id=1, source_target_pairs={{1,0},{2,1},{3,2},{4,3},{5,4},{6,5},{7,6},{8,7},{9,8},{10,9},{11,1... | collective-permute-start | bytes 98312 | tf_op jit(solution)/shard_map/ppermute | solution.py:344
  138.0 1.9 %collective-permute-start.6 = (f32[2,32,128]{2,1,0:T(8,128)S(1)}, f32[2,32,128]{2,1,0:T(8,128)S(1)}, u32[]{:S(2)}, u32[]{:S(2)}) collective-permute-start(f32[2,32,128]{2,1,0:T(8,128)S(1)} %get-tuple-element.76), channel_id=1, source_target_pairs={{0,1},{1,2},{2,3},{3,4},{4,5},{5,6},{6,7},{7,8},{8,9},{9,10},{10,1... | collective-permute-start | bytes 98312 | tf_op jit(solution)/shard_map/ppermute | solution.py:341
  140.0 5.9 %collective-permute-done.6.left_ref = f32[2,32,128]{2,1,0:T(8,128)S(1)} collective-permute-done((f32[2,32,128]{2,1,0:T(8,128)S(1)}, f32[2,32,128]{2,1,0:T(8,128)S(1)}, u32[]{:S(2)}, u32[]{:S(2)}) %collective-permute-start.6) | collective-permute-done | bytes 32800 | tf_op jit(solution)/shard_map/ppermute | solution.py:341
  145.9 1.0 edge_bins.1.edge_ref
  146.9 3.9 %inner_bins.1 = f32[128,256]{1,0:T(8,128)} custom-call(f32[2,128,128]{2,1,0:T(8,128)S(1)} %pad_maximum_fusion.3.outer_ref, f32[2,128,128]{2,1,0:T(8,128)S(1)} %pad_maximum_fusion.10.mid_ref, f32[2,32,128]{2,1,0:T(8,128)S(1)} %edge_bins.1.edge_ref, bf16[6144,256]{1,0:T(8,128)(2,1)S(1)} %get-tuple-element.33.high_ref, bf16[6144,256]{1,0:T(8,128)(2,1)S(1)} %copy-done.2), custom_call_target="tpu_custom_call" | custom-call | tf_op jit(solution)/shard_map/inner_bins/pallas_call | solution.py:353
  (81 shorter events, 5.2 us)
Async XLA Ops:
  0.0 16.0 %copy-start.14 = (s32[512,64]{0,1:T(8,128)S(1)}, s32[512,64]{0,1:T(8,128)}, u32[]{:S(2)}) copy-start(s32[512,64]{0,1:T(8,128)} %param.6) | copy-start | bytes 393220
  0.0 16.4 %copy-start.19 = (s32[15]{0:T(128)S(1)}, s32[15]{0:T(128)}, u32[]{:S(2)}) copy-start(s32[15]{0:T(128)} %param.7) | copy-start | bytes 184
  0.0 38.9 %all-to-all-start = ((f32[32,16,512]{2,1,0:T(8,128)}), f32[32,16,512]{2,1,0:T(8,128)}, u32[]{:S(2)}, u32[]{:S(2)}) async-start(f32[32,16,512]{2,1,0:T(8,128)} %bitcast.150), calls=%async_computation | async-start | bytes 2097152 | tf_op jit(solution)/shard_map/all_to_all | solution.py:299
  23.9 1.6 %copy-start.1 = (bf16[6144,256]{1,0:T(8,128)(2,1)}, bf16[6144,256]{1,0:T(8,128)(2,1)S(1)}, u32[]{:S(2)}) copy-start(bf16[6144,256]{1,0:T(8,128)(2,1)S(1)} %get-tuple-element.34.low_ref) | copy-start | bytes 9437188
  25.5 0.7 copy-start.4
  46.6 2.6 %copy-start.7 = (f32[16,128,128]{1,2,0:T(8,128)S(1)}, f32[16,128,128]{1,2,0:T(8,128)}, u32[]{:S(2)}) copy-start(f32[16,128,128]{1,2,0:T(8,128)} %copy.44) | copy-start | bytes 3145732
  46.6 3.9 %copy-start.10 = (f32[128,128]{0,1:T(8,128)S(1)}, f32[128,128]{0,1:T(8,128)}, u32[]{:S(2)}) copy-start(f32[128,128]{0,1:T(8,128)} %get-tuple-element.83) | copy-start | bytes 196612
  46.6 3.9 %copy-start.11 = (f32[128,128]{0,1:T(8,128)S(1)}, f32[128,128]{0,1:T(8,128)}, u32[]{:S(2)}) copy-start(f32[128,128]{0,1:T(8,128)} %get-tuple-element.84) | copy-start | bytes 196612
  50.4 0.8 copy-start.12
  50.4 0.9 copy-start.13
  54.1 32.9 %all-to-all-start.1 = ((f32[32,4,16,128]{3,2,1,0:T(8,128)}), f32[32,4,16,128]{3,2,1,0:T(8,128)}, u32[]{:S(2)}, u32[]{:S(2)}) async-start(f32[32,4,16,128]{3,2,1,0:T(8,128)} %bitcast.147), calls=%async_computation.1 | async-start | bytes 2097152 | tf_op jit(solution)/shard_map/all_to_all | solution.py:301
  66.1 1.7 %copy-start.15 = (pred[256]{0:T(512)(128)(4,1)S(1)}, pred[256]{0:T(512)(128)(4,1)}, u32[]{:S(2)}) copy-start(pred[256]{0:T(512)(128)(4,1)} %get-tuple-element.94) | copy-start | bytes 772
  66.1 1.7 %copy-start.16 = (s32[8]{0:T(128)S(1)}, s32[8]{0:T(128)}, u32[]{:S(2)}) copy-start(s32[8]{0:T(128)} %iota_multiply_fusion.2) | copy-start | bytes 100
  66.1 1.7 %copy-start.17 = (s32[4]{0:T(128)S(1)}, s32[4]{0:T(128)}, u32[]{:S(2)}) copy-start(s32[4]{0:T(128)} %iota_multiply_fusion.1) | copy-start | bytes 52
  66.1 1.7 %copy-start.18 = (pred[256]{0:T(512)(128)(4,1)S(1)}, pred[256]{0:T(512)(128)(4,1)}, u32[]{:S(2)}) copy-start(pred[256]{0:T(512)(128)(4,1)} %get-tuple-element.93) | copy-start | bytes 772
  87.0 2.2 %copy-start = (bf16[8,4,256,256]{3,2,1,0:T(8,128)(2,1)S(1)}, bf16[8,4,256,256]{3,2,1,0:T(8,128)(2,1)}, u32[]{:S(2)}) copy-start(bf16[8,4,256,256]{3,2,1,0:T(8,128)(2,1)} %fusion.8.spread_ref) | copy-start | bytes 12582916
  89.2 1.7 %copy-start.3 = (f32[9,2,256,128]{3,2,1,0:T(8,128)S(1)}, f32[9,2,256,128]{3,2,1,0:T(8,128)}, u32[]{:S(2)}) copy-start(f32[9,2,256,128]{3,2,1,0:T(8,128)} %pad_maximum_fusion.tab_ref) | copy-start | bytes 7077892
  90.9 0.9 copy-start.6
  104.7 13.5 %copy-start.9 = (f32[3,2,128,128]{3,2,1,0:T(8,128)S(1)}, f32[3,2,128,128]{3,2,1,0:T(8,128)}, u32[]{:S(2)}) copy-start(f32[3,2,128,128]{3,2,1,0:T(8,128)} %pad_maximum_fusion.1) | copy-start | bytes 1179652
  104.7 15.2 %copy-start.8 = (f32[3,2,128,128]{3,2,1,0:T(8,128)S(1)}, f32[3,2,128,128]{3,2,1,0:T(8,128)}, u32[]{:S(2)}) copy-start(f32[3,2,128,128]{3,2,1,0:T(8,128)} %pad_maximum_fusion.2) | copy-start | bytes 1179652
  104.7 13.5 %collective-permute-start = (f32[2,128,128]{2,1,0:T(8,128)S(1)}, f32[2,128,128]{2,1,0:T(8,128)S(1)}, u32[]{:S(2)}, u32[]{:S(2)}) collective-permute-start(f32[2,128,128]{2,1,0:T(8,128)S(1)} %subband.2), channel_id=1, source_target_pairs={{0,32},{32,0},{64,96},{96,64},{128,160},{160,128},{192,224},{224,1... | collective-permute-start | bytes 393224 | tf_op jit(solution)/shard_map/ppermute | solution.py:331
  117.7 2.1 %collective-permute-start.3 = (f32[2,128,128]{2,1,0:T(8,128)S(1)}, f32[2,128,128]{2,1,0:T(8,128)S(1)}, u32[]{:S(2)}, u32[]{:S(2)}) collective-permute-start(f32[2,128,128]{2,1,0:T(8,128)S(1)} %subband.3), channel_id=1, source_target_pairs={{0,32},{32,0},{64,96},{96,64},{128,160},{160,128},{192,224},{224,1... | collective-permute-start | bytes 393224 | tf_op jit(solution)/shard_map/ppermute | solution.py:331
  118.2 6.4 %collective-permute-start.1 = (f32[2,128,128]{2,1,0:T(8,128)S(1)}, f32[2,128,128]{2,1,0:T(8,128)S(1)}, u32[]{:S(2)}, u32[]{:S(2)}) collective-permute-start(f32[2,128,128]{2,1,0:T(8,128)S(1)} %pad_maximum_fusion.6), channel_id=1, source_target_pairs={{0,64},{32,96},{64,0},{96,32},{128,192},{160,224},{192,128},{224,1... | collective-permute-start | bytes 393224 | tf_op jit(solution)/shard_map/ppermute | solution.py:331
  119.9 8.0 %collective-permute-start.4 = (f32[2,128,128]{2,1,0:T(8,128)S(1)}, f32[2,128,128]{2,1,0:T(8,128)S(1)}, u32[]{:S(2)}, u32[]{:S(2)}) collective-permute-start(f32[2,128,128]{2,1,0:T(8,128)S(1)} %pad_maximum_fusion.8), channel_id=1, source_target_pairs={{0,64},{32,96},{64,0},{96,32},{128,192},{160,224},{192,128},{224,1... | collective-permute-start | bytes 393224 | tf_op jit(solution)/shard_map/ppermute | solution.py:331
  124.7 21.2 %copy-start.5 = (bf16[1024,128]{1,0:T(8,128)(2,1)S(1)}, bf16[1024,128]{1,0:T(8,128)(2,1)}, u32[]{:S(2)}) copy-start(bf16[1024,128]{1,0:T(8,128)(2,1)} %copy-done.4) | copy-start | bytes 786436
  124.8 22.1 %copy-start.2 = (bf16[6144,256]{1,0:T(8,128)(2,1)S(1)}, bf16[6144,256]{1,0:T(8,128)(2,1)}, u32[]{:S(2)}) copy-start(bf16[6144,256]{1,0:T(8,128)(2,1)} %copy-done.1) | copy-start | bytes 9437188
  124.8 8.0 %collective-permute-start.2 = (f32[2,128,128]{2,1,0:T(8,128)S(1)}, f32[2,128,128]{2,1,0:T(8,128)S(1)}, u32[]{:S(2)}, u32[]{:S(2)}) collective-permute-start(f32[2,128,128]{2,1,0:T(8,128)S(1)} %pad_maximum_fusion.7), channel_id=1, source_target_pairs={{0,128},{32,160},{64,192},{96,224},{128,0},{160,32},{192,64},{224,... | collective-permute-start | bytes 393224 | tf_op jit(solution)/shard_map/ppermute | solution.py:331
  128.0 12.0 %collective-permute-start.5 = (f32[2,128,128]{2,1,0:T(8,128)S(1)}, f32[2,128,128]{2,1,0:T(8,128)S(1)}, u32[]{:S(2)}, u32[]{:S(2)}) collective-permute-start(f32[2,128,128]{2,1,0:T(8,128)S(1)} %pad_maximum_fusion.9), channel_id=1, source_target_pairs={{0,128},{32,160},{64,192},{96,224},{128,0},{160,32},{192,64},{224,... | collective-permute-start | bytes 393224 | tf_op jit(solution)/shard_map/ppermute | solution.py:331
  132.9 7.2 %collective-permute-start.7 = (f32[2,32,128]{2,1,0:T(8,128)S(1)}, f32[2,32,128]{2,1,0:T(8,128)S(1)}, u32[]{:S(2)}, u32[]{:S(2)}) collective-permute-start(f32[2,32,128]{2,1,0:T(8,128)S(1)} %get-tuple-element.75), channel_id=1, source_target_pairs={{1,0},{2,1},{3,2},{4,3},{5,4},{6,5},{7,6},{8,7},{9,8},{10,9},{11,1... | collective-permute-start | bytes 98312 | tf_op jit(solution)/shard_map/ppermute | solution.py:344
  138.0 7.9 %collective-permute-start.6 = (f32[2,32,128]{2,1,0:T(8,128)S(1)}, f32[2,32,128]{2,1,0:T(8,128)S(1)}, u32[]{:S(2)}, u32[]{:S(2)}) collective-permute-start(f32[2,32,128]{2,1,0:T(8,128)S(1)} %get-tuple-element.76), channel_id=1, source_target_pairs={{0,1},{1,2},{2,3},{3,4},{4,5},{5,6},{6,7},{7,8},{8,9},{9,10},{10,1... | collective-permute-start | bytes 98312 | tf_op jit(solution)/shard_map/ppermute | solution.py:341

commit v3 on v2

--- a/solution.py
+++ b/solution.py
@@ -11,8 +11,8 @@
 REACH = 32
 LANES = 128
 GROUP = 8
-SUB_VMEM = 20 * 2**20
-FILTER_VMEM = 20 * 2**20
+SUB_VMEM = 12 * 2**20
+FILTER_VMEM = 8 * 2**20
 
 two_pi = 2.0 * math.pi
 top_precision = lax.Precision.HIGHEST
@@ -23,6 +23,12 @@
 def turning(count, modulus):
     angle = (count % modulus).astype(f32) * (two_pi / modulus)
     return (jnp.cos(angle), jnp.sin(angle))
+
+
+def turning_pair(count, modulus, axis):
+    quarter_back = jnp.array([0, modulus // 4 * 3], jnp.int32)
+    offset = quarter_back.reshape([2 if i == axis else 1 for i in range(count.ndim + 1)])
+    return turning(jnp.expand_dims(count, axis) + offset, modulus)[0]
 
 
 def rotate(real, imag, cosine, sine_part):
@@ -68,15 +74,15 @@
     halves = [2 * first_bin + LANES * q + GROUP - 1 for q in range(4)]
     halves += [2 * GROUP] + [2 * b + 1 for b in range(GROUP // 2)]
     count = both[None] * jnp.stack([jnp.int32(h) for h in halves])[:, None, None]
-    return jnp.stack(turning(count, 2 * length), axis=1)
+    return turning_pair(count, 2 * length, 1)
 
 
 def spreading():
-    shape = (LANES // 2 // GROUP, GROUP // 2, 2 * LANES, 2 * LANES)
+    shape = (LANES // 2 // GROUP, GROUP // 2, LANES, 2 * LANES)
     i = [lax.broadcasted_iota(jnp.int32, shape, d) for d in range(4)]
     half = LANES // 2
     source = i[0] * GROUP + i[1] * 2 + i[3] // LANES + i[3] % LANES // half * half
-    return (i[2] % LANES == source).astype(bf16)
+    return (i[2] == source).astype(bf16)
 
 
 def sub_kernel(quarters, spec_ref, tab_ref, spread_ref, tw_ref, out_ref, parts, centre, wide):
@@ -109,11 +115,13 @@
     def bins(step, carry):
         slot = step // steps
         for n in range(GROUP // 2):
+            one_hot = spread_ref[step % steps, n]
+            one_hot = jnp.concatenate([one_hot, one_hot], axis=0)
             for r in range(2):
                 at = slice(r * per_sub, (r + 1) * per_sub)
                 wide[n, at, :] = jnp.dot(
                     parts[slot, at, :],
-                    spread_ref[step % steps, n],
+                    one_hot,
                     preferred_element_type=f32,
                 )
 
@@ -170,29 +178,29 @@
     lax.fori_loop(0, out_ref.shape[1] // GROUP, bins, 0)
 
 
-def toeplitz_kernel(profile_ref, high_ref, low_ref, edge_high_ref, edge_low_ref):
-    rows = high_ref.shape[0] // profile_ref.shape[0]
+def toeplitz_kernel(profile_ref, band_ref):
+    rows = 2 * REACH
 
     def body(a, carry):
         row = profile_ref[pl.ds(a, 1), :]
         wide = jnp.broadcast_to(row, (rows, row.shape[1]))
         high, low = split_bf16(pltpu.roll(wide, 0, 1, stride=1, stride_axis=0))
         at = pl.ds(pl.multiple_of(a * rows, rows), rows)
-        high_ref[at, :] = high
-        low_ref[at, :] = low
-        at = pl.ds(pl.multiple_of(a * REACH, REACH), REACH)
-        edge_high_ref[at, :] = high[:REACH, :LANES]
-        edge_low_ref[at, :] = low[:REACH, :LANES]
+        band_ref[at, :LANES] = high
+        band_ref[at, LANES:] = low
         return carry
 
-    lax.fori_loop(0, profile_ref.shape[0], body, 0)
-
-
-def products(high, low, win_high, win_low):
-    return (
-        jnp.dot(high, win_high, preferred_element_type=f32)
-        + jnp.dot(high, win_low, preferred_element_type=f32)
-        + jnp.dot(low, win_high, preferred_element_type=f32)
+    lax.fori_loop(0, profile_ref.shape[0], body, 0, unroll=4)
+
+
+def windows(value):
+    high, low = split_bf16(value)
+    return jnp.concatenate([high, high], axis=0), jnp.concatenate([low, low], axis=0)
+
+
+def products(band, high, low):
+    return jnp.dot(band, high, preferred_element_type=f32) + jnp.dot(
+        band, low, preferred_element_type=f32
     )
 
 
@@ -201,18 +209,21 @@
     return re * re + im * im
 
 
-def edge_kernel(left_ref, outer_ref, right_ref, high_ref, low_ref, out_ref):
+def edge_kernel(left_ref, outer_ref, right_ref, band_ref, out_ref):
     near = 2 * REACH
     pad = jnp.zeros((LANES - 3 * REACH, LANES), f32)
     columns = [
         jnp.concatenate([left_ref[x], outer_ref[x, :near], pad], axis=0) for x in range(2)
     ] + [jnp.concatenate([outer_ref[x, near:], right_ref[x], pad], axis=0) for x in range(2)]
-    win_high, win_low = split_bf16(jnp.concatenate(columns, axis=1))
+    high, low = windows(jnp.concatenate(columns, axis=1))
     per = 8
     best = [jnp.zeros((REACH, LANES), f32)] * 2
-    for step in range(high_ref.shape[0] // (per * REACH)):
-        at = slice(step * per * REACH, (step + 1) * per * REACH)
-        got = products(high_ref[at, :], low_ref[at, :], win_high, win_low)
+    for step in range(band_ref.shape[0] // (per * near)):
+        first = step * per * near
+        band = jnp.concatenate(
+            [band_ref[first + i * near : first + i * near + REACH, :] for i in range(per)], axis=0
+        )
+        got = products(band, high, low)
         for i in range(per):
             mine = got[i * REACH : (i + 1) * REACH]
             for side in range(2):
@@ -222,26 +233,26 @@
     out_ref[1] = best[1]
 
 
-def inner_kernel(outer_ref, mid_ref, edge_ref, high_ref, low_ref, out_ref):
+def inner_kernel(outer_ref, mid_ref, edge_ref, band_ref, out_ref):
     near = 2 * REACH
-    rows = out_ref.shape[1] - near
-    per = 2
+    blocks = out_ref.shape[1] // near - 1
     columns = [
         jnp.concatenate([outer_ref[x, :near], mid_ref[x], outer_ref[x, near:]], axis=0)
         for x in range(2)
     ]
-    win_high, win_low = split_bf16(jnp.concatenate(columns, axis=1))
-
-    def body(step, best):
-        at = pl.ds(pl.multiple_of(step * per * rows, rows), per * rows)
-        got = products(high_ref[at, :], low_ref[at, :], win_high, win_low)
-        for i in range(per):
-            best = jnp.maximum(best, power(got[i * rows : (i + 1) * rows]))
-        return best
-
-    steps = high_ref.shape[0] // (per * rows)
-    best = lax.fori_loop(0, steps, body, jnp.zeros((rows, LANES), f32), unroll=4)
-    out_ref[...] = jnp.concatenate([edge_ref[0], best, edge_ref[1]], axis=0).T
+    whole = jnp.concatenate(columns, axis=1)
+    per = 4
+    best = []
+    for i in range(blocks):
+        high, low = windows(whole[i * near : i * near + LANES])
+        mine = jnp.zeros((near, LANES), f32)
+        for step in range(band_ref.shape[0] // (per * near)):
+            at = slice(step * per * near, (step + 1) * per * near)
+            got = products(band_ref[at, :], high, low)
+            for j in range(per):
+                mine = jnp.maximum(mine, power(got[j * near : (j + 1) * near]))
+        best.append(mine)
+    out_ref[...] = jnp.concatenate([edge_ref[0]] + best + [edge_ref[1]], axis=0).T
 
 
 def per_device(samples, channel_delay, merge_slope, tap_offset, tap_weight):
@@ -276,21 +287,18 @@
         count = shifts[:, None, :] * bins_index[None, :, None]
         turns.append(
             (
-                jnp.stack(turning(count[0], length)),
-                jnp.stack(turning(count[1:], length), axis=1),
+                turning_pair(count[0], length, 0),
+                turning_pair(count[1:], length, 1),
             )
         )
-    matches = tap_offset[:, :, None] + REACH == lax.iota(jnp.int32, bins_dev)[None, None, :]
+    matches = tap_offset[:, :, None] + REACH == lax.iota(jnp.int32, LANES)[None, None, :]
     profile = jnp.sum(jnp.where(matches, tap_weight[:, :, None], 0.0), axis=1)
     templates = profile.shape[0]
-    inner_bins = bins_dev - 2 * REACH
-    band_shape = jax.ShapeDtypeStruct((templates * inner_bins, bins_dev), bf16)
-    edge_shape = jax.ShapeDtypeStruct((templates * REACH, LANES), bf16)
-    bands = pl.pallas_call(
+    band = pl.pallas_call(
         toeplitz_kernel,
-        out_shape=(band_shape, band_shape, edge_shape, edge_shape),
+        out_shape=jax.ShapeDtypeStruct((templates * 2 * REACH, 2 * LANES), bf16),
         in_specs=[vmem],
-        out_specs=(vmem,) * 4,
+        out_specs=vmem,
         compiler_params=pltpu.CompilerParams(vmem_limit_bytes=FILTER_VMEM),
         name="toeplitz",
     )(profile)
@@ -299,8 +307,8 @@
     blocks = lax.all_to_all(blocks, "freq", split_axis=0, concat_axis=0, tiled=True)
     spec = transform(blocks, length)
     spec = lax.all_to_all(spec, "freq", split_axis=0, concat_axis=0, tiled=True)
-    spec, turns, tabs, spread, bands = lax.optimization_barrier(
-        (spec, turns, tabs, spread, bands)
+    spec, turns, tabs, spread, band = lax.optimization_barrier(
+        (spec, turns, tabs, spread, band)
     )
 
     current = []
@@ -345,19 +353,19 @@
     edges = pl.pallas_call(
         edge_kernel,
         out_shape=jax.ShapeDtypeStruct((2, REACH, block), f32),
-        in_specs=[vmem] * 5,
+        in_specs=[vmem] * 4,
         out_specs=vmem,
         compiler_params=pltpu.CompilerParams(vmem_limit_bytes=FILTER_VMEM),
         name="edge_bins",
-    )(from_left, outer, from_right, bands[2], bands[3])
+    )(from_left, outer, from_right, band)
     return pl.pallas_call(
         inner_kernel,
         out_shape=jax.ShapeDtypeStruct((block, bins_dev), f32),
-        in_specs=[vmem] * 5,
+        in_specs=[vmem] * 4,
         out_specs=vmem,
         compiler_params=pltpu.CompilerParams(vmem_limit_bytes=FILTER_VMEM),
         name="inner_bins",
-    )(outer, middle, edges, bands[0], bands[1])
+    )(outer, middle, edges, band)
 
 
 def solution(mesh):

time: 152 us -> 142 us (0.934)
  local copies, waits for them, and re-layouts: 19.2 us -> 12 us
  Pallas kernels: 34.1 us -> 30.3 us
  waiting for transfers between devices: 33.8 us -> 37 us
    all_to_all x1, waiting for transfers between devices: 4.89 us -> 14.1 us  [per_device(): lax.all_to_all(blocks, 'freq', split_axis=0, concat_axis=0, tiled=True)]
    cos x3, other arithmetic: 6.08 us -> 14 us  [turning(): return (jnp.cos(angle), jnp.sin(angle))]
    all_to_all x1, waiting for transfers between devices: 16.4 us -> 10.3 us  [per_device(): spec = lax.all_to_all(spec, 'freq', split_axis=0, concat_axis=0, tiled=True)]
    unnamed x41 -> x35, local copies, waits for them, and re-layouts: 8.39 us -> 3.81 us
    another operation x7 -> x2, other arithmetic: 5.45 us -> 1.14 us  [the longest x4 3.15 us: per_device(): jnp.stack(turning(count[1:], length), axis=1)]
    pallas_call x1, Pallas kernels: 3.41 us -> 0.83 us  [per_device(): pl.pallas_call(toeplitz_kernel, out_shape=jax.ShapeDtypeStruct((templates...]
    reshape x2, local copies, waits for them, and re-layouts: 4.85 us -> 2.62 us  [transform(): grid = blocks.transpose(1, 0, 2).reshape(rows, inner, LANES)]
    transpose x1, local copies, waits for them, and re-layouts: 2.83 us -> 0.61 us  [transform(): grid = blocks.transpose(1, 0, 2).reshape(rows, inner, LANES)]
  transfers between devices with their start and end apart: 10 -> 10, of which waited for: 5 -> 5; matrix products, arithmetic and copies ran while one was open for 18% -> 20% of each run, Pallas kernels for 11% -> 10%
where the time goes in v3:
time: 142 us
  waiting for transfers between devices  37 us (26%)
  starting transfers between devices  33.3 us (23%)
  Pallas kernels  30.3 us (21%)
  other arithmetic  24.8 us (17%)
  local copies, waits for them, and re-layouts  12 us (8%)
  matrix products  3.72 us (3%)
    pallas_call x2, Pallas kernels, per_device(): pl.pallas_call(functools.partial(sub_kernel, pair), out_shape=jax.ShapeDt...  26.2 us
    all_to_all x1, waiting for transfers between devices, per_device(): lax.all_to_all(blocks, 'freq', split_axis=0, concat_axis=0, tiled=True)  14.1 us
    cos x3, other arithmetic, turning(): return (jnp.cos(angle), jnp.sin(angle))  14 us
    all_to_all x1, starting transfers between devices, per_device(): lax.all_to_all(blocks, 'freq', split_axis=0, concat_axis=0, tiled=True)  11.5 us
    all_to_all x1, waiting for transfers between devices, per_device(): spec = lax.all_to_all(spec, 'freq', split_axis=0, concat_axis=0, tiled=True)  10.3 us
    ppermute x6, starting transfers between devices, per_device(): lax.ppermute(mine, 'band', [(j, j ^ half) for j in range(band_count)])  8.19 us
    ppermute x6, waiting for transfers between devices, per_device(): lax.ppermute(mine, 'band', [(j, j ^ half) for j in range(band_count)])  6.68 us
    all_to_all x1, starting transfers between devices, per_device(): spec = lax.all_to_all(spec, 'freq', split_axis=0, concat_axis=0, tiled=True)  6.56 us
  transfers between devices with their start and end apart: 10, of which 5 were waited for; matrix products, arithmetic and copies ran while one was open for 20% of the time, Pallas kernels for 10%

profile of v3, /device:TPU:32, one launch (start us, length us, event | category | flops | bytes accessed | tf_op | source)
XLA Modules:
  0.0 141.6 jit_solution(16138255850876842502)
XLA Ops:
  0.0 11.5 %all-to-all-start = ((f32[32,16,512]{2,1,0:T(8,128)}), f32[32,16,512]{2,1,0:T(8,128)S(1)}, u32[]{:S(2)}, u32[]{:S(2)}) async-start(f32[32,16,512]{2,1,0:T(8,128)} %bitcast.140), calls=%async_computation | async-start | bytes 2097152 | tf_op jit(solution)/shard_map/all_to_all | solution.py:307
  11.6 0.7 broadcast_add_fusion
  12.4 0.8 copy.47
  13.2 0.8 copy.45
  14.1 0.7 fusion.81
  14.8 1.2 and_select_fusion.4
  16.0 1.3 and_select_fusion
  17.5 0.7 slice.207
  18.4 0.8 toeplitz.1.band_ref
  19.2 0.6 stack.57
  19.8 0.6 iota_multiply_fusion.3
  20.4 0.6 iota_multiply_fusion.4
  21.0 0.5 iota_multiply_fusion.2
  21.5 0.6 compare_and_fusion
  22.4 0.6 slice_bitcast_fusion
  23.0 0.6 slice_bitcast_fusion.1
  23.6 1.0 select_multiply_fusion.1
  24.6 14.1 %all-to-all-done = f32[32,16,512]{2,1,0:T(8,128)S(1)} async-done(((f32[32,16,512]{2,1,0:T(8,128)}), f32[32,16,512]{2,1,0:T(8,128)S(1)}, u32[]{:S(2)}, u32[]{:S(2)}) %all-to-all-start) | async-done | bytes 1048608 | tf_op jit(solution)/shard_map/all_to_all | solution.py:307
  38.8 0.6 copy.38
  39.4 1.1 reshape.509
  40.4 1.6 %copy.40 = f32[16,128,128]{1,2,0:T(8,128)S(1)} copy(f32[16,128,128]{2,1,0:T(8,128)} %reshape.509) | data formatting | bytes 2097152 | tf_op jit(solution)/shard_map/reshape | solution.py:50
  42.0 1.2 fusion.54
  43.3 1.2 fusion.56
  44.9 0.5 copy-done.6
  45.3 1.2 fusion.13
  46.6 1.6 %copy.44 = f32[128,16,128]{2,1,0:T(8,128)} copy(f32[128,16,128]{2,0,1:T(8,128)S(1)} %fusion.13) | data formatting | bytes 2097152 | tf_op jit(solution)/shard_map/ckb,bm->mck/dot_general | solution.py:65
  48.2 6.6 %all-to-all-start.1 = ((f32[32,4,16,128]{3,2,1,0:T(8,128)}), f32[32,4,16,128]{3,2,1,0:T(8,128)}, u32[]{:S(2)}, u32[]{:S(2)}) async-start(f32[32,4,16,128]{3,2,1,0:T(8,128)} %bitcast.11), calls=%async_computation.1 | async-start | bytes 2097152 | tf_op jit(solution)/shard_map/all_to_all | solution.py:309
  54.9 1.7 %fusion.30 = (f32[2,128,128]{2,1,0:T(8,128)S(1)}, f32[2,128,128]{2,1,0:T(8,128)}) fusion(s32[128,128]{1,0:T(8,128)S(1)} %copy-done.7, s32[2]{0:T(128)S(1)} %copy-done.10, s32[128,128]{1,0:T(8,128)S(1)} %copy-done.8), kind=kLoop, calls=%fused_computation.72 | loop fusion | flops 917504 | bytes 393224 | tf_op jit(solution)/shard_map/cos | solution.py:25
  56.6 3.8 %fusion.22 = (f32[3,2,128,128]{3,2,1,0:T(8,128)}, f32[3,2,128,128]{3,2,1,0:T(8,128)}) fusion(s32[3,128,128]{2,1,0:T(8,128)S(1)} %slice.209, s32[2]{0:T(128)S(1)} %copy-done.10, s32[3,128,128]{2,1,0:T(8,128)S(1)} %copy-done.4), kind=kLoop, calls=%fused_computation.47 | loop fusion | flops 2752512 | bytes 1179656 | tf_op jit(solution)/shard_map/cos | solution.py:25
  60.6 8.5 %fusion.11.tab_ref = f32[9,2,256,128]{3,2,1,0:T(8,128)S(1)} fusion(s32[2]{0:T(128)S(1)} %copy-done.16, s32[9,256,128]{2,1,0:T(8,128)S(1)} %broadcast_multiply_fusion), kind=kLoop, calls=%fused_computation.23 | loop fusion | flops 8257536 | bytes 3538952 | tf_op jit(solution)/shard_map/cos | solution.py:25
  69.1 1.9 %fusion.8.spread_ref = bf16[8,4,128,256]{3,2,1,0:T(8,128)(2,1)} fusion(s32[256]{0:T(256)S(1)} %get-tuple-element.74, s32[256]{0:T(256)S(1)} %get-tuple-element.77, s32[256]{0:T(256)S(1)} %get-tuple-element.73, s32[256]{0:T(256)S(1)} %get-tuple-element.78, s32[4]{0:T(128)S(1)} %iota_multiply_fusion.1, s32[8]{0:T(128)S(1)} %copy-done.12, ...), kind=kLoop, calls=%fused_computation.18 | loop fusion | flops 24117248 | bytes 2101808 | tf_op jit(solution)/shard_map/convert_element_type | solution.py:85
  71.0 10.3 %all-to-all-done.1.spec_ref = f32[32,4,16,128]{3,2,1,0:T(8,128)} async-done(((f32[32,4,16,128]{3,2,1,0:T(8,128)}), f32[32,4,16,128]{3,2,1,0:T(8,128)}, u32[]{:S(2)}, u32[]{:S(2)}) %all-to-all-start.1) | async-done | bytes 1048608 | tf_op jit(solution)/shard_map/all_to_all | solution.py:309
  81.3 1.6 %copy-done = bf16[8,4,128,256]{3,2,1,0:T(8,128)(2,1)S(1)} copy-done((bf16[8,4,128,256]{3,2,1,0:T(8,128)(2,1)S(1)}, bf16[8,4,128,256]{3,2,1,0:T(8,128)(2,1)}, u32[]{:S(2)}) %copy-start) | copy-done | bytes 2097176
  82.9 0.9 copy-done.1
  83.8 13.2 %subband.2 = f32[2,128,128]{2,1,0:T(8,128)S(1)} custom-call(f32[32,4,16,128]{3,2,1,0:T(8,128)} %all-to-all-done.1.spec_ref, f32[9,2,256,128]{3,2,1,0:T(8,128)S(1)} %fusion.11.tab_ref, bf16[8,4,128,256]{3,2,1,0:T(8,128)(2,1)S(1)} %copy-done, f32[2,128,128]{2,1,0:T(8,128)S(1)} %copy-done.1), custom_call_target="tpu_custom_call" | custom-call | flops 10000000000 | bytes 8388608 | tf_op jit(solution)/shard_map/subband/pallas_call | solution.py:317
  97.1 13.0 %subband.3 = f32[2,128,128]{2,1,0:T(8,128)S(1)} custom-call(f32[32,4,16,128]{3,2,1,0:T(8,128)} %all-to-all-done.1.spec_ref, f32[9,2,256,128]{3,2,1,0:T(8,128)S(1)} %fusion.11.tab_ref, bf16[8,4,128,256]{3,2,1,0:T(8,128)(2,1)S(1)} %copy-done, f32[2,128,128]{2,1,0:T(8,128)S(1)} %get-tuple-element.18.tw_ref), custom_call_target="tpu_custom_call" | custom-call | flops 10000000000 | bytes 8388608 | tf_op jit(solution)/shard_map/subband/pallas_call | solution.py:317
  110.2 0.5 collective-permute-start.3
  110.7 1.6 %collective-permute-start.1 = (f32[2,128,128]{2,1,0:T(8,128)S(1)}, f32[2,128,128]{2,1,0:T(8,128)S(1)}, u32[]{:S(2)}, u32[]{:S(2)}) collective-permute-start(f32[2,128,128]{2,1,0:T(8,128)S(1)} %pad_maximum_fusion.1), channel_id=1, source_target_pairs={{0,64},{32,96},{64,0},{96,32},{128,192},{160,224},{192,128},{224,1... | collective-permute-start | bytes 393224 | tf_op jit(solution)/shard_map/ppermute | solution.py:339
  112.4 0.9 collective-permute-start.4
  113.3 3.9 %collective-permute-done.1 = f32[2,128,128]{2,1,0:T(8,128)S(1)} collective-permute-done((f32[2,128,128]{2,1,0:T(8,128)S(1)}, f32[2,128,128]{2,1,0:T(8,128)S(1)}, u32[]{:S(2)}, u32[]{:S(2)}) %collective-permute-start.1) | collective-permute-done | bytes 131104 | tf_op jit(solution)/shard_map/ppermute | solution.py:339
  117.2 3.1 %collective-permute-start.2 = (f32[2,128,128]{2,1,0:T(8,128)S(1)}, f32[2,128,128]{2,1,0:T(8,128)S(1)}, u32[]{:S(2)}, u32[]{:S(2)}) collective-permute-start(f32[2,128,128]{2,1,0:T(8,128)S(1)} %pad_maximum_fusion.2), channel_id=1, source_target_pairs={{0,128},{32,160},{64,192},{96,224},{128,0},{160,32},{192,64},{224,... | collective-permute-start | bytes 393224 | tf_op jit(solution)/shard_map/ppermute | solution.py:339
  120.4 2.0 %collective-permute-start.5 = (f32[2,128,128]{2,1,0:T(8,128)S(1)}, f32[2,128,128]{2,1,0:T(8,128)S(1)}, u32[]{:S(2)}, u32[]{:S(2)}) collective-permute-start(f32[2,128,128]{2,1,0:T(8,128)S(1)} %pad_maximum_fusion.4), channel_id=1, source_target_pairs={{0,128},{32,160},{64,192},{96,224},{128,0},{160,32},{192,64},{224,... | collective-permute-start | bytes 393224 | tf_op jit(solution)/shard_map/ppermute | solution.py:339
  122.5 2.8 %collective-permute-done.2 = f32[2,128,128]{2,1,0:T(8,128)S(1)} collective-permute-done((f32[2,128,128]{2,1,0:T(8,128)S(1)}, f32[2,128,128]{2,1,0:T(8,128)S(1)}, u32[]{:S(2)}, u32[]{:S(2)}) %collective-permute-start.2) | collective-permute-done | bytes 131104 | tf_op jit(solution)/shard_map/ppermute | solution.py:339
  125.3 5.1 %collective-permute-start.7 = (f32[2,32,128]{2,1,0:T(8,128)S(1)}, f32[2,32,128]{2,1,0:T(8,128)S(1)}, u32[]{:S(2)}, u32[]{:S(2)}) collective-permute-start(f32[2,32,128]{2,1,0:T(8,128)S(1)} %get-tuple-element.51), channel_id=1, source_target_pairs={{1,0},{2,1},{3,2},{4,3},{5,4},{6,5},{7,6},{8,7},{9,8},{10,9},{11,1... | collective-permute-start | bytes 98312 | tf_op jit(solution)/shard_map/ppermute | solution.py:352
  130.4 1.9 %collective-permute-start.6 = (f32[2,32,128]{2,1,0:T(8,128)S(1)}, f32[2,32,128]{2,1,0:T(8,128)S(1)}, u32[]{:S(2)}, u32[]{:S(2)}) collective-permute-start(f32[2,32,128]{2,1,0:T(8,128)S(1)} %get-tuple-element.52), channel_id=1, source_target_pairs={{0,1},{1,2},{2,3},{3,4},{4,5},{5,6},{6,7},{7,8},{8,9},{9,10},{10,1... | collective-permute-start | bytes 98312 | tf_op jit(solution)/shard_map/ppermute | solution.py:349
  132.5 5.9 %collective-permute-done.6.left_ref = f32[2,32,128]{2,1,0:T(8,128)S(1)} collective-permute-done((f32[2,32,128]{2,1,0:T(8,128)S(1)}, f32[2,32,128]{2,1,0:T(8,128)S(1)}, u32[]{:S(2)}, u32[]{:S(2)}) %collective-permute-start.6) | collective-permute-done | bytes 32800 | tf_op jit(solution)/shard_map/ppermute | solution.py:349
  138.4 0.7 edge_bins.1.edge_ref
  139.1 2.5 %inner_bins.1 = f32[128,256]{1,0:T(8,128)} custom-call(f32[2,128,128]{2,1,0:T(8,128)S(1)} %pad_maximum_fusion.outer_ref, f32[2,128,128]{2,1,0:T(8,128)S(1)} %pad_maximum_fusion.5.mid_ref, f32[2,32,128]{2,1,0:T(8,128)S(1)} %edge_bins.1.edge_ref, bf16[2048,256]{1,0:T(8,128)(2,1)S(1)} %toeplitz.1.band_ref), custom_call_target="tpu_custom_call" | custom-call | tf_op jit(solution)/shard_map/inner_bins/pallas_call | solution.py:361
  (75 shorter events, 1.9 us)
Async XLA Ops:
  0.0 13.1 %copy-start.9 = (s32[512,64]{0,1:T(8,128)S(1)}, s32[512,64]{0,1:T(8,128)}, u32[]{:S(2)}) copy-start(s32[512,64]{0,1:T(8,128)} %param.11) | copy-start | bytes 393220
  0.0 14.1 %copy-start.15 = (s32[15]{0:T(128)S(1)}, s32[15]{0:T(128)}, u32[]{:S(2)}) copy-start(s32[15]{0:T(128)} %param.12) | copy-start | bytes 184
  0.0 38.8 %all-to-all-start = ((f32[32,16,512]{2,1,0:T(8,128)}), f32[32,16,512]{2,1,0:T(8,128)S(1)}, u32[]{:S(2)}, u32[]{:S(2)}) async-start(f32[32,16,512]{2,1,0:T(8,128)} %bitcast.140), calls=%async_computation | async-start | bytes 2097152 | tf_op jit(solution)/shard_map/all_to_all | solution.py:307
  44.5 0.8 copy-start.6
  46.6 8.2 %copy-start.7 = (s32[128,128]{1,0:T(8,128)S(1)}, s32[128,128]{1,0:T(8,128)}, u32[]{:S(2)}) copy-start(s32[128,128]{1,0:T(8,128)} %slice_bitcast_fusion) | copy-start | bytes 196612
  46.6 8.2 %copy-start.8 = (s32[128,128]{1,0:T(8,128)S(1)}, s32[128,128]{1,0:T(8,128)}, u32[]{:S(2)}) copy-start(s32[128,128]{1,0:T(8,128)} %slice_bitcast_fusion.1) | copy-start | bytes 196612
  46.6 8.2 %copy-start.10 = (s32[2]{0:T(128)S(1)}, s32[2]{0:T(128)}, u32[]{:S(2)}) copy-start(s32[2]{0:T(128)} %iota_multiply_fusion.3) | copy-start | bytes 28
  46.6 9.9 %copy-start.4 = (s32[3,128,128]{2,1,0:T(8,128)S(1)}, s32[3,128,128]{2,1,0:T(8,128)}, u32[]{:S(2)}) copy-start(s32[3,128,128]{2,1,0:T(8,128)} %slice.207) | copy-start | bytes 589828
  48.2 12.1 %copy-start.5 = (s32[256,128]{1,0:T(8,128)S(1)}, s32[256,128]{1,0:T(8,128)}, u32[]{:S(2)}) copy-start(s32[256,128]{1,0:T(8,128)} %copy.45) | copy-start | bytes 393220
  48.2 12.1 %copy-start.11 = (s32[9]{0:T(128)S(1)}, s32[9]{0:T(128)}, u32[]{:S(2)}) copy-start(s32[9]{0:T(128)} %stack.57) | copy-start | bytes 112
  48.2 33.1 %all-to-all-start.1 = ((f32[32,4,16,128]{3,2,1,0:T(8,128)}), f32[32,4,16,128]{3,2,1,0:T(8,128)}, u32[]{:S(2)}, u32[]{:S(2)}) async-start(f32[32,4,16,128]{3,2,1,0:T(8,128)} %bitcast.11), calls=%async_computation.1 | async-start | bytes 2097152 | tf_op jit(solution)/shard_map/all_to_all | solution.py:309
  54.8 5.7 %copy-start.16 = (s32[2]{0:T(128)S(1)}, s32[2]{0:T(128)}, u32[]{:S(2)}) copy-start(s32[2]{0:T(128)} %iota_multiply_fusion.4) | copy-start | bytes 28
  60.4 8.7 %copy-start.12 = (s32[8]{0:T(128)S(1)}, s32[8]{0:T(128)}, u32[]{:S(2)}) copy-start(s32[8]{0:T(128)} %iota_multiply_fusion.2) | copy-start | bytes 100
  60.4 8.7 %copy-start.13 = (pred[256]{0:T(512)(128)(4,1)S(1)}, pred[256]{0:T(512)(128)(4,1)}, u32[]{:S(2)}) copy-start(pred[256]{0:T(512)(128)(4,1)} %get-tuple-element.75) | copy-start | bytes 772
  60.4 8.7 %copy-start.14 = (pred[256]{0:T(512)(128)(4,1)S(1)}, pred[256]{0:T(512)(128)(4,1)}, u32[]{:S(2)}) copy-start(pred[256]{0:T(512)(128)(4,1)} %get-tuple-element.76) | copy-start | bytes 772
  81.3 1.6 %copy-start = (bf16[8,4,128,256]{3,2,1,0:T(8,128)(2,1)S(1)}, bf16[8,4,128,256]{3,2,1,0:T(8,128)(2,1)}, u32[]{:S(2)}) copy-start(bf16[8,4,128,256]{3,2,1,0:T(8,128)(2,1)} %fusion.8.spread_ref) | copy-start | bytes 6291460
  82.9 0.9 copy-start.1
  97.0 13.6 %copy-start.3 = (f32[3,2,128,128]{3,2,1,0:T(8,128)S(1)}, f32[3,2,128,128]{3,2,1,0:T(8,128)}, u32[]{:S(2)}) copy-start(f32[3,2,128,128]{3,2,1,0:T(8,128)} %get-tuple-element.17) | copy-start | bytes 1179652
  97.0 15.3 %copy-start.2 = (f32[3,2,128,128]{3,2,1,0:T(8,128)S(1)}, f32[3,2,128,128]{3,2,1,0:T(8,128)}, u32[]{:S(2)}) copy-start(f32[3,2,128,128]{3,2,1,0:T(8,128)} %get-tuple-element.19) | copy-start | bytes 1179652
  97.0 13.6 %collective-permute-start = (f32[2,128,128]{2,1,0:T(8,128)S(1)}, f32[2,128,128]{2,1,0:T(8,128)S(1)}, u32[]{:S(2)}, u32[]{:S(2)}) collective-permute-start(f32[2,128,128]{2,1,0:T(8,128)S(1)} %subband.2), channel_id=1, source_target_pairs={{0,32},{32,0},{64,96},{96,64},{128,160},{160,128},{192,224},{224,1... | collective-permute-start | bytes 393224 | tf_op jit(solution)/shard_map/ppermute | solution.py:339
  110.2 2.1 %collective-permute-start.3 = (f32[2,128,128]{2,1,0:T(8,128)S(1)}, f32[2,128,128]{2,1,0:T(8,128)S(1)}, u32[]{:S(2)}, u32[]{:S(2)}) collective-permute-start(f32[2,128,128]{2,1,0:T(8,128)S(1)} %subband.3), channel_id=1, source_target_pairs={{0,32},{32,0},{64,96},{96,64},{128,160},{160,128},{192,224},{224,1... | collective-permute-start | bytes 393224 | tf_op jit(solution)/shard_map/ppermute | solution.py:339
  110.7 6.4 %collective-permute-start.1 = (f32[2,128,128]{2,1,0:T(8,128)S(1)}, f32[2,128,128]{2,1,0:T(8,128)S(1)}, u32[]{:S(2)}, u32[]{:S(2)}) collective-permute-start(f32[2,128,128]{2,1,0:T(8,128)S(1)} %pad_maximum_fusion.1), channel_id=1, source_target_pairs={{0,64},{32,96},{64,0},{96,32},{128,192},{160,224},{192,128},{224,1... | collective-permute-start | bytes 393224 | tf_op jit(solution)/shard_map/ppermute | solution.py:339
  112.4 8.0 %collective-permute-start.4 = (f32[2,128,128]{2,1,0:T(8,128)S(1)}, f32[2,128,128]{2,1,0:T(8,128)S(1)}, u32[]{:S(2)}, u32[]{:S(2)}) collective-permute-start(f32[2,128,128]{2,1,0:T(8,128)S(1)} %pad_maximum_fusion.3), channel_id=1, source_target_pairs={{0,64},{32,96},{64,0},{96,32},{128,192},{160,224},{192,128},{224,1... | collective-permute-start | bytes 393224 | tf_op jit(solution)/shard_map/ppermute | solution.py:339
  117.2 8.0 %collective-permute-start.2 = (f32[2,128,128]{2,1,0:T(8,128)S(1)}, f32[2,128,128]{2,1,0:T(8,128)S(1)}, u32[]{:S(2)}, u32[]{:S(2)}) collective-permute-start(f32[2,128,128]{2,1,0:T(8,128)S(1)} %pad_maximum_fusion.2), channel_id=1, source_target_pairs={{0,128},{32,160},{64,192},{96,224},{128,0},{160,32},{192,64},{224,... | collective-permute-start | bytes 393224 | tf_op jit(solution)/shard_map/ppermute | solution.py:339
  120.4 12.0 %collective-permute-start.5 = (f32[2,128,128]{2,1,0:T(8,128)S(1)}, f32[2,128,128]{2,1,0:T(8,128)S(1)}, u32[]{:S(2)}, u32[]{:S(2)}) collective-permute-start(f32[2,128,128]{2,1,0:T(8,128)S(1)} %pad_maximum_fusion.4), channel_id=1, source_target_pairs={{0,128},{32,160},{64,192},{96,224},{128,0},{160,32},{192,64},{224,... | collective-permute-start | bytes 393224 | tf_op jit(solution)/shard_map/ppermute | solution.py:339
  125.3 7.2 %collective-permute-start.7 = (f32[2,32,128]{2,1,0:T(8,128)S(1)}, f32[2,32,128]{2,1,0:T(8,128)S(1)}, u32[]{:S(2)}, u32[]{:S(2)}) collective-permute-start(f32[2,32,128]{2,1,0:T(8,128)S(1)} %get-tuple-element.51), channel_id=1, source_target_pairs={{1,0},{2,1},{3,2},{4,3},{5,4},{6,5},{7,6},{8,7},{9,8},{10,9},{11,1... | collective-permute-start | bytes 98312 | tf_op jit(solution)/shard_map/ppermute | solution.py:352
  130.4 7.9 %collective-permute-start.6 = (f32[2,32,128]{2,1,0:T(8,128)S(1)}, f32[2,32,128]{2,1,0:T(8,128)S(1)}, u32[]{:S(2)}, u32[]{:S(2)}) collective-permute-start(f32[2,32,128]{2,1,0:T(8,128)S(1)} %get-tuple-element.52), channel_id=1, source_target_pairs={{0,1},{1,2},{2,3},{3,4},{4,5},{5,6},{6,7},{7,8},{8,9},{9,10},{10,1... | collective-permute-start | bytes 98312 | tf_op jit(solution)/shard_map/ppermute | solution.py:349

commit v4 on v3

--- a/solution.py
+++ b/solution.py
@@ -15,7 +15,6 @@
 FILTER_VMEM = 8 * 2**20
 
 two_pi = 2.0 * math.pi
-top_precision = lax.Precision.HIGHEST
 f32 = jnp.float32
 bf16 = jnp.bfloat16
 
@@ -44,28 +43,50 @@
     return high, (value - high.astype(f32)).astype(bf16)
 
 
-def transform(blocks, length):
-    sources, rows, samp = blocks.shape
+def transform_tables(length):
     inner = length // LANES
-    grid = blocks.transpose(1, 0, 2).reshape(rows, inner, LANES)
     index = lax.iota(jnp.int32, LANES)
-    cos_first, sin_first = turning(index[:, None] * index[None, :], inner)
-    part_re = jnp.einsum("cab,ak->ckb", grid, cos_first, precision=top_precision)
-    part_im = -jnp.einsum("cab,ak->ckb", grid, sin_first, precision=top_precision)
-    cos_twist, sin_twist = turning(index[:, None] * index[None, :], length)
-    part_re, part_im = rotate(part_re, part_im, cos_twist, sin_twist)
-    column = lax.iota(jnp.int32, LANES)
-    kept = column // 4 * 2 + column % 2
-    imag_col = (column // 2 % 2 == 1)[None, :]
-    cos_second, sin_second = turning(index[:, None] * kept[None, :], LANES)
+    sources = LANES // 4
+    block_no = index % sources * 4 + index // sources
+    cos_first, sin_first = turning(index[:, None] * block_no[None, :], inner)
+    first = jnp.concatenate([cos_first, -sin_first], axis=0)
+    twist = turning_pair(index[:, None] * index[None, :], length, 0)
+    kept = index // 4 * 2 + index % 2
+    imag_row = (index // 2 % 2 == 1)[:, None]
+    cos_second, sin_second = turning(kept[:, None] * index[None, :], LANES)
     scale = 1.0 / math.sqrt(length) / 16.0 / 4.0
-    from_re = jnp.where(imag_col, -sin_second, cos_second) * scale
-    from_im = jnp.where(imag_col, cos_second, sin_second) * scale
-    both = jnp.concatenate([part_re, part_im], axis=2)
-    out = jnp.einsum(
-        "ckb,bm->mck", both, jnp.concatenate([from_re, from_im], axis=0), precision=top_precision
-    )
-    return out.reshape(LANES // 4, 4, rows, LANES)
+    from_re = jnp.where(imag_row, -sin_second, cos_second) * scale
+    from_im = jnp.where(imag_row, cos_second, sin_second) * scale
+    return first, twist, jnp.concatenate([from_re, from_im], axis=1)
+
+
+def transform_kernel(blocks_ref, first_ref, twist_ref, second_ref, out_ref, tall):
+    channels = out_ref.shape[0] // LANES
+    held = blocks_ref.shape[0]
+    for r in range(blocks_ref.shape[1] // LANES):
+        tall[r * held : (r + 1) * held, :] = blocks_ref[:, r * LANES : (r + 1) * LANES]
+    first = jnp.concatenate(split_bf16(first_ref[...]), axis=1)
+    second_high, second_low = split_bf16(second_ref[...])
+    second = jnp.concatenate([second_high, second_low], axis=0)
+    across = (((1,), (1,)), ((), ()))
+    for pair in range(channels // 2):
+        mine = (2 * pair, 2 * pair + 1)
+        columns = [tall[pl.ds(c, LANES, stride=channels), :] for c in mine]
+        part = products(first, *windows(jnp.concatenate(columns, axis=1)))
+        rows = []
+        for j in range(2):
+            lanes = slice(j * LANES, (j + 1) * LANES)
+            turned = rotate(part[:LANES, lanes], part[LANES:, lanes], twist_ref[0], twist_ref[1])
+            rows.append(jnp.concatenate(turned, axis=1))
+        high, low = split_bf16(jnp.concatenate(rows, axis=0))
+        got = lax.dot_general(second, high, across, preferred_element_type=f32)
+        got = (
+            got[:LANES]
+            + got[LANES:]
+            + lax.dot_general(second_high, low, across, preferred_element_type=f32)
+        )
+        for j, c in enumerate(mine):
+            out_ref[pl.ds(c, LANES, stride=channels), :] = got[:, j * LANES : (j + 1) * LANES]
 
 
 def delay_turns(channel_delay, first_bin, length):
@@ -209,41 +230,26 @@
     return re * re + im * im
 
 
-def edge_kernel(left_ref, outer_ref, right_ref, band_ref, out_ref):
+def filter_kernel(outer_ref, rest_ref, band_ref, out_ref):
     near = 2 * REACH
-    pad = jnp.zeros((LANES - 3 * REACH, LANES), f32)
+    mid = rest_ref.shape[1] - near
     columns = [
-        jnp.concatenate([left_ref[x], outer_ref[x, :near], pad], axis=0) for x in range(2)
-    ] + [jnp.concatenate([outer_ref[x, near:], right_ref[x], pad], axis=0) for x in range(2)]
-    high, low = windows(jnp.concatenate(columns, axis=1))
-    per = 8
-    best = [jnp.zeros((REACH, LANES), f32)] * 2
-    for step in range(band_ref.shape[0] // (per * near)):
-        first = step * per * near
-        band = jnp.concatenate(
-            [band_ref[first + i * near : first + i * near + REACH, :] for i in range(per)], axis=0
-        )
-        got = products(band, high, low)
-        for i in range(per):
-            mine = got[i * REACH : (i + 1) * REACH]
-            for side in range(2):
-                lanes = slice(side * 2 * LANES, (side + 1) * 2 * LANES)
-                best[side] = jnp.maximum(best[side], power(mine[:, lanes]))
-    out_ref[0] = best[0]
-    out_ref[1] = best[1]
-
-
-def inner_kernel(outer_ref, mid_ref, edge_ref, band_ref, out_ref):
-    near = 2 * REACH
-    blocks = out_ref.shape[1] // near - 1
-    columns = [
-        jnp.concatenate([outer_ref[x, :near], mid_ref[x], outer_ref[x, near:]], axis=0)
+        jnp.concatenate(
+            [
+                rest_ref[x, mid : mid + REACH],
+                outer_ref[x, :near],
+                rest_ref[x, :mid],
+                outer_ref[x, near:],
+                rest_ref[x, mid + REACH :],
+            ],
+            axis=0,
+        )
         for x in range(2)
     ]
     whole = jnp.concatenate(columns, axis=1)
     per = 4
     best = []
-    for i in range(blocks):
+    for i in range(out_ref.shape[1] // near):
         high, low = windows(whole[i * near : i * near + LANES])
         mine = jnp.zeros((near, LANES), f32)
         for step in range(band_ref.shape[0] // (per * near)):
@@ -252,7 +258,7 @@
             for j in range(per):
                 mine = jnp.maximum(mine, power(got[j * near : (j + 1) * near]))
         best.append(mine)
-    out_ref[...] = jnp.concatenate([edge_ref[0]] + best + [edge_ref[1]], axis=0).T
+    out_ref[...] = jnp.concatenate(best, axis=0).T
 
 
 def per_device(samples, channel_delay, merge_slope, tap_offset, tap_weight):
@@ -284,10 +290,15 @@
     turns = []
     for pair in chunks:
         bins_index = jnp.concatenate([first_bin + q * quarter + within for q in pair])
+        if pair == chunks[1]:
+            reach = lax.iota(jnp.int32, REACH)
+            bins_index = jnp.concatenate(
+                [bins_index, first_bin - REACH + reach, first_bin + bins_dev + reach]
+            )
         count = shifts[:, None, :] * bins_index[None, :, None]
         turns.append(
             (
-                turning_pair(count[0], length, 0),
+                turning_pair(count[0, : 2 * quarter], length, 0),
                 turning_pair(count[1:], length, 1),
             )
         )
@@ -303,10 +314,21 @@
         name="toeplitz",
     )(profile)
 
+    tables = transform_tables(length)
     blocks = samples.reshape(freq_count, chan_dev // freq_count, samp_dev)
     blocks = lax.all_to_all(blocks, "freq", split_axis=0, concat_axis=0, tiled=True)
-    spec = transform(blocks, length)
+    spec = pl.pallas_call(
+        transform_kernel,
+        out_shape=jax.ShapeDtypeStruct((chan_dev // freq_count * LANES, LANES), f32),
+        in_specs=[vmem] * 4,
+        out_specs=vmem,
+        scratch_shapes=[pltpu.VMEM((chan_dev // freq_count * LANES, LANES), f32)],
+        compiler_params=pltpu.CompilerParams(vmem_limit_bytes=FILTER_VMEM),
+        name="transform",
+    )(blocks.reshape(chan_dev, samp_dev), *tables)
+    spec = spec.reshape(freq_count, chan_dev * 4 // freq_count, LANES)
     spec = lax.all_to_all(spec, "freq", split_axis=0, concat_axis=0, tiled=True)
+    spec = spec.reshape(freq_count, 4, chan_dev // freq_count, LANES)
     spec, turns, tabs, spread, band = lax.optimization_barrier(
         (spec, turns, tabs, spread, band)
     )
@@ -332,6 +354,12 @@
             )(spec, tabs, spread, turn[0])
         )
 
+    ends = freq_count - 1
+    from_left = lax.ppermute(
+        current[0][:, bins_dev // 2 - REACH :], "freq", [(i, i + 1) for i in range(ends)]
+    )
+    from_right = lax.ppermute(current[0][:, :REACH], "freq", [(i + 1, i) for i in range(ends)])
+    current[1] = jnp.concatenate([current[1], from_left, from_right], axis=1)
     for s in range(1, sections):
         half = 1 << (s - 1)
         for i in range(len(chunks)):
@@ -344,28 +372,14 @@
             up_re, up_im = rotate(upper[0], upper[1], turn[0], turn[1])
             current[i] = jnp.stack([lower[0] + up_re, lower[1] + up_im])
 
-    outer, middle = current
-    ends = freq_count - 1
-    from_left = lax.ppermute(
-        outer[:, bins_dev // 2 - REACH :], "freq", [(i, i + 1) for i in range(ends)]
-    )
-    from_right = lax.ppermute(outer[:, :REACH], "freq", [(i + 1, i) for i in range(ends)])
-    edges = pl.pallas_call(
-        edge_kernel,
-        out_shape=jax.ShapeDtypeStruct((2, REACH, block), f32),
-        in_specs=[vmem] * 4,
+    return pl.pallas_call(
+        filter_kernel,
+        out_shape=jax.ShapeDtypeStruct((block, bins_dev), f32),
+        in_specs=[vmem] * 3,
         out_specs=vmem,
         compiler_params=pltpu.CompilerParams(vmem_limit_bytes=FILTER_VMEM),
-        name="edge_bins",
-    )(from_left, outer, from_right, band)
-    return pl.pallas_call(
-        inner_kernel,
-        out_shape=jax.ShapeDtypeStruct((block, bins_dev), f32),
-        in_specs=[vmem] * 4,
-        out_specs=vmem,
-        compiler_params=pltpu.CompilerParams(vmem_limit_bytes=FILTER_VMEM),
-        name="inner_bins",
-    )(outer, middle, edges, band)
+        name="templates",
+    )(current[0], current[1], band)
 
 
 def solution(mesh):

time: 142 us -> 138 us (0.972)
  local copies, waits for them, and re-layouts: 12 us -> 6.35 us
  matrix products: 3.72 us -> 0 us
  waiting for transfers between devices: 37 us -> 39.9 us
  other arithmetic: 24.8 us -> 26.8 us
    ppermute x6, waiting for transfers between devices: 6.68 us -> 16.6 us  [per_device(): lax.ppermute(mine, 'band', [(j, j ^ half) for j in range(band_count)])]
    ppermute x2, waiting for transfers between devices: 5.87 us -> 0.01 us  [the longest x1 0.01 us: per_device(): lax.ppermute(current[0][:, bins_dev // 2 - REACH:], 'freq', [(i, i + 1) f...]
    cos x3 -> x5, other arithmetic: 14 us -> 17.1 us  [turning(): return (jnp.cos(angle), jnp.sin(angle))]
    pallas_call x2, Pallas kernels: 3.26 us -> 6.04 us  [the longest x1 3.08 us: per_device(): pl.pallas_call(filter_kernel, out_shape=jax.ShapeDtypeStruct((block, bins...]
    pallas_call x2, Pallas kernels: 26.2 us -> 23.5 us  [per_device(): pl.pallas_call(functools.partial(sub_kernel, pair), out_shape=jax.ShapeDt...]
    reshape x2 -> x0, local copies, waits for them, and re-layouts: 2.62 us -> none  [transform(): grid = blocks.transpose(1, 0, 2).reshape(rows, inner, LANES)]
    unnamed x2 -> x0, matrix products: 2.48 us -> none
    dot_general x1 -> x0, local copies, waits for them, and re-layouts: 1.61 us -> none  [transform(): jnp.einsum('ckb,bm->mck', both, jnp.concatenate([from_re, from_im], axis=...]
  transfers between devices with their start and end apart: 10 -> 10, of which waited for: 5 -> 6; matrix products, arithmetic and copies ran while one was open for 20% -> 22% of each run, Pallas kernels for 10% -> 9%
where the time goes in v4:
time: 138 us; the launch traced here: 137 us
  waiting for transfers between devices  39.9 us (29%)
  starting transfers between devices  33.6 us (24%)
  Pallas kernels  30.4 us (22%)
  other arithmetic  26.8 us (19%)
  local copies, waits for them, and re-layouts  6.35 us (5%)
    pallas_call x2, Pallas kernels, per_device(): pl.pallas_call(functools.partial(sub_kernel, pair), out_shape=jax.ShapeDt...  23.5 us
    cos x5, other arithmetic, turning(): return (jnp.cos(angle), jnp.sin(angle))  17.1 us
    ppermute x6, waiting for transfers between devices, per_device(): lax.ppermute(mine, 'band', [(j, j ^ half) for j in range(band_count)])  16.6 us
    all_to_all x1, waiting for transfers between devices, per_device(): lax.all_to_all(blocks, 'freq', split_axis=0, concat_axis=0, tiled=True)  14.3 us
    all_to_all x1, starting transfers between devices, per_device(): lax.all_to_all(blocks, 'freq', split_axis=0, concat_axis=0, tiled=True)  11.5 us
    all_to_all x1, waiting for transfers between devices, per_device(): spec = lax.all_to_all(spec, 'freq', split_axis=0, concat_axis=0, tiled=True)  9 us
    ppermute x6, starting transfers between devices, per_device(): lax.ppermute(mine, 'band', [(j, j ^ half) for j in range(band_count)])  7.66 us
    all_to_all x1, starting transfers between devices, per_device(): spec = lax.all_to_all(spec, 'freq', split_axis=0, concat_axis=0, tiled=True)  6.5 us
  transfers between devices with their start and end apart: 10, of which 6 were waited for; matrix products, arithmetic and copies ran while one was open for 22% of the time, Pallas kernels for 9%

profile of v4, /device:TPU:32, one launch (start us, length us, event | category | flops | bytes accessed | tf_op | source)
XLA Modules:
  0.0 137.4 jit_solution(658058402425332642)
XLA Ops:
  0.0 11.5 %all-to-all-start = ((f32[32,16,512]{2,1,0:T(8,128)}), f32[32,16,512]{2,1,0:T(8,128)S(1)}, u32[]{:S(2)}, u32[]{:S(2)}) async-start(f32[32,16,512]{2,1,0:T(8,128)} %bitcast.123), calls=%async_computation | async-start | bytes 2097152 | tf_op jit(solution)/shard_map/all_to_all | solution.py:319
  11.6 0.6 iota_multiply_fusion.4
  12.2 0.6 iota_multiply_fusion.2
  12.7 0.7 broadcast_add_fusion
  13.5 0.8 copy.17
  14.3 0.1 copy.15
  14.5 0.7 fusion.68
  15.2 1.3 and_select_fusion.4
  16.5 1.2 and_select_fusion
  17.7 0.1 broadcast_multiply_fusion.2
  17.8 0.7 slice.207
  18.5 0.1 pad_add_fusion.2
  18.6 0.1 broadcast_multiply_fusion.1
  18.7 0.7 slice.209
  19.4 0.2 select_reduce_fusion.profile_ref
  19.6 0.8 toeplitz.1.band_ref
  20.5 0.7 stack.57
  21.2 0.5 compare_and_fusion
  21.7 0.6 iota_shift-right-logical_fusion
  22.3 0.3 select_multiply_fusion.1
  22.7 0.3 fusion.59
  23.0 1.5 %fusion.29 = (f32[2,128,128]{2,1,0:T(8,128)S(1)}, f32[2,128,128]{2,1,0:T(8,128)S(1)}, f32[2,128,128]{2,1,0:T(8,128)S(1)}) fusion(s32[128,128]{1,0:T(8,128)S(1)} %slice_bitcast_fusion, s32[2]{0:T(128)S(1)} %iota_multiply_fusion.3, s32[128,128]{1,0:T(8,128)S(1)} %slice_bitcast_fusion.1, s32[128,128]{1,0:T(8,128)S(1)} %iota_multiply_fusion), kind=kLoop, calls=%fused_computation.74 | loop fusion | flops 1376256 | bytes 589832 | tf_op jit(solution)/shard_map/cos | solution.py:24
  24.5 14.3 %all-to-all-done = f32[32,16,512]{2,1,0:T(8,128)S(1)} async-done(((f32[32,16,512]{2,1,0:T(8,128)}), f32[32,16,512]{2,1,0:T(8,128)S(1)}, u32[]{:S(2)}, u32[]{:S(2)}) %all-to-all-start) | async-done | bytes 1048608 | tf_op jit(solution)/shard_map/all_to_all | solution.py:319
  38.8 3.0 %transform.1 = f32[2048,128]{1,0:T(8,128)} custom-call(f32[512,512]{1,0:T(8,128)S(1)} %bitcast.120, f32[256,128]{1,0:T(8,128)S(1)} %pad_maximum_fusion.4.first_ref, f32[2,128,128]{2,1,0:T(8,128)S(1)} %get-tuple-element.57.twist_ref, f32[128,256]{1,0:T(8,128)S(1)} %pad_maximum_fusion.5.second_ref), custom_call_target="tpu_custom_call" | custom-call | tf_op jit(solution)/shard_map/transform/pallas_call | solution.py:320
  41.7 6.5 %all-to-all-start.1 = ((f32[32,64,128]{2,1,0:T(8,128)}), f32[32,64,128]{2,1,0:T(8,128)S(1)}, u32[]{:S(2)}, u32[]{:S(2)}) async-start(f32[32,64,128]{2,1,0:T(8,128)} %bitcast.2), calls=%async_computation.1 | async-start | bytes 2097152 | tf_op jit(solution)/shard_map/all_to_all | solution.py:330
  48.3 2.4 %fusion.19 = f32[3,2,128,128]{3,2,1,0:T(8,128)S(1)} fusion(s32[2]{0:T(128)S(1)} %iota_multiply_fusion.3, s32[3,128,128]{2,1,0:T(8,128)} %slice.207), kind=kLoop, calls=%fused_computation.42 | loop fusion | flops 1376256 | bytes 589832 | tf_op jit(solution)/shard_map/cos | solution.py:24
  50.7 3.2 %fusion.15 = f32[3,2,192,128]{3,2,1,0:T(8,128)S(1)} fusion(s32[2]{0:T(128)S(1)} %iota_multiply_fusion.3, s32[3,192,128]{2,1,0:T(8,128)} %slice.209), kind=kLoop, calls=%fused_computation.37 | loop fusion | flops 2064384 | bytes 884744 | tf_op jit(solution)/shard_map/cos | solution.py:24
  53.9 0.2 broadcast_multiply_fusion
  54.1 9.7 %fusion.11.tab_ref = f32[9,2,256,128]{3,2,1,0:T(8,128)} fusion(s32[2]{0:T(128)S(1)} %copy-done.9, s32[9,256,128]{2,1,0:T(8,128)S(1)} %broadcast_multiply_fusion), kind=kLoop, calls=%fused_computation.23 | loop fusion | flops 8257536 | bytes 3538952 | tf_op jit(solution)/shard_map/cos | solution.py:24
  63.8 1.9 %fusion.8.spread_ref = bf16[8,4,128,256]{3,2,1,0:T(8,128)(2,1)} fusion(s32[256]{0:T(256)S(1)} %copy-done.3, s32[256]{0:T(256)S(1)} %get-tuple-element.74, s32[256]{0:T(256)S(1)} %get-tuple-element.70, s32[256]{0:T(256)S(1)} %get-tuple-element.75, s32[4]{0:T(128)S(1)} %iota_multiply_fusion.1, s32[8]{0:T(128)S(1)} %copy-done.5, ...), kind=kLoop, calls=%fused_computation.18 | loop fusion | flops 24117248 | bytes 2101808 | tf_op jit(solution)/shard_map/convert_element_type | solution.py:106
  65.7 9.0 %all-to-all-done.1 = f32[32,64,128]{2,1,0:T(8,128)S(1)} async-done(((f32[32,64,128]{2,1,0:T(8,128)}), f32[32,64,128]{2,1,0:T(8,128)S(1)}, u32[]{:S(2)}, u32[]{:S(2)}) %all-to-all-start.1) | async-done | bytes 1048608 | tf_op jit(solution)/shard_map/all_to_all | solution.py:330
  74.7 1.7 %copy-done = f32[9,2,256,128]{3,2,1,0:T(8,128)S(1)} copy-done((f32[9,2,256,128]{3,2,1,0:T(8,128)S(1)}, f32[9,2,256,128]{3,2,1,0:T(8,128)}, u32[]{:S(2)}) %copy-start) | copy-done | bytes 2359320
  76.4 1.6 %copy-done.1 = bf16[8,4,128,256]{3,2,1,0:T(8,128)(2,1)S(1)} copy-done((bf16[8,4,128,256]{3,2,1,0:T(8,128)(2,1)S(1)}, bf16[8,4,128,256]{3,2,1,0:T(8,128)(2,1)}, u32[]{:S(2)}) %copy-start.1) | copy-done | bytes 2097176
  78.0 11.8 %subband.2 = f32[2,128,128]{2,1,0:T(8,128)S(1)} custom-call(f32[32,4,16,128]{3,2,1,0:T(8,128)S(1)} %bitcast.121, f32[9,2,256,128]{3,2,1,0:T(8,128)S(1)} %copy-done, bf16[8,4,128,256]{3,2,1,0:T(8,128)(2,1)S(1)} %copy-done.1, f32[2,128,128]{2,1,0:T(8,128)S(1)} %get-tuple-element.16.tw_ref), custom_call_target="tpu_custom_call" | custom-call | flops 10000000000 | bytes 8388608 | tf_op jit(solution)/shard_map/subband/pallas_call | solution.py:339
  89.7 0.1 collective-permute-start
  89.8 3.0 %collective-permute-start.3 = (f32[2,32,128]{2,1,0:T(8,128)S(1)}, f32[2,32,128]{2,1,0:T(8,128)S(1)}, u32[]{:S(2)}, u32[]{:S(2)}) collective-permute-start(f32[2,32,128]{2,1,0:T(8,128)S(1)} %get-tuple-element.49), channel_id=1, source_target_pairs={{0,1},{1,2},{2,3},{3,4},{4,5},{5,6},{6,7},{7,8},{8,9},{9,10},{10,1... | collective-permute-start | bytes 98312 | tf_op jit(solution)/shard_map/ppermute | solution.py:358
  92.9 4.9 %collective-permute-start.4 = (f32[2,32,128]{2,1,0:T(8,128)S(1)}, f32[2,32,128]{2,1,0:T(8,128)S(1)}, u32[]{:S(2)}, u32[]{:S(2)}) collective-permute-start(f32[2,32,128]{2,1,0:T(8,128)S(1)} %get-tuple-element.50), channel_id=1, source_target_pairs={{1,0},{2,1},{3,2},{4,3},{5,4},{6,5},{7,6},{8,7},{9,8},{10,9},{11,1... | collective-permute-start | bytes 98312 | tf_op jit(solution)/shard_map/ppermute | solution.py:361
  97.8 11.8 %subband.3 = f32[2,128,128]{2,1,0:T(8,128)S(1)} custom-call(f32[32,4,16,128]{3,2,1,0:T(8,128)S(1)} %bitcast.122, f32[9,2,256,128]{3,2,1,0:T(8,128)S(1)} %copy-done, bf16[8,4,128,256]{3,2,1,0:T(8,128)(2,1)S(1)} %copy-done.1, f32[2,128,128]{2,1,0:T(8,128)S(1)} %get-tuple-element.18.tw_ref), custom_call_target="tpu_custom_call" | custom-call | flops 10000000000 | bytes 8388608 | tf_op jit(solution)/shard_map/subband/pallas_call | solution.py:339
  109.6 0.1 collective-permute-start.5
  109.8 1.6 %collective-permute-start.1 = (f32[2,128,128]{2,1,0:T(8,128)S(1)}, f32[2,128,128]{2,1,0:T(8,128)S(1)}, u32[]{:S(2)}, u32[]{:S(2)}) collective-permute-start(f32[2,128,128]{2,1,0:T(8,128)S(1)} %pad_maximum_fusion.6), channel_id=1, source_target_pairs={{0,64},{32,96},{64,0},{96,32},{128,192},{160,224},{192,128},{224,1... | collective-permute-start | bytes 393224 | tf_op jit(solution)/shard_map/ppermute | solution.py:367
  111.4 4.3 %collective-permute-done.1 = f32[2,128,128]{2,1,0:T(8,128)S(1)} collective-permute-done((f32[2,128,128]{2,1,0:T(8,128)S(1)}, f32[2,128,128]{2,1,0:T(8,128)S(1)}, u32[]{:S(2)}, u32[]{:S(2)}) %collective-permute-start.1) | collective-permute-done | bytes 131104 | tf_op jit(solution)/shard_map/ppermute | solution.py:367
  115.8 3.1 %collective-permute-start.2 = (f32[2,128,128]{2,1,0:T(8,128)S(1)}, f32[2,128,128]{2,1,0:T(8,128)S(1)}, u32[]{:S(2)}, u32[]{:S(2)}) collective-permute-start(f32[2,128,128]{2,1,0:T(8,128)S(1)} %pad_maximum_fusion.7), channel_id=1, source_target_pairs={{0,128},{32,160},{64,192},{96,224},{128,0},{160,32},{192,64},{224,... | collective-permute-start | bytes 393224 | tf_op jit(solution)/shard_map/ppermute | solution.py:367
  119.0 0.7 collective-permute-start.6
  119.7 3.7 %collective-permute-done.2 = f32[2,128,128]{2,1,0:T(8,128)S(1)} collective-permute-done((f32[2,128,128]{2,1,0:T(8,128)S(1)}, f32[2,128,128]{2,1,0:T(8,128)S(1)}, u32[]{:S(2)}, u32[]{:S(2)}) %collective-permute-start.2) | collective-permute-done | bytes 131104 | tf_op jit(solution)/shard_map/ppermute | solution.py:367
  123.4 3.4 %collective-permute-done.6 = f32[2,192,128]{2,1,0:T(8,128)S(1)} collective-permute-done((f32[2,192,128]{2,1,0:T(8,128)S(1)}, f32[2,192,128]{2,1,0:T(8,128)S(1)}, u32[]{:S(2)}, u32[]{:S(2)}) %collective-permute-start.6) | collective-permute-done | bytes 196640 | tf_op jit(solution)/shard_map/ppermute | solution.py:367
  126.9 2.1 %collective-permute-start.7 = (f32[2,192,128]{2,1,0:T(8,128)S(1)}, f32[2,192,128]{2,1,0:T(8,128)S(1)}, u32[]{:S(2)}, u32[]{:S(2)}) collective-permute-start(f32[2,192,128]{2,1,0:T(8,128)S(1)} %pad_maximum_fusion.2), channel_id=1, source_target_pairs={{0,128},{32,160},{64,192},{96,224},{128,0},{160,32},{192,64},{224,... | collective-permute-start | bytes 589832 | tf_op jit(solution)/shard_map/ppermute | solution.py:367
  129.1 5.1 %collective-permute-done.7 = f32[2,192,128]{2,1,0:T(8,128)S(1)} collective-permute-done((f32[2,192,128]{2,1,0:T(8,128)S(1)}, f32[2,192,128]{2,1,0:T(8,128)S(1)}, u32[]{:S(2)}, u32[]{:S(2)}) %collective-permute-start.7) | collective-permute-done | bytes 196640 | tf_op jit(solution)/shard_map/ppermute | solution.py:367
  134.3 3.1 %templates.1 = f32[128,256]{1,0:T(8,128)} custom-call(f32[2,128,128]{2,1,0:T(8,128)S(1)} %pad_maximum_fusion.8.outer_ref, f32[2,192,128]{2,1,0:T(8,128)S(1)} %pad_maximum_fusion.3.rest_ref, bf16[2048,256]{1,0:T(8,128)(2,1)S(1)} %toeplitz.1.band_ref), custom_call_target="tpu_custom_call" | custom-call | tf_op jit(solution)/shard_map/templates/pallas_call | solution.py:375
  (61 shorter events, 0.8 us)
Async XLA Ops:
  0.0 14.3 %copy-start.2 = (s32[512,64]{0,1:T(8,128)S(1)}, s32[512,64]{0,1:T(8,128)}, u32[]{:S(2)}) copy-start(s32[512,64]{0,1:T(8,128)} %param.12) | copy-start | bytes 393220
  0.0 14.5 %copy-start.8 = (s32[15]{0:T(128)S(1)}, s32[15]{0:T(128)}, u32[]{:S(2)}) copy-start(s32[15]{0:T(128)} %param.13) | copy-start | bytes 184
  0.0 38.8 %all-to-all-start = ((f32[32,16,512]{2,1,0:T(8,128)}), f32[32,16,512]{2,1,0:T(8,128)S(1)}, u32[]{:S(2)}, u32[]{:S(2)}) async-start(f32[32,16,512]{2,1,0:T(8,128)} %bitcast.123), calls=%async_computation | async-start | bytes 2097152 | tf_op jit(solution)/shard_map/all_to_all | solution.py:319
  41.7 12.1 %copy-start.4 = (s32[9]{0:T(128)S(1)}, s32[9]{0:T(128)}, u32[]{:S(2)}) copy-start(s32[9]{0:T(128)} %stack.57) | copy-start | bytes 112
  41.7 12.3 %copy-start.9 = (s32[2]{0:T(128)S(1)}, s32[2]{0:T(128)}, u32[]{:S(2)}) copy-start(s32[2]{0:T(128)} %iota_multiply_fusion.4) | copy-start | bytes 28
  41.7 33.0 %all-to-all-start.1 = ((f32[32,64,128]{2,1,0:T(8,128)}), f32[32,64,128]{2,1,0:T(8,128)S(1)}, u32[]{:S(2)}, u32[]{:S(2)}) async-start(f32[32,64,128]{2,1,0:T(8,128)} %bitcast.2), calls=%async_computation.1 | async-start | bytes 2097152 | tf_op jit(solution)/shard_map/all_to_all | solution.py:330
  53.8 10.0 %copy-start.3 = (s32[256]{0:T(256)S(1)}, s32[256]{0:T(256)}, u32[]{:S(2)}) copy-start(s32[256]{0:T(256)} %get-tuple-element.71) | copy-start | bytes 3076
  53.9 9.9 %copy-start.5 = (s32[8]{0:T(128)S(1)}, s32[8]{0:T(128)}, u32[]{:S(2)}) copy-start(s32[8]{0:T(128)} %iota_multiply_fusion.2) | copy-start | bytes 100
  53.9 9.9 %copy-start.6 = (pred[256]{0:T(512)(128)(4,1)S(1)}, pred[256]{0:T(512)(128)(4,1)}, u32[]{:S(2)}) copy-start(pred[256]{0:T(512)(128)(4,1)} %get-tuple-element.72) | copy-start | bytes 772
  53.9 9.9 %copy-start.7 = (pred[256]{0:T(512)(128)(4,1)S(1)}, pred[256]{0:T(512)(128)(4,1)}, u32[]{:S(2)}) copy-start(pred[256]{0:T(512)(128)(4,1)} %get-tuple-element.73) | copy-start | bytes 772
  74.7 1.7 %copy-start = (f32[9,2,256,128]{3,2,1,0:T(8,128)S(1)}, f32[9,2,256,128]{3,2,1,0:T(8,128)}, u32[]{:S(2)}) copy-start(f32[9,2,256,128]{3,2,1,0:T(8,128)} %fusion.11.tab_ref) | copy-start | bytes 7077892
  76.4 1.6 %copy-start.1 = (bf16[8,4,128,256]{3,2,1,0:T(8,128)(2,1)S(1)}, bf16[8,4,128,256]{3,2,1,0:T(8,128)(2,1)}, u32[]{:S(2)}) copy-start(bf16[8,4,128,256]{3,2,1,0:T(8,128)(2,1)} %fusion.8.spread_ref) | copy-start | bytes 6291460
  89.7 20.0 %collective-permute-start = (f32[2,128,128]{2,1,0:T(8,128)S(1)}, f32[2,128,128]{2,1,0:T(8,128)S(1)}, u32[]{:S(2)}, u32[]{:S(2)}) collective-permute-start(f32[2,128,128]{2,1,0:T(8,128)S(1)} %subband.2), channel_id=1, source_target_pairs={{0,32},{32,0},{64,96},{96,64},{128,160},{160,128},{192,224},{224,1... | collective-permute-start | bytes 393224 | tf_op jit(solution)/shard_map/ppermute | solution.py:367
  89.8 19.7 %collective-permute-start.3 = (f32[2,32,128]{2,1,0:T(8,128)S(1)}, f32[2,32,128]{2,1,0:T(8,128)S(1)}, u32[]{:S(2)}, u32[]{:S(2)}) collective-permute-start(f32[2,32,128]{2,1,0:T(8,128)S(1)} %get-tuple-element.49), channel_id=1, source_target_pairs={{0,1},{1,2},{2,3},{3,4},{4,5},{5,6},{6,7},{7,8},{8,9},{9,10},{10,1... | collective-permute-start | bytes 98312 | tf_op jit(solution)/shard_map/ppermute | solution.py:358
  92.9 16.7 %collective-permute-start.4 = (f32[2,32,128]{2,1,0:T(8,128)S(1)}, f32[2,32,128]{2,1,0:T(8,128)S(1)}, u32[]{:S(2)}, u32[]{:S(2)}) collective-permute-start(f32[2,32,128]{2,1,0:T(8,128)S(1)} %get-tuple-element.50), channel_id=1, source_target_pairs={{1,0},{2,1},{3,2},{4,3},{5,4},{6,5},{7,6},{8,7},{9,8},{10,9},{11,1... | collective-permute-start | bytes 98312 | tf_op jit(solution)/shard_map/ppermute | solution.py:361
  109.6 1.8 %collective-permute-start.5 = (f32[2,192,128]{2,1,0:T(8,128)S(1)}, f32[2,192,128]{2,1,0:T(8,128)S(1)}, u32[]{:S(2)}, u32[]{:S(2)}) collective-permute-start(f32[2,192,128]{2,1,0:T(8,128)S(1)} %pad_maximum_fusion), channel_id=1, source_target_pairs={{0,32},{32,0},{64,96},{96,64},{128,160},{160,128},{192,224},{224,1... | collective-permute-start | bytes 589832 | tf_op jit(solution)/shard_map/ppermute | solution.py:367
  109.8 6.0 %collective-permute-start.1 = (f32[2,128,128]{2,1,0:T(8,128)S(1)}, f32[2,128,128]{2,1,0:T(8,128)S(1)}, u32[]{:S(2)}, u32[]{:S(2)}) collective-permute-start(f32[2,128,128]{2,1,0:T(8,128)S(1)} %pad_maximum_fusion.6), channel_id=1, source_target_pairs={{0,64},{32,96},{64,0},{96,32},{128,192},{160,224},{192,128},{224,1... | collective-permute-start | bytes 393224 | tf_op jit(solution)/shard_map/ppermute | solution.py:367
  115.8 7.6 %collective-permute-start.2 = (f32[2,128,128]{2,1,0:T(8,128)S(1)}, f32[2,128,128]{2,1,0:T(8,128)S(1)}, u32[]{:S(2)}, u32[]{:S(2)}) collective-permute-start(f32[2,128,128]{2,1,0:T(8,128)S(1)} %pad_maximum_fusion.7), channel_id=1, source_target_pairs={{0,128},{32,160},{64,192},{96,224},{128,0},{160,32},{192,64},{224,... | collective-permute-start | bytes 393224 | tf_op jit(solution)/shard_map/ppermute | solution.py:367
  119.0 7.8 %collective-permute-start.6 = (f32[2,192,128]{2,1,0:T(8,128)S(1)}, f32[2,192,128]{2,1,0:T(8,128)S(1)}, u32[]{:S(2)}, u32[]{:S(2)}) collective-permute-start(f32[2,192,128]{2,1,0:T(8,128)S(1)} %pad_maximum_fusion.1), channel_id=1, source_target_pairs={{0,64},{32,96},{64,0},{96,32},{128,192},{160,224},{192,128},{224,1... | collective-permute-start | bytes 589832 | tf_op jit(solution)/shard_map/ppermute | solution.py:367
  126.9 7.3 %collective-permute-start.7 = (f32[2,192,128]{2,1,0:T(8,128)S(1)}, f32[2,192,128]{2,1,0:T(8,128)S(1)}, u32[]{:S(2)}, u32[]{:S(2)}) collective-permute-start(f32[2,192,128]{2,1,0:T(8,128)S(1)} %pad_maximum_fusion.2), channel_id=1, source_target_pairs={{0,128},{32,160},{64,192},{96,224},{128,0},{160,32},{192,64},{224,... | collective-permute-start | bytes 589832 | tf_op jit(solution)/shard_map/ppermute | solution.py:367

commit v5 on v3

--- a/solution.py
+++ b/solution.py
@@ -15,7 +15,6 @@
 FILTER_VMEM = 8 * 2**20
 
 two_pi = 2.0 * math.pi
-top_precision = lax.Precision.HIGHEST
 f32 = jnp.float32
 bf16 = jnp.bfloat16
 
@@ -44,48 +43,67 @@
     return high, (value - high.astype(f32)).astype(bf16)
 
 
-def transform(blocks, length):
-    sources, rows, samp = blocks.shape
+def transform_tables(length):
     inner = length // LANES
-    grid = blocks.transpose(1, 0, 2).reshape(rows, inner, LANES)
     index = lax.iota(jnp.int32, LANES)
-    cos_first, sin_first = turning(index[:, None] * index[None, :], inner)
-    part_re = jnp.einsum("cab,ak->ckb", grid, cos_first, precision=top_precision)
-    part_im = -jnp.einsum("cab,ak->ckb", grid, sin_first, precision=top_precision)
-    cos_twist, sin_twist = turning(index[:, None] * index[None, :], length)
-    part_re, part_im = rotate(part_re, part_im, cos_twist, sin_twist)
-    column = lax.iota(jnp.int32, LANES)
-    kept = column // 4 * 2 + column % 2
-    imag_col = (column // 2 % 2 == 1)[None, :]
-    cos_second, sin_second = turning(index[:, None] * kept[None, :], LANES)
+    sources = LANES // 4
+    block_no = index % sources * 4 + index // sources
+    cos_first, sin_first = turning(index[:, None] * block_no[None, :], inner)
+    first = jnp.concatenate([cos_first, -sin_first], axis=0)
+    twist = turning_pair(index[:, None] * index[None, :], length, 0)
+    kept = index // 4 * 2 + index % 2
+    imag_row = (index // 2 % 2 == 1)[:, None]
+    cos_second, sin_second = turning(kept[:, None] * index[None, :], LANES)
     scale = 1.0 / math.sqrt(length) / 16.0 / 4.0
-    from_re = jnp.where(imag_col, -sin_second, cos_second) * scale
-    from_im = jnp.where(imag_col, cos_second, sin_second) * scale
-    both = jnp.concatenate([part_re, part_im], axis=2)
-    out = jnp.einsum(
-        "ckb,bm->mck", both, jnp.concatenate([from_re, from_im], axis=0), precision=top_precision
-    )
-    return out.reshape(LANES // 4, 4, rows, LANES)
+    from_re = jnp.where(imag_row, -sin_second, cos_second) * scale
+    from_im = jnp.where(imag_row, cos_second, sin_second) * scale
+    return first, twist, jnp.concatenate([from_re, from_im], axis=1)
+
+
+def transform_kernel(blocks_ref, first_ref, twist_ref, second_ref, out_ref, tall):
+    channels = out_ref.shape[0] // LANES
+    held = blocks_ref.shape[0]
+    for r in range(blocks_ref.shape[1] // LANES):
+        tall[r * held : (r + 1) * held, :] = blocks_ref[:, r * LANES : (r + 1) * LANES]
+    first = jnp.concatenate(split_bf16(first_ref[...]), axis=1)
+    second_high, second_low = split_bf16(second_ref[...])
+    second = jnp.concatenate([second_high, second_low], axis=0)
+    across = (((1,), (1,)), ((), ()))
+    for pair in range(channels // 2):
+        mine = (2 * pair, 2 * pair + 1)
+        columns = [tall[pl.ds(c, LANES, stride=channels), :] for c in mine]
+        part = products(first, *windows(jnp.concatenate(columns, axis=1)))
+        rows = []
+        for j in range(2):
+            lanes = slice(j * LANES, (j + 1) * LANES)
+            turned = rotate(part[:LANES, lanes], part[LANES:, lanes], twist_ref[0], twist_ref[1])
+            rows.append(jnp.concatenate(turned, axis=1))
+        high, low = split_bf16(jnp.concatenate(rows, axis=0))
+        got = lax.dot_general(second, high, across, preferred_element_type=f32)
+        got = (
+            got[:LANES]
+            + got[LANES:]
+            + lax.dot_general(second_high, low, across, preferred_element_type=f32)
+        )
+        for j, c in enumerate(mine):
+            out_ref[pl.ds(c, LANES, stride=channels), :] = got[:, j * LANES : (j + 1) * LANES]
 
 
 def delay_turns(channel_delay, first_bin, length):
     per_sub = channel_delay.shape[0] // 2
     both = jnp.concatenate([channel_delay[:per_sub], channel_delay[per_sub:]], axis=1)
-    halves = [2 * first_bin + LANES * q + GROUP - 1 for q in range(4)]
-    halves += [2 * GROUP] + [2 * b + 1 for b in range(GROUP // 2)]
+    halves = [2 * first_bin + GROUP - 1, 2 * GROUP, 1]
     count = both[None] * jnp.stack([jnp.int32(h) for h in halves])[:, None, None]
     return turning_pair(count, 2 * length, 1)
 
 
-def spreading():
-    shape = (LANES // 2 // GROUP, GROUP // 2, LANES, 2 * LANES)
-    i = [lax.broadcasted_iota(jnp.int32, shape, d) for d in range(4)]
-    half = LANES // 2
-    source = i[0] * GROUP + i[1] * 2 + i[3] // LANES + i[3] % LANES // half * half
-    return (i[2] == source).astype(bf16)
-
-
-def sub_kernel(quarters, spec_ref, tab_ref, spread_ref, tw_ref, out_ref, parts, centre, wide):
+def add_angles(a, b):
+    return (a[0] * b[0] - a[1] * b[1], a[1] * b[0] + a[0] * b[1])
+
+
+def sub_kernel(
+    quarters, spec_ref, tab_ref, tw_ref, out_ref, parts, centre, wide, offset, spread
+):
     half = LANES // 2
     per_sub = centre.shape[2]
     sources = spec_ref.shape[0] // 2
@@ -106,16 +124,36 @@
                 high, low = split_bf16(pair)
                 parts[slot, to, 0:LANES] = high
                 parts[slot, to, LANES:] = low
-                centre[slot, x, at, :] = tab_ref[q, x, at, :]
+        first, step, unit = ((tab_ref[i, 0, at, :], tab_ref[i, 1, at, :]) for i in range(3))
+        bin_turn = add_angles(unit, unit)
+        for b in range(GROUP // 2):
+            offset[b, 0, at, :], offset[b, 1, at, :] = unit
+            unit = add_angles(unit, bin_turn)
+        for _ in range(3):
+            step = add_angles(step, step)
+        for q in range(4):
+            if q in quarters:
+                slot = quarters.index(q)
+                centre[slot, 0, at, :], centre[slot, 1, at, :] = first
+            first = add_angles(first, step)
         return carry
 
     lax.fori_loop(0, sources, arrange, 0, unroll=2)
-    steps = spread_ref.shape[0]
+    steps = half // GROUP
+    source = lax.broadcasted_iota(jnp.int32, (LANES, 2 * LANES), 0)
+    target = lax.broadcasted_iota(jnp.int32, (LANES, 2 * LANES), 1)
+    apart = source - target // LANES - target % LANES // half * half
+
+    def one_hots(n, carry):
+        spread[n] = jnp.where(apart == 2 * n, 1.0, 0.0).astype(bf16)
+        return carry
+
+    lax.fori_loop(0, spread.shape[0], one_hots, 0)
 
     def bins(step, carry):
         slot = step // steps
         for n in range(GROUP // 2):
-            one_hot = spread_ref[step % steps, n]
+            one_hot = spread[step % steps * (GROUP // 2) + n]
             one_hot = jnp.concatenate([one_hot, one_hot], axis=0)
             for r in range(2):
                 at = slice(r * per_sub, (r + 1) * per_sub)
@@ -133,8 +171,8 @@
             mid_cos = centre[slot, 0, at, :]
             mid_sin = centre[slot, 1, at, :]
             for b in range(GROUP // 2):
-                off_cos = tab_ref[5 + b, 0, at, :]
-                off_sin = tab_ref[5 + b, 1, at, :]
+                off_cos = offset[b, 0, at, :]
+                off_sin = offset[b, 1, at, :]
                 cc, ss = mid_cos * off_cos, mid_sin * off_sin
                 sc, cs = mid_sin * off_cos, mid_cos * off_sin
                 for j, cosine, sine in (
@@ -146,8 +184,8 @@
                     imag = wide[j // 2, at_im, lanes]
                     re[j] = re[j] + (real * cosine + imag * sine)
                     im[j] = im[j] + (imag * cosine - real * sine)
-            step_cos = tab_ref[4, 0, at, :]
-            step_sin = tab_ref[4, 1, at, :]
+            step_cos = tab_ref[1, 0, at, :]
+            step_sin = tab_ref[1, 1, at, :]
             centre[slot, 0, at, :] = mid_cos * step_cos - mid_sin * step_sin
             centre[slot, 1, at, :] = mid_sin * step_cos + mid_cos * step_sin
             return tuple(re) + tuple(im)
@@ -269,7 +307,6 @@
 
     first_bin = freq_pos * bins_dev
     tabs = delay_turns(channel_delay, first_bin, length)
-    spread = spreading()
     sections = band_count.bit_length()
     shifts = []
     for s in range(sections):
@@ -303,13 +340,22 @@
         name="toeplitz",
     )(profile)
 
+    tables = transform_tables(length)
     blocks = samples.reshape(freq_count, chan_dev // freq_count, samp_dev)
     blocks = lax.all_to_all(blocks, "freq", split_axis=0, concat_axis=0, tiled=True)
-    spec = transform(blocks, length)
+    spec = pl.pallas_call(
+        transform_kernel,
+        out_shape=jax.ShapeDtypeStruct((chan_dev // freq_count * LANES, LANES), f32),
+        in_specs=[vmem] * 4,
+        out_specs=vmem,
+        scratch_shapes=[pltpu.VMEM((chan_dev // freq_count * LANES, LANES), f32)],
+        compiler_params=pltpu.CompilerParams(vmem_limit_bytes=FILTER_VMEM),
+        name="transform",
+    )(blocks.reshape(chan_dev, samp_dev), *tables)
+    spec = spec.reshape(freq_count, chan_dev * 4 // freq_count, LANES)
     spec = lax.all_to_all(spec, "freq", split_axis=0, concat_axis=0, tiled=True)
-    spec, turns, tabs, spread, band = lax.optimization_barrier(
-        (spec, turns, tabs, spread, band)
-    )
+    spec = spec.reshape(freq_count, 4, chan_dev // freq_count, LANES)
+    spec, turns, tabs, band = lax.optimization_barrier((spec, turns, tabs, band))
 
     current = []
     for pair, turn in zip(chunks, turns):
@@ -317,19 +363,21 @@
             pl.pallas_call(
                 functools.partial(sub_kernel, pair),
                 out_shape=jax.ShapeDtypeStruct((2, bins_dev // 2, block), f32),
-                in_specs=[vmem] * 4,
+                in_specs=[vmem] * 3,
                 out_specs=vmem,
                 scratch_shapes=[
                     pltpu.VMEM((2, chan_dev, 2 * LANES), bf16),
                     pltpu.VMEM((2, 2, chan_dev // 2, LANES), f32),
                     pltpu.VMEM((GROUP // 2, chan_dev, 2 * LANES), f32),
+                    pltpu.VMEM((GROUP // 2, 2, chan_dev // 2, LANES), f32),
+                    pltpu.VMEM((LANES // 4, LANES, 2 * LANES), bf16),
                 ],
                 cost_estimate=pl.CostEstimate(
                     flops=10**10, bytes_accessed=2**23, transcendentals=0
                 ),
                 compiler_params=pltpu.CompilerParams(vmem_limit_bytes=SUB_VMEM),
                 name="subband",
-            )(spec, tabs, spread, turn[0])
+            )(spec, tabs, turn[0])
         )
 
     for s in range(1, sections):

time: 142 us -> 131 us (0.923)
  waiting for transfers between devices: 37 us -> 49.4 us
  other arithmetic: 24.8 us -> 13.2 us
  local copies, waits for them, and re-layouts: 12 us -> 3.37 us
  matrix products: 3.72 us -> 0 us
    all_to_all x1, waiting for transfers between devices: 14.1 us -> 20.6 us  [per_device(): lax.all_to_all(blocks, 'freq', split_axis=0, concat_axis=0, tiled=True)]
    all_to_all x1, waiting for transfers between devices: 10.3 us -> 16.3 us  [per_device(): spec = lax.all_to_all(spec, 'freq', split_axis=0, concat_axis=0, tiled=True)]
    cos x3 -> x4, other arithmetic: 14 us -> 8.38 us  [turning(): return (jnp.cos(angle), jnp.sin(angle))]
    pallas_call x0 -> x1, Pallas kernels: none -> 2.97 us  [per_device(): pl.pallas_call(transform_kernel, out_shape=jax.ShapeDtypeStruct((chan_dev...]
    reshape x2 -> x0, local copies, waits for them, and re-layouts: 2.62 us -> none  [transform(): grid = blocks.transpose(1, 0, 2).reshape(rows, inner, LANES)]
    unnamed x2 -> x0, matrix products: 2.48 us -> none
    unnamed x35 -> x15, local copies, waits for them, and re-layouts: 3.81 us -> 1.8 us
    pallas_call x2, Pallas kernels: 26.2 us -> 24.3 us  [per_device(): pl.pallas_call(functools.partial(sub_kernel, pair), out_shape=jax.ShapeDt...]
  transfers between devices with their start and end apart: 10 -> 10, of which waited for: 5 -> 5; matrix products, arithmetic and copies ran while one was open for 20% -> 11% of each run, Pallas kernels for 10% -> 10%
where the time goes in v5:
time: 131 us
  waiting for transfers between devices  49.4 us (38%)
  starting transfers between devices  33.1 us (25%)
  Pallas kernels  31.4 us (24%)
  other arithmetic  13.2 us (10%)
  local copies, waits for them, and re-layouts  3.37 us (3%)
    pallas_call x2, Pallas kernels, per_device(): pl.pallas_call(functools.partial(sub_kernel, pair), out_shape=jax.ShapeDt...  24.3 us
    all_to_all x1, waiting for transfers between devices, per_device(): lax.all_to_all(blocks, 'freq', split_axis=0, concat_axis=0, tiled=True)  20.6 us
    all_to_all x1, waiting for transfers between devices, per_device(): spec = lax.all_to_all(spec, 'freq', split_axis=0, concat_axis=0, tiled=True)  16.3 us
    all_to_all x1, starting transfers between devices, per_device(): lax.all_to_all(blocks, 'freq', split_axis=0, concat_axis=0, tiled=True)  11.4 us
    ppermute x6, starting transfers between devices, per_device(): lax.ppermute(mine, 'band', [(j, j ^ half) for j in range(band_count)])  8.39 us
    cos x4, other arithmetic, turning(): return (jnp.cos(angle), jnp.sin(angle))  8.38 us
    ppermute x6, waiting for transfers between devices, per_device(): lax.ppermute(mine, 'band', [(j, j ^ half) for j in range(band_count)])  6.62 us
    all_to_all x1, starting transfers between devices, per_device(): spec = lax.all_to_all(spec, 'freq', split_axis=0, concat_axis=0, tiled=True)  6.37 us
  transfers between devices with their start and end apart: 10, of which 5 were waited for; matrix products, arithmetic and copies ran while one was open for 11% of the time, Pallas kernels for 10%

profile of v5, /device:TPU:32, one launch (start us, length us, event | category | flops | bytes accessed | tf_op | source)
XLA Modules:
  0.0 130.9 jit_solution(4324801207535681032)
XLA Ops:
  0.0 11.4 %all-to-all-start = ((f32[32,16,512]{2,1,0:T(8,128)}), f32[32,16,512]{2,1,0:T(8,128)S(1)}, u32[]{:S(2)}, u32[]{:S(2)}) async-start(f32[32,16,512]{2,1,0:T(8,128)} %bitcast.120), calls=%async_computation | async-start | bytes 2097152 | tf_op jit(solution)/shard_map/all_to_all | solution.py:345
  11.5 0.1 pad_add_fusion.2
  11.6 0.7 copy-done.6
  12.2 0.7 fusion.59
  13.0 1.4 %and_select_fusion.4 = (s32[1,128]{1,0:T(1,128)S(1)}, s32[1,128]{1,0:T(1,128)S(1)}) fusion(s32[]{:T(128)} %get-tuple-element.20, s32[]{:T(128)S(6)} %mul.354, s32[]{:T(128)} %get-tuple-element.19), kind=kLoop, calls=%fused_computation.179 | loop fusion | flops 7040 | bytes 1036 | tf_op jit(solution)/shard_map/jit(remainder)/select_n | solution.py:316
  14.3 0.1 pad_add_fusion.3
  14.4 1.3 and_select_fusion
  15.7 0.3 select_multiply_fusion.1
  16.1 0.3 fusion.52
  16.4 0.1 broadcast_multiply_fusion.1
  16.5 1.5 %fusion.20 = (f32[2,128,128]{2,1,0:T(8,128)S(1)}, f32[2,128,128]{2,1,0:T(8,128)S(1)}, f32[2,128,128]{2,1,0:T(8,128)S(1)}) fusion(s32[128,128]{1,0:T(8,128)S(1)} %slice_bitcast_fusion, s32[2]{0:T(128)S(1)} %iota_multiply_fusion.1, s32[128,128]{1,0:T(8,128)S(1)} %slice_bitcast_fusion.1, s32[128,128]{1,0:T(8,128)S(1)} %iota_multiply_fusion), kind=kLoop, calls=%fused_computation.58 | loop fusion | flops 1376256 | bytes 589832 | tf_op jit(solution)/shard_map/cos | solution.py:24
  18.0 20.6 %all-to-all-done = f32[32,16,512]{2,1,0:T(8,128)S(1)} async-done(((f32[32,16,512]{2,1,0:T(8,128)}), f32[32,16,512]{2,1,0:T(8,128)S(1)}, u32[]{:S(2)}, u32[]{:S(2)}) %all-to-all-start) | async-done | bytes 1048608 | tf_op jit(solution)/shard_map/all_to_all | solution.py:345
  38.6 3.0 %transform.1 = f32[2048,128]{1,0:T(8,128)} custom-call(f32[512,512]{1,0:T(8,128)S(1)} %bitcast.117, f32[256,128]{1,0:T(8,128)S(1)} %pad_maximum_fusion.1.first_ref, f32[2,128,128]{2,1,0:T(8,128)S(1)} %get-tuple-element.59.twist_ref, f32[128,256]{1,0:T(8,128)S(1)} %pad_maximum_fusion.2.second_ref), custom_call_target="tpu_custom_call" | custom-call | tf_op jit(solution)/shard_map/transform/pallas_call | solution.py:346
  41.6 6.4 %all-to-all-start.1 = ((f32[32,64,128]{2,1,0:T(8,128)}), f32[32,64,128]{2,1,0:T(8,128)S(1)}, u32[]{:S(2)}, u32[]{:S(2)}) async-start(f32[32,64,128]{2,1,0:T(8,128)} %bitcast.2), calls=%async_computation.1 | async-start | bytes 2097152 | tf_op jit(solution)/shard_map/all_to_all | solution.py:356
  48.0 0.7 slice.209
  48.7 0.7 slice.207
  49.4 0.1 copy.16
  49.5 0.6 copy-done.4
  50.1 0.1 copy.17
  50.2 0.1 copy.15
  50.3 0.2 select_reduce_fusion.profile_ref
  50.5 0.8 toeplitz.1.band_ref
  51.4 0.1 pad_add_fusion.4
  51.4 0.1 broadcast_multiply_fusion
  51.6 2.9 %fusion.2.tab_ref = f32[3,2,256,128]{3,2,1,0:T(8,128)S(1)} fusion(s32[2]{0:T(128)S(1)} %iota_multiply_fusion.2, s32[3,256,128]{2,1,0:T(8,128)S(1)} %broadcast_multiply_fusion), kind=kLoop, calls=%fused_computation.7 | loop fusion | flops 2752512 | bytes 1179656 | tf_op jit(solution)/shard_map/cos | solution.py:24
  54.5 3.7 %fusion.9 = (f32[3,2,128,128]{3,2,1,0:T(8,128)S(1)}, f32[3,2,128,128]{3,2,1,0:T(8,128)}) fusion(s32[3,128,128]{2,1,0:T(8,128)S(1)} %copy-done.1, s32[2]{0:T(128)S(1)} %iota_multiply_fusion.1, s32[3,128,128]{2,1,0:T(8,128)S(1)} %copy-done.2), kind=kLoop, calls=%fused_computation.24 | loop fusion | flops 2752512 | bytes 1179656 | tf_op jit(solution)/shard_map/cos | solution.py:24
  58.2 16.3 %all-to-all-done.1 = f32[32,64,128]{2,1,0:T(8,128)S(1)} async-done(((f32[32,64,128]{2,1,0:T(8,128)}), f32[32,64,128]{2,1,0:T(8,128)S(1)}, u32[]{:S(2)}, u32[]{:S(2)}) %all-to-all-start.1) | async-done | bytes 1048608 | tf_op jit(solution)/shard_map/all_to_all | solution.py:356
  74.5 12.2 %subband.2 = f32[2,128,128]{2,1,0:T(8,128)S(1)} custom-call(f32[32,4,16,128]{3,2,1,0:T(8,128)S(1)} %bitcast.118, f32[3,2,256,128]{3,2,1,0:T(8,128)S(1)} %fusion.2.tab_ref, f32[2,128,128]{2,1,0:T(8,128)S(1)} %get-tuple-element.14.tw_ref), custom_call_target="tpu_custom_call" | custom-call | flops 10000000000 | bytes 8388608 | tf_op jit(solution)/shard_map/subband/pallas_call | solution.py:363
  86.6 0.2 collective-permute-start
  86.8 12.2 %subband.3 = f32[2,128,128]{2,1,0:T(8,128)S(1)} custom-call(f32[32,4,16,128]{3,2,1,0:T(8,128)S(1)} %bitcast.119, f32[3,2,256,128]{3,2,1,0:T(8,128)S(1)} %fusion.2.tab_ref, f32[2,128,128]{2,1,0:T(8,128)S(1)} %get-tuple-element.16.tw_ref), custom_call_target="tpu_custom_call" | custom-call | flops 10000000000 | bytes 8388608 | tf_op jit(solution)/shard_map/subband/pallas_call | solution.py:363
  99.0 0.5 collective-permute-start.3
  99.5 0.0 collective-permute-done
  99.5 0.4 copy-done
  100.0 1.6 %collective-permute-start.1 = (f32[2,128,128]{2,1,0:T(8,128)S(1)}, f32[2,128,128]{2,1,0:T(8,128)S(1)}, u32[]{:S(2)}, u32[]{:S(2)}) collective-permute-start(f32[2,128,128]{2,1,0:T(8,128)S(1)} %pad_maximum_fusion.3), channel_id=1, source_target_pairs={{0,64},{32,96},{64,0},{96,32},{128,192},{160,224},{192,128},{224,1... | collective-permute-start | bytes 393224 | tf_op jit(solution)/shard_map/ppermute | solution.py:387
  101.6 0.0 collective-permute-done.3
  101.7 0.6 collective-permute-start.4
  102.3 4.1 %collective-permute-done.1 = f32[2,128,128]{2,1,0:T(8,128)S(1)} collective-permute-done((f32[2,128,128]{2,1,0:T(8,128)S(1)}, f32[2,128,128]{2,1,0:T(8,128)S(1)}, u32[]{:S(2)}, u32[]{:S(2)}) %collective-permute-start.1) | collective-permute-done | bytes 131104 | tf_op jit(solution)/shard_map/ppermute | solution.py:387
  106.5 3.1 %collective-permute-start.2 = (f32[2,128,128]{2,1,0:T(8,128)S(1)}, f32[2,128,128]{2,1,0:T(8,128)S(1)}, u32[]{:S(2)}, u32[]{:S(2)}) collective-permute-start(f32[2,128,128]{2,1,0:T(8,128)S(1)} %pad_maximum_fusion.4), channel_id=1, source_target_pairs={{0,128},{32,160},{64,192},{96,224},{128,0},{160,32},{192,64},{224,... | collective-permute-start | bytes 393224 | tf_op jit(solution)/shard_map/ppermute | solution.py:387
  109.6 0.0 collective-permute-done.4
  109.7 2.3 %collective-permute-start.5 = (f32[2,128,128]{2,1,0:T(8,128)S(1)}, f32[2,128,128]{2,1,0:T(8,128)S(1)}, u32[]{:S(2)}, u32[]{:S(2)}) collective-permute-start(f32[2,128,128]{2,1,0:T(8,128)S(1)} %pad_maximum_fusion.6), channel_id=1, source_target_pairs={{0,128},{32,160},{64,192},{96,224},{128,0},{160,32},{192,64},{224,... | collective-permute-start | bytes 393224 | tf_op jit(solution)/shard_map/ppermute | solution.py:387
  112.0 2.5 %collective-permute-done.2 = f32[2,128,128]{2,1,0:T(8,128)S(1)} collective-permute-done((f32[2,128,128]{2,1,0:T(8,128)S(1)}, f32[2,128,128]{2,1,0:T(8,128)S(1)}, u32[]{:S(2)}, u32[]{:S(2)}) %collective-permute-start.2) | collective-permute-done | bytes 131104 | tf_op jit(solution)/shard_map/ppermute | solution.py:387
  114.6 5.1 %collective-permute-start.7 = (f32[2,32,128]{2,1,0:T(8,128)S(1)}, f32[2,32,128]{2,1,0:T(8,128)S(1)}, u32[]{:S(2)}, u32[]{:S(2)}) collective-permute-start(f32[2,32,128]{2,1,0:T(8,128)S(1)} %get-tuple-element.47), channel_id=1, source_target_pairs={{1,0},{2,1},{3,2},{4,3},{5,4},{6,5},{7,6},{8,7},{9,8},{10,9},{11,1... | collective-permute-start | bytes 98312 | tf_op jit(solution)/shard_map/ppermute | solution.py:400
  119.7 1.9 %collective-permute-start.6 = (f32[2,32,128]{2,1,0:T(8,128)S(1)}, f32[2,32,128]{2,1,0:T(8,128)S(1)}, u32[]{:S(2)}, u32[]{:S(2)}) collective-permute-start(f32[2,32,128]{2,1,0:T(8,128)S(1)} %get-tuple-element.48), channel_id=1, source_target_pairs={{0,1},{1,2},{2,3},{3,4},{4,5},{5,6},{6,7},{7,8},{8,9},{9,10},{10,1... | collective-permute-start | bytes 98312 | tf_op jit(solution)/shard_map/ppermute | solution.py:397
  121.6 0.0 collective-permute-done.5
  121.7 0.0 collective-permute-done.7.right_ref
  121.7 5.9 %collective-permute-done.6.left_ref = f32[2,32,128]{2,1,0:T(8,128)S(1)} collective-permute-done((f32[2,32,128]{2,1,0:T(8,128)S(1)}, f32[2,32,128]{2,1,0:T(8,128)S(1)}, u32[]{:S(2)}, u32[]{:S(2)}) %collective-permute-start.6) | collective-permute-done | bytes 32800 | tf_op jit(solution)/shard_map/ppermute | solution.py:397
  127.6 0.7 edge_bins.1.edge_ref
  128.3 2.5 %inner_bins.1 = f32[128,256]{1,0:T(8,128)} custom-call(f32[2,128,128]{2,1,0:T(8,128)S(1)} %pad_maximum_fusion.outer_ref, f32[2,128,128]{2,1,0:T(8,128)S(1)} %pad_maximum_fusion.7.mid_ref, f32[2,32,128]{2,1,0:T(8,128)S(1)} %edge_bins.1.edge_ref, bf16[2048,256]{1,0:T(8,128)(2,1)S(1)} %toeplitz.1.band_ref), custom_call_target="tpu_custom_call" | custom-call | tf_op jit(solution)/shard_map/inner_bins/pallas_call | solution.py:409
  (46 shorter events, 0.5 us)
Async XLA Ops:
  0.0 38.6 %all-to-all-start = ((f32[32,16,512]{2,1,0:T(8,128)}), f32[32,16,512]{2,1,0:T(8,128)S(1)}, u32[]{:S(2)}, u32[]{:S(2)}) async-start(f32[32,16,512]{2,1,0:T(8,128)} %bitcast.120), calls=%async_computation | async-start | bytes 2097152 | tf_op jit(solution)/shard_map/all_to_all | solution.py:345
  11.6 0.7 copy-start.6
  41.6 32.8 %all-to-all-start.1 = ((f32[32,64,128]{2,1,0:T(8,128)}), f32[32,64,128]{2,1,0:T(8,128)S(1)}, u32[]{:S(2)}, u32[]{:S(2)}) async-start(f32[32,64,128]{2,1,0:T(8,128)} %bitcast.2), calls=%async_computation.1 | async-start | bytes 2097152 | tf_op jit(solution)/shard_map/all_to_all | solution.py:356
  48.7 0.7 copy-start.5
  48.7 1.5 %copy-start.3 = (s32[512,64]{0,1:T(8,128)S(1)}, s32[512,64]{0,1:T(8,128)}, u32[]{:S(2)}) copy-start(s32[512,64]{0,1:T(8,128)} %param.12) | copy-start | bytes 393220
  49.4 0.7 copy-start.4
  51.5 2.9 %copy-start.1 = (s32[3,128,128]{2,1,0:T(8,128)S(1)}, s32[3,128,128]{2,1,0:T(8,128)}, u32[]{:S(2)}) copy-start(s32[3,128,128]{2,1,0:T(8,128)} %slice.209) | copy-start | bytes 589828
  51.6 2.9 %copy-start.2 = (s32[3,128,128]{2,1,0:T(8,128)S(1)}, s32[3,128,128]{2,1,0:T(8,128)}, u32[]{:S(2)}) copy-start(s32[3,128,128]{2,1,0:T(8,128)} %slice.207) | copy-start | bytes 589828
  86.6 12.9 %collective-permute-start = (f32[2,128,128]{2,1,0:T(8,128)S(1)}, f32[2,128,128]{2,1,0:T(8,128)S(1)}, u32[]{:S(2)}, u32[]{:S(2)}) collective-permute-start(f32[2,128,128]{2,1,0:T(8,128)S(1)} %subband.2), channel_id=1, source_target_pairs={{0,32},{32,0},{64,96},{96,64},{128,160},{160,128},{192,224},{224,1... | collective-permute-start | bytes 393224 | tf_op jit(solution)/shard_map/ppermute | solution.py:387
  99.0 1.0 copy-start
  99.0 2.6 %collective-permute-start.3 = (f32[2,128,128]{2,1,0:T(8,128)S(1)}, f32[2,128,128]{2,1,0:T(8,128)S(1)}, u32[]{:S(2)}, u32[]{:S(2)}) collective-permute-start(f32[2,128,128]{2,1,0:T(8,128)S(1)} %subband.3), channel_id=1, source_target_pairs={{0,32},{32,0},{64,96},{96,64},{128,160},{160,128},{192,224},{224,1... | collective-permute-start | bytes 393224 | tf_op jit(solution)/shard_map/ppermute | solution.py:387
  100.0 6.4 %collective-permute-start.1 = (f32[2,128,128]{2,1,0:T(8,128)S(1)}, f32[2,128,128]{2,1,0:T(8,128)S(1)}, u32[]{:S(2)}, u32[]{:S(2)}) collective-permute-start(f32[2,128,128]{2,1,0:T(8,128)S(1)} %pad_maximum_fusion.3), channel_id=1, source_target_pairs={{0,64},{32,96},{64,0},{96,32},{128,192},{160,224},{192,128},{224,1... | collective-permute-start | bytes 393224 | tf_op jit(solution)/shard_map/ppermute | solution.py:387
  101.7 7.9 %collective-permute-start.4 = (f32[2,128,128]{2,1,0:T(8,128)S(1)}, f32[2,128,128]{2,1,0:T(8,128)S(1)}, u32[]{:S(2)}, u32[]{:S(2)}) collective-permute-start(f32[2,128,128]{2,1,0:T(8,128)S(1)} %pad_maximum_fusion.5), channel_id=1, source_target_pairs={{0,64},{32,96},{64,0},{96,32},{128,192},{160,224},{192,128},{224,1... | collective-permute-start | bytes 393224 | tf_op jit(solution)/shard_map/ppermute | solution.py:387
  106.5 8.0 %collective-permute-start.2 = (f32[2,128,128]{2,1,0:T(8,128)S(1)}, f32[2,128,128]{2,1,0:T(8,128)S(1)}, u32[]{:S(2)}, u32[]{:S(2)}) collective-permute-start(f32[2,128,128]{2,1,0:T(8,128)S(1)} %pad_maximum_fusion.4), channel_id=1, source_target_pairs={{0,128},{32,160},{64,192},{96,224},{128,0},{160,32},{192,64},{224,... | collective-permute-start | bytes 393224 | tf_op jit(solution)/shard_map/ppermute | solution.py:387
  109.7 12.0 %collective-permute-start.5 = (f32[2,128,128]{2,1,0:T(8,128)S(1)}, f32[2,128,128]{2,1,0:T(8,128)S(1)}, u32[]{:S(2)}, u32[]{:S(2)}) collective-permute-start(f32[2,128,128]{2,1,0:T(8,128)S(1)} %pad_maximum_fusion.6), channel_id=1, source_target_pairs={{0,128},{32,160},{64,192},{96,224},{128,0},{160,32},{192,64},{224,... | collective-permute-start | bytes 393224 | tf_op jit(solution)/shard_map/ppermute | solution.py:387
  114.6 7.2 %collective-permute-start.7 = (f32[2,32,128]{2,1,0:T(8,128)S(1)}, f32[2,32,128]{2,1,0:T(8,128)S(1)}, u32[]{:S(2)}, u32[]{:S(2)}) collective-permute-start(f32[2,32,128]{2,1,0:T(8,128)S(1)} %get-tuple-element.47), channel_id=1, source_target_pairs={{1,0},{2,1},{3,2},{4,3},{5,4},{6,5},{7,6},{8,7},{9,8},{10,9},{11,1... | collective-permute-start | bytes 98312 | tf_op jit(solution)/shard_map/ppermute | solution.py:400
  119.7 7.9 %collective-permute-start.6 = (f32[2,32,128]{2,1,0:T(8,128)S(1)}, f32[2,32,128]{2,1,0:T(8,128)S(1)}, u32[]{:S(2)}, u32[]{:S(2)}) collective-permute-start(f32[2,32,128]{2,1,0:T(8,128)S(1)} %get-tuple-element.48), channel_id=1, source_target_pairs={{0,1},{1,2},{2,3},{3,4},{4,5},{5,6},{6,7},{7,8},{8,9},{9,10},{10,1... | collective-permute-start | bytes 98312 | tf_op jit(solution)/shard_map/ppermute | solution.py:397

commit v6 on v5

--- a/solution.py
+++ b/solution.py
@@ -11,7 +11,7 @@
 REACH = 32
 LANES = 128
 GROUP = 8
-SUB_VMEM = 12 * 2**20
+SUB_VMEM = 14 * 2**20
 FILTER_VMEM = 8 * 2**20
 
 two_pi = 2.0 * math.pi
@@ -139,7 +139,7 @@
         return carry
 
     lax.fori_loop(0, sources, arrange, 0, unroll=2)
-    steps = half // GROUP
+    passes = half // (2 * GROUP)
     source = lax.broadcasted_iota(jnp.int32, (LANES, 2 * LANES), 0)
     target = lax.broadcasted_iota(jnp.int32, (LANES, 2 * LANES), 1)
     apart = source - target // LANES - target % LANES // half * half
@@ -151,9 +151,9 @@
     lax.fori_loop(0, spread.shape[0], one_hots, 0)
 
     def bins(step, carry):
-        slot = step // steps
-        for n in range(GROUP // 2):
-            one_hot = spread[step % steps * (GROUP // 2) + n]
+        slot = step // passes
+        for n in range(GROUP):
+            one_hot = spread[step % passes * GROUP + n]
             one_hot = jnp.concatenate([one_hot, one_hot], axis=0)
             for r in range(2):
                 at = slice(r * per_sub, (r + 1) * per_sub)
@@ -164,38 +164,40 @@
                 )
 
         def channels(g, sums):
-            re = list(sums[:GROUP])
-            im = list(sums[GROUP:])
+            re = list(sums[: 2 * GROUP])
+            im = list(sums[2 * GROUP :])
             at = pl.ds(pl.multiple_of(8 * g, 8), 8)
             at_im = pl.ds(pl.multiple_of(per_sub + 8 * g, 8), 8)
-            mid_cos = centre[slot, 0, at, :]
-            mid_sin = centre[slot, 1, at, :]
+            advance = (tab_ref[1, 0, at, :], tab_ref[1, 1, at, :])
+            mids = [(centre[slot, 0, at, :], centre[slot, 1, at, :])]
+            mids.append(add_angles(mids[0], advance))
             for b in range(GROUP // 2):
                 off_cos = offset[b, 0, at, :]
                 off_sin = offset[b, 1, at, :]
-                cc, ss = mid_cos * off_cos, mid_sin * off_sin
-                sc, cs = mid_sin * off_cos, mid_cos * off_sin
-                for j, cosine, sine in (
-                    (GROUP // 2 + b, cc - ss, sc + cs),
-                    (GROUP // 2 - 1 - b, cc + ss, sc - cs),
-                ):
-                    lanes = slice(j % 2 * LANES, j % 2 * LANES + LANES)
-                    real = wide[j // 2, at, lanes]
-                    imag = wide[j // 2, at_im, lanes]
-                    re[j] = re[j] + (real * cosine + imag * sine)
-                    im[j] = im[j] + (imag * cosine - real * sine)
-            step_cos = tab_ref[1, 0, at, :]
-            step_sin = tab_ref[1, 1, at, :]
-            centre[slot, 0, at, :] = mid_cos * step_cos - mid_sin * step_sin
-            centre[slot, 1, at, :] = mid_sin * step_cos + mid_cos * step_sin
+                for h, (mid_cos, mid_sin) in enumerate(mids):
+                    cc, ss = mid_cos * off_cos, mid_sin * off_sin
+                    sc, cs = mid_sin * off_cos, mid_cos * off_sin
+                    for j, cosine, sine in (
+                        (h * GROUP + GROUP // 2 + b, cc - ss, sc + cs),
+                        (h * GROUP + GROUP // 2 - 1 - b, cc + ss, sc - cs),
+                    ):
+                        lanes = slice(j % 2 * LANES, j % 2 * LANES + LANES)
+                        real = wide[j // 2, at, lanes]
+                        imag = wide[j // 2, at_im, lanes]
+                        re[j] = re[j] + (real * cosine + imag * sine)
+                        im[j] = im[j] + (imag * cosine - real * sine)
+            centre[slot, 0, at, :], centre[slot, 1, at, :] = add_angles(mids[1], advance)
             return tuple(re) + tuple(im)
 
         zero = jnp.zeros((8, LANES), f32)
-        sums = lax.fori_loop(0, per_sub // 8, channels, (zero,) * (2 * GROUP), unroll=per_sub // 8)
-        at = pl.ds(pl.multiple_of(step * GROUP, GROUP), GROUP)
+        sums = lax.fori_loop(0, per_sub // 8, channels, (zero,) * (4 * GROUP), unroll=per_sub // 8)
+        at = pl.ds(pl.multiple_of(step * 2 * GROUP, 2 * GROUP), 2 * GROUP)
         re, im = (
             jnp.concatenate(
-                [jnp.sum(v, axis=0, keepdims=True) for v in sums[x * GROUP : (x + 1) * GROUP]],
+                [
+                    jnp.sum(v, axis=0, keepdims=True)
+                    for v in sums[x * 2 * GROUP : (x + 1) * 2 * GROUP]
+                ],
                 axis=0,
             )
             for x in range(2)
@@ -213,7 +215,7 @@
         out_ref[1, at, :] = jnp.where(lower, im, im_turn) + up_im
         return carry
 
-    lax.fori_loop(0, out_ref.shape[1] // GROUP, bins, 0)
+    lax.fori_loop(0, out_ref.shape[1] // (2 * GROUP), bins, 0)
 
 
 def toeplitz_kernel(profile_ref, band_ref):
@@ -368,7 +370,7 @@
                 scratch_shapes=[
                     pltpu.VMEM((2, chan_dev, 2 * LANES), bf16),
                     pltpu.VMEM((2, 2, chan_dev // 2, LANES), f32),
-                    pltpu.VMEM((GROUP // 2, chan_dev, 2 * LANES), f32),
+                    pltpu.VMEM((GROUP, chan_dev, 2 * LANES), f32),
                     pltpu.VMEM((GROUP // 2, 2, chan_dev // 2, LANES), f32),
                     pltpu.VMEM((LANES // 4, LANES, 2 * LANES), bf16),
                 ],

time: 131 us -> 129 us (0.985)
  Pallas kernels: 31.4 us -> 28.7 us
    pallas_call x2, Pallas kernels: 24.3 us -> 21.6 us  [per_device(): pl.pallas_call(functools.partial(sub_kernel, pair), out_shape=jax.ShapeDt...]
  transfers between devices with their start and end apart: 10 -> 10, of which waited for: 5 -> 5; matrix products, arithmetic and copies ran while one was open for 11% -> 12% of each run, Pallas kernels for 10% -> 9%
where the time goes in v6:
time: 129 us; the launch traced here: 128 us
  waiting for transfers between devices  49.4 us (38%)
  starting transfers between devices  33.1 us (26%)
  Pallas kernels  28.7 us (22%)
  other arithmetic  13.2 us (10%)
  local copies, waits for them, and re-layouts  3.37 us (3%)
    pallas_call x2, Pallas kernels, per_device(): pl.pallas_call(functools.partial(sub_kernel, pair), out_shape=jax.ShapeDt...  21.6 us
    all_to_all x1, waiting for transfers between devices, per_device(): lax.all_to_all(blocks, 'freq', split_axis=0, concat_axis=0, tiled=True)  20.6 us
    all_to_all x1, waiting for transfers between devices, per_device(): spec = lax.all_to_all(spec, 'freq', split_axis=0, concat_axis=0, tiled=True)  16.3 us
    all_to_all x1, starting transfers between devices, per_device(): lax.all_to_all(blocks, 'freq', split_axis=0, concat_axis=0, tiled=True)  11.4 us
    ppermute x6, starting transfers between devices, per_device(): lax.ppermute(mine, 'band', [(j, j ^ half) for j in range(band_count)])  8.39 us
    cos x4, other arithmetic, turning(): return (jnp.cos(angle), jnp.sin(angle))  8.38 us
    ppermute x6, waiting for transfers between devices, per_device(): lax.ppermute(mine, 'band', [(j, j ^ half) for j in range(band_count)])  6.61 us
    all_to_all x1, starting transfers between devices, per_device(): spec = lax.all_to_all(spec, 'freq', split_axis=0, concat_axis=0, tiled=True)  6.37 us
  transfers between devices with their start and end apart: 10, of which 5 were waited for; matrix products, arithmetic and copies ran while one was open for 12% of the time, Pallas kernels for 9%

profile of v6, /device:TPU:32, one launch (start us, length us, event | category | flops | bytes accessed | tf_op | source)
XLA Modules:
  0.0 128.2 jit_solution(16002798025006888219)
XLA Ops:
  0.0 11.4 %all-to-all-start = ((f32[32,16,512]{2,1,0:T(8,128)}), f32[32,16,512]{2,1,0:T(8,128)S(1)}, u32[]{:S(2)}, u32[]{:S(2)}) async-start(f32[32,16,512]{2,1,0:T(8,128)} %bitcast.120), calls=%async_computation | async-start | bytes 2097152 | tf_op jit(solution)/shard_map/all_to_all | solution.py:347
  11.5 0.1 pad_add_fusion.2
  11.6 0.7 copy-done.6
  12.2 0.7 fusion.59
  13.0 1.4 %and_select_fusion.4 = (s32[1,128]{1,0:T(1,128)S(1)}, s32[1,128]{1,0:T(1,128)S(1)}) fusion(s32[]{:T(128)} %get-tuple-element.20, s32[]{:T(128)S(6)} %mul.354, s32[]{:T(128)} %get-tuple-element.19), kind=kLoop, calls=%fused_computation.179 | loop fusion | flops 7040 | bytes 1036 | tf_op jit(solution)/shard_map/jit(remainder)/select_n | solution.py:318
  14.3 0.1 pad_add_fusion.3
  14.4 1.3 and_select_fusion
  15.7 0.3 select_multiply_fusion.1
  16.1 0.3 fusion.52
  16.4 0.1 broadcast_multiply_fusion.1
  16.5 1.5 %fusion.20 = (f32[2,128,128]{2,1,0:T(8,128)S(1)}, f32[2,128,128]{2,1,0:T(8,128)S(1)}, f32[2,128,128]{2,1,0:T(8,128)S(1)}) fusion(s32[128,128]{1,0:T(8,128)S(1)} %slice_bitcast_fusion, s32[2]{0:T(128)S(1)} %iota_multiply_fusion.1, s32[128,128]{1,0:T(8,128)S(1)} %slice_bitcast_fusion.1, s32[128,128]{1,0:T(8,128)S(1)} %iota_multiply_fusion), kind=kLoop, calls=%fused_computation.58 | loop fusion | flops 1376256 | bytes 589832 | tf_op jit(solution)/shard_map/cos | solution.py:24
  18.0 20.6 %all-to-all-done = f32[32,16,512]{2,1,0:T(8,128)S(1)} async-done(((f32[32,16,512]{2,1,0:T(8,128)}), f32[32,16,512]{2,1,0:T(8,128)S(1)}, u32[]{:S(2)}, u32[]{:S(2)}) %all-to-all-start) | async-done | bytes 1048608 | tf_op jit(solution)/shard_map/all_to_all | solution.py:347
  38.6 3.0 %transform.1 = f32[2048,128]{1,0:T(8,128)} custom-call(f32[512,512]{1,0:T(8,128)S(1)} %bitcast.117, f32[256,128]{1,0:T(8,128)S(1)} %pad_maximum_fusion.1.first_ref, f32[2,128,128]{2,1,0:T(8,128)S(1)} %get-tuple-element.59.twist_ref, f32[128,256]{1,0:T(8,128)S(1)} %pad_maximum_fusion.2.second_ref), custom_call_target="tpu_custom_call" | custom-call | tf_op jit(solution)/shard_map/transform/pallas_call | solution.py:348
  41.6 6.4 %all-to-all-start.1 = ((f32[32,64,128]{2,1,0:T(8,128)}), f32[32,64,128]{2,1,0:T(8,128)S(1)}, u32[]{:S(2)}, u32[]{:S(2)}) async-start(f32[32,64,128]{2,1,0:T(8,128)} %bitcast.2), calls=%async_computation.1 | async-start | bytes 2097152 | tf_op jit(solution)/shard_map/all_to_all | solution.py:358
  48.0 0.7 slice.209
  48.7 0.7 slice.207
  49.4 0.1 copy.16
  49.5 0.6 copy-done.4
  50.1 0.1 copy.17
  50.2 0.1 copy.15
  50.3 0.2 select_reduce_fusion.profile_ref
  50.5 0.8 toeplitz.1.band_ref
  51.4 0.1 pad_add_fusion.4
  51.4 0.1 broadcast_multiply_fusion
  51.6 2.9 %fusion.2.tab_ref = f32[3,2,256,128]{3,2,1,0:T(8,128)S(1)} fusion(s32[2]{0:T(128)S(1)} %iota_multiply_fusion.2, s32[3,256,128]{2,1,0:T(8,128)S(1)} %broadcast_multiply_fusion), kind=kLoop, calls=%fused_computation.7 | loop fusion | flops 2752512 | bytes 1179656 | tf_op jit(solution)/shard_map/cos | solution.py:24
  54.5 3.7 %fusion.9 = (f32[3,2,128,128]{3,2,1,0:T(8,128)S(1)}, f32[3,2,128,128]{3,2,1,0:T(8,128)}) fusion(s32[3,128,128]{2,1,0:T(8,128)S(1)} %copy-done.1, s32[2]{0:T(128)S(1)} %iota_multiply_fusion.1, s32[3,128,128]{2,1,0:T(8,128)S(1)} %copy-done.2), kind=kLoop, calls=%fused_computation.24 | loop fusion | flops 2752512 | bytes 1179656 | tf_op jit(solution)/shard_map/cos | solution.py:24
  58.2 16.3 %all-to-all-done.1 = f32[32,64,128]{2,1,0:T(8,128)S(1)} async-done(((f32[32,64,128]{2,1,0:T(8,128)}), f32[32,64,128]{2,1,0:T(8,128)S(1)}, u32[]{:S(2)}, u32[]{:S(2)}) %all-to-all-start.1) | async-done | bytes 1048608 | tf_op jit(solution)/shard_map/all_to_all | solution.py:358
  74.5 10.8 %subband.2 = f32[2,128,128]{2,1,0:T(8,128)S(1)} custom-call(f32[32,4,16,128]{3,2,1,0:T(8,128)S(1)} %bitcast.118, f32[3,2,256,128]{3,2,1,0:T(8,128)S(1)} %fusion.2.tab_ref, f32[2,128,128]{2,1,0:T(8,128)S(1)} %get-tuple-element.14.tw_ref), custom_call_target="tpu_custom_call" | custom-call | flops 10000000000 | bytes 8388608 | tf_op jit(solution)/shard_map/subband/pallas_call | solution.py:365
  85.3 0.2 collective-permute-start
  85.5 10.8 %subband.3 = f32[2,128,128]{2,1,0:T(8,128)S(1)} custom-call(f32[32,4,16,128]{3,2,1,0:T(8,128)S(1)} %bitcast.119, f32[3,2,256,128]{3,2,1,0:T(8,128)S(1)} %fusion.2.tab_ref, f32[2,128,128]{2,1,0:T(8,128)S(1)} %get-tuple-element.16.tw_ref), custom_call_target="tpu_custom_call" | custom-call | flops 10000000000 | bytes 8388608 | tf_op jit(solution)/shard_map/subband/pallas_call | solution.py:365
  96.3 0.5 collective-permute-start.3
  96.8 0.0 collective-permute-done
  96.9 0.4 copy-done
  97.3 1.6 %collective-permute-start.1 = (f32[2,128,128]{2,1,0:T(8,128)S(1)}, f32[2,128,128]{2,1,0:T(8,128)S(1)}, u32[]{:S(2)}, u32[]{:S(2)}) collective-permute-start(f32[2,128,128]{2,1,0:T(8,128)S(1)} %pad_maximum_fusion.3), channel_id=1, source_target_pairs={{0,64},{32,96},{64,0},{96,32},{128,192},{160,224},{192,128},{224,1... | collective-permute-start | bytes 393224 | tf_op jit(solution)/shard_map/ppermute | solution.py:389
  98.9 0.0 collective-permute-done.3
  99.0 0.6 collective-permute-start.4
  99.6 4.1 %collective-permute-done.1 = f32[2,128,128]{2,1,0:T(8,128)S(1)} collective-permute-done((f32[2,128,128]{2,1,0:T(8,128)S(1)}, f32[2,128,128]{2,1,0:T(8,128)S(1)}, u32[]{:S(2)}, u32[]{:S(2)}) %collective-permute-start.1) | collective-permute-done | bytes 131104 | tf_op jit(solution)/shard_map/ppermute | solution.py:389
  103.8 3.1 %collective-permute-start.2 = (f32[2,128,128]{2,1,0:T(8,128)S(1)}, f32[2,128,128]{2,1,0:T(8,128)S(1)}, u32[]{:S(2)}, u32[]{:S(2)}) collective-permute-start(f32[2,128,128]{2,1,0:T(8,128)S(1)} %pad_maximum_fusion.4), channel_id=1, source_target_pairs={{0,128},{32,160},{64,192},{96,224},{128,0},{160,32},{192,64},{224,... | collective-permute-start | bytes 393224 | tf_op jit(solution)/shard_map/ppermute | solution.py:389
  106.9 0.0 collective-permute-done.4
  107.0 2.3 %collective-permute-start.5 = (f32[2,128,128]{2,1,0:T(8,128)S(1)}, f32[2,128,128]{2,1,0:T(8,128)S(1)}, u32[]{:S(2)}, u32[]{:S(2)}) collective-permute-start(f32[2,128,128]{2,1,0:T(8,128)S(1)} %pad_maximum_fusion.6), channel_id=1, source_target_pairs={{0,128},{32,160},{64,192},{96,224},{128,0},{160,32},{192,64},{224,... | collective-permute-start | bytes 393224 | tf_op jit(solution)/shard_map/ppermute | solution.py:389
  109.3 2.5 %collective-permute-done.2 = f32[2,128,128]{2,1,0:T(8,128)S(1)} collective-permute-done((f32[2,128,128]{2,1,0:T(8,128)S(1)}, f32[2,128,128]{2,1,0:T(8,128)S(1)}, u32[]{:S(2)}, u32[]{:S(2)}) %collective-permute-start.2) | collective-permute-done | bytes 131104 | tf_op jit(solution)/shard_map/ppermute | solution.py:389
  111.9 5.1 %collective-permute-start.7 = (f32[2,32,128]{2,1,0:T(8,128)S(1)}, f32[2,32,128]{2,1,0:T(8,128)S(1)}, u32[]{:S(2)}, u32[]{:S(2)}) collective-permute-start(f32[2,32,128]{2,1,0:T(8,128)S(1)} %get-tuple-element.47), channel_id=1, source_target_pairs={{1,0},{2,1},{3,2},{4,3},{5,4},{6,5},{7,6},{8,7},{9,8},{10,9},{11,1... | collective-permute-start | bytes 98312 | tf_op jit(solution)/shard_map/ppermute | solution.py:402
  117.0 1.9 %collective-permute-start.6 = (f32[2,32,128]{2,1,0:T(8,128)S(1)}, f32[2,32,128]{2,1,0:T(8,128)S(1)}, u32[]{:S(2)}, u32[]{:S(2)}) collective-permute-start(f32[2,32,128]{2,1,0:T(8,128)S(1)} %get-tuple-element.48), channel_id=1, source_target_pairs={{0,1},{1,2},{2,3},{3,4},{4,5},{5,6},{6,7},{7,8},{8,9},{9,10},{10,1... | collective-permute-start | bytes 98312 | tf_op jit(solution)/shard_map/ppermute | solution.py:399
  119.0 0.0 collective-permute-done.5
  119.0 0.0 collective-permute-done.7.right_ref
  119.1 5.9 %collective-permute-done.6.left_ref = f32[2,32,128]{2,1,0:T(8,128)S(1)} collective-permute-done((f32[2,32,128]{2,1,0:T(8,128)S(1)}, f32[2,32,128]{2,1,0:T(8,128)S(1)}, u32[]{:S(2)}, u32[]{:S(2)}) %collective-permute-start.6) | collective-permute-done | bytes 32800 | tf_op jit(solution)/shard_map/ppermute | solution.py:399
  124.9 0.7 edge_bins.1.edge_ref
  125.7 2.5 %inner_bins.1 = f32[128,256]{1,0:T(8,128)} custom-call(f32[2,128,128]{2,1,0:T(8,128)S(1)} %pad_maximum_fusion.outer_ref, f32[2,128,128]{2,1,0:T(8,128)S(1)} %pad_maximum_fusion.7.mid_ref, f32[2,32,128]{2,1,0:T(8,128)S(1)} %edge_bins.1.edge_ref, bf16[2048,256]{1,0:T(8,128)(2,1)S(1)} %toeplitz.1.band_ref), custom_call_target="tpu_custom_call" | custom-call | tf_op jit(solution)/shard_map/inner_bins/pallas_call | solution.py:411
  (46 shorter events, 0.5 us)
Async XLA Ops:
  0.0 38.6 %all-to-all-start = ((f32[32,16,512]{2,1,0:T(8,128)}), f32[32,16,512]{2,1,0:T(8,128)S(1)}, u32[]{:S(2)}, u32[]{:S(2)}) async-start(f32[32,16,512]{2,1,0:T(8,128)} %bitcast.120), calls=%async_computation | async-start | bytes 2097152 | tf_op jit(solution)/shard_map/all_to_all | solution.py:347
  11.6 0.7 copy-start.6
  41.6 32.8 %all-to-all-start.1 = ((f32[32,64,128]{2,1,0:T(8,128)}), f32[32,64,128]{2,1,0:T(8,128)S(1)}, u32[]{:S(2)}, u32[]{:S(2)}) async-start(f32[32,64,128]{2,1,0:T(8,128)} %bitcast.2), calls=%async_computation.1 | async-start | bytes 2097152 | tf_op jit(solution)/shard_map/all_to_all | solution.py:358
  48.7 0.7 copy-start.5
  48.7 1.5 %copy-start.3 = (s32[512,64]{0,1:T(8,128)S(1)}, s32[512,64]{0,1:T(8,128)}, u32[]{:S(2)}) copy-start(s32[512,64]{0,1:T(8,128)} %param.12) | copy-start | bytes 393220
  49.4 0.7 copy-start.4
  51.5 2.9 %copy-start.1 = (s32[3,128,128]{2,1,0:T(8,128)S(1)}, s32[3,128,128]{2,1,0:T(8,128)}, u32[]{:S(2)}) copy-start(s32[3,128,128]{2,1,0:T(8,128)} %slice.209) | copy-start | bytes 589828
  51.6 2.9 %copy-start.2 = (s32[3,128,128]{2,1,0:T(8,128)S(1)}, s32[3,128,128]{2,1,0:T(8,128)}, u32[]{:S(2)}) copy-start(s32[3,128,128]{2,1,0:T(8,128)} %slice.207) | copy-start | bytes 589828
  85.3 11.6 %collective-permute-start = (f32[2,128,128]{2,1,0:T(8,128)S(1)}, f32[2,128,128]{2,1,0:T(8,128)S(1)}, u32[]{:S(2)}, u32[]{:S(2)}) collective-permute-start(f32[2,128,128]{2,1,0:T(8,128)S(1)} %subband.2), channel_id=1, source_target_pairs={{0,32},{32,0},{64,96},{96,64},{128,160},{160,128},{192,224},{224,1... | collective-permute-start | bytes 393224 | tf_op jit(solution)/shard_map/ppermute | solution.py:389
  96.3 1.0 copy-start
  96.3 2.6 %collective-permute-start.3 = (f32[2,128,128]{2,1,0:T(8,128)S(1)}, f32[2,128,128]{2,1,0:T(8,128)S(1)}, u32[]{:S(2)}, u32[]{:S(2)}) collective-permute-start(f32[2,128,128]{2,1,0:T(8,128)S(1)} %subband.3), channel_id=1, source_target_pairs={{0,32},{32,0},{64,96},{96,64},{128,160},{160,128},{192,224},{224,1... | collective-permute-start | bytes 393224 | tf_op jit(solution)/shard_map/ppermute | solution.py:389
  97.3 6.4 %collective-permute-start.1 = (f32[2,128,128]{2,1,0:T(8,128)S(1)}, f32[2,128,128]{2,1,0:T(8,128)S(1)}, u32[]{:S(2)}, u32[]{:S(2)}) collective-permute-start(f32[2,128,128]{2,1,0:T(8,128)S(1)} %pad_maximum_fusion.3), channel_id=1, source_target_pairs={{0,64},{32,96},{64,0},{96,32},{128,192},{160,224},{192,128},{224,1... | collective-permute-start | bytes 393224 | tf_op jit(solution)/shard_map/ppermute | solution.py:389
  99.0 7.9 %collective-permute-start.4 = (f32[2,128,128]{2,1,0:T(8,128)S(1)}, f32[2,128,128]{2,1,0:T(8,128)S(1)}, u32[]{:S(2)}, u32[]{:S(2)}) collective-permute-start(f32[2,128,128]{2,1,0:T(8,128)S(1)} %pad_maximum_fusion.5), channel_id=1, source_target_pairs={{0,64},{32,96},{64,0},{96,32},{128,192},{160,224},{192,128},{224,1... | collective-permute-start | bytes 393224 | tf_op jit(solution)/shard_map/ppermute | solution.py:389
  103.8 8.0 %collective-permute-start.2 = (f32[2,128,128]{2,1,0:T(8,128)S(1)}, f32[2,128,128]{2,1,0:T(8,128)S(1)}, u32[]{:S(2)}, u32[]{:S(2)}) collective-permute-start(f32[2,128,128]{2,1,0:T(8,128)S(1)} %pad_maximum_fusion.4), channel_id=1, source_target_pairs={{0,128},{32,160},{64,192},{96,224},{128,0},{160,32},{192,64},{224,... | collective-permute-start | bytes 393224 | tf_op jit(solution)/shard_map/ppermute | solution.py:389
  107.0 12.0 %collective-permute-start.5 = (f32[2,128,128]{2,1,0:T(8,128)S(1)}, f32[2,128,128]{2,1,0:T(8,128)S(1)}, u32[]{:S(2)}, u32[]{:S(2)}) collective-permute-start(f32[2,128,128]{2,1,0:T(8,128)S(1)} %pad_maximum_fusion.6), channel_id=1, source_target_pairs={{0,128},{32,160},{64,192},{96,224},{128,0},{160,32},{192,64},{224,... | collective-permute-start | bytes 393224 | tf_op jit(solution)/shard_map/ppermute | solution.py:389
  111.9 7.2 %collective-permute-start.7 = (f32[2,32,128]{2,1,0:T(8,128)S(1)}, f32[2,32,128]{2,1,0:T(8,128)S(1)}, u32[]{:S(2)}, u32[]{:S(2)}) collective-permute-start(f32[2,32,128]{2,1,0:T(8,128)S(1)} %get-tuple-element.47), channel_id=1, source_target_pairs={{1,0},{2,1},{3,2},{4,3},{5,4},{6,5},{7,6},{8,7},{9,8},{10,9},{11,1... | collective-permute-start | bytes 98312 | tf_op jit(solution)/shard_map/ppermute | solution.py:402
  117.0 7.9 %collective-permute-start.6 = (f32[2,32,128]{2,1,0:T(8,128)S(1)}, f32[2,32,128]{2,1,0:T(8,128)S(1)}, u32[]{:S(2)}, u32[]{:S(2)}) collective-permute-start(f32[2,32,128]{2,1,0:T(8,128)S(1)} %get-tuple-element.48), channel_id=1, source_target_pairs={{0,1},{1,2},{2,3},{3,4},{4,5},{5,6},{6,7},{7,8},{8,9},{9,10},{10,1... | collective-permute-start | bytes 98312 | tf_op jit(solution)/shard_map/ppermute | solution.py:399

commit v7 on v6

--- a/solution.py
+++ b/solution.py
@@ -249,7 +249,26 @@
     return re * re + im * im
 
 
-def edge_kernel(left_ref, outer_ref, right_ref, band_ref, out_ref):
+def inner_kernel(outer_ref, mid_ref, band_ref, out_ref):
+    near = 2 * REACH
+    columns = [
+        jnp.concatenate([outer_ref[x, :near], mid_ref[x], outer_ref[x, near:]], axis=0)
+        for x in range(2)
+    ]
+    whole = jnp.concatenate(columns, axis=1)
+    per = 4
+    for i in range(out_ref.shape[0] // near):
+        high, low = windows(whole[i * near : i * near + LANES])
+        best = jnp.zeros((near, LANES), f32)
+        for step in range(band_ref.shape[0] // (per * near)):
+            at = slice(step * per * near, (step + 1) * per * near)
+            got = products(band_ref[at, :], high, low)
+            for j in range(per):
+                best = jnp.maximum(best, power(got[j * near : (j + 1) * near]))
+        out_ref[i * near : (i + 1) * near, :] = best
+
+
+def edge_kernel(left_ref, outer_ref, right_ref, inner_ref, band_ref, out_ref):
     near = 2 * REACH
     pad = jnp.zeros((LANES - 3 * REACH, LANES), f32)
     columns = [
@@ -269,30 +288,7 @@
             for side in range(2):
                 lanes = slice(side * 2 * LANES, (side + 1) * 2 * LANES)
                 best[side] = jnp.maximum(best[side], power(mine[:, lanes]))
-    out_ref[0] = best[0]
-    out_ref[1] = best[1]
-
-
-def inner_kernel(outer_ref, mid_ref, edge_ref, band_ref, out_ref):
-    near = 2 * REACH
-    blocks = out_ref.shape[1] // near - 1
-    columns = [
-        jnp.concatenate([outer_ref[x, :near], mid_ref[x], outer_ref[x, near:]], axis=0)
-        for x in range(2)
-    ]
-    whole = jnp.concatenate(columns, axis=1)
-    per = 4
-    best = []
-    for i in range(blocks):
-        high, low = windows(whole[i * near : i * near + LANES])
-        mine = jnp.zeros((near, LANES), f32)
-        for step in range(band_ref.shape[0] // (per * near)):
-            at = slice(step * per * near, (step + 1) * per * near)
-            got = products(band_ref[at, :], high, low)
-            for j in range(per):
-                mine = jnp.maximum(mine, power(got[j * near : (j + 1) * near]))
-        best.append(mine)
-    out_ref[...] = jnp.concatenate([edge_ref[0]] + best + [edge_ref[1]], axis=0).T
+    out_ref[...] = jnp.concatenate([best[0], inner_ref[...], best[1]], axis=0).T
 
 
 def per_device(samples, channel_delay, merge_slope, tap_offset, tap_weight):
@@ -400,22 +396,23 @@
         outer[:, bins_dev // 2 - REACH :], "freq", [(i, i + 1) for i in range(ends)]
     )
     from_right = lax.ppermute(outer[:, :REACH], "freq", [(i + 1, i) for i in range(ends)])
-    edges = pl.pallas_call(
+    inner = pl.pallas_call(
+        inner_kernel,
+        out_shape=jax.ShapeDtypeStruct((bins_dev - 2 * REACH, block), f32),
+        in_specs=[vmem] * 3,
+        out_specs=vmem,
+        cost_estimate=pl.CostEstimate(flops=2 * 10**9, bytes_accessed=2**21, transcendentals=0),
+        compiler_params=pltpu.CompilerParams(vmem_limit_bytes=FILTER_VMEM),
+        name="inner_bins",
+    )(outer, middle, band)
+    return pl.pallas_call(
         edge_kernel,
-        out_shape=jax.ShapeDtypeStruct((2, REACH, block), f32),
-        in_specs=[vmem] * 4,
+        out_shape=jax.ShapeDtypeStruct((block, bins_dev), f32),
+        in_specs=[vmem] * 5,
         out_specs=vmem,
         compiler_params=pltpu.CompilerParams(vmem_limit_bytes=FILTER_VMEM),
         name="edge_bins",
-    )(from_left, outer, from_right, band)
-    return pl.pallas_call(
-        inner_kernel,
-        out_shape=jax.ShapeDtypeStruct((block, bins_dev), f32),
-        in_specs=[vmem] * 4,
-        out_specs=vmem,
-        compiler_params=pltpu.CompilerParams(vmem_limit_bytes=FILTER_VMEM),
-        name="inner_bins",
-    )(outer, middle, edges, band)
+    )(from_left, outer, from_right, inner, band)
 
 
 def solution(mesh):

time: 129 us -> 127 us (0.984)
  waiting for transfers between devices: 49.4 us -> 47.6 us
    ppermute x1, waiting for transfers between devices: 5.87 us -> 4.05 us  [per_device(): lax.ppermute(outer[:, bins_dev // 2 - REACH:], 'freq', [(i, i + 1) for i...]
  transfers between devices with their start and end apart: 10 -> 10, of which waited for: 5 -> 5; matrix products, arithmetic and copies ran while one was open for 12% -> 12% of each run, Pallas kernels for 9% -> 11%
where the time goes in v7:
time: 127 us; the launch traced here: 126 us
  waiting for transfers between devices  47.6 us (37%)
  starting transfers between devices  33.1 us (26%)
  Pallas kernels  28.7 us (23%)
  other arithmetic  13.2 us (10%)
  local copies, waits for them, and re-layouts  3.37 us (3%)
    pallas_call x2, Pallas kernels, per_device(): pl.pallas_call(functools.partial(sub_kernel, pair), out_shape=jax.ShapeDt...  21.6 us
    all_to_all x1, waiting for transfers between devices, per_device(): lax.all_to_all(blocks, 'freq', split_axis=0, concat_axis=0, tiled=True)  20.6 us
    all_to_all x1, waiting for transfers between devices, per_device(): spec = lax.all_to_all(spec, 'freq', split_axis=0, concat_axis=0, tiled=True)  16.3 us
    all_to_all x1, starting transfers between devices, per_device(): lax.all_to_all(blocks, 'freq', split_axis=0, concat_axis=0, tiled=True)  11.4 us
    ppermute x6, starting transfers between devices, per_device(): lax.ppermute(mine, 'band', [(j, j ^ half) for j in range(band_count)])  8.39 us
    cos x4, other arithmetic, turning(): return (jnp.cos(angle), jnp.sin(angle))  8.38 us
    ppermute x6, waiting for transfers between devices, per_device(): lax.ppermute(mine, 'band', [(j, j ^ half) for j in range(band_count)])  6.61 us
    all_to_all x1, starting transfers between devices, per_device(): spec = lax.all_to_all(spec, 'freq', split_axis=0, concat_axis=0, tiled=True)  6.37 us
  transfers between devices with their start and end apart: 10, of which 5 were waited for; matrix products, arithmetic and copies ran while one was open for 12% of the time, Pallas kernels for 11%

profile of v7, /device:TPU:32, one launch (start us, length us, event | category | flops | bytes accessed | tf_op | source)
XLA Modules:
  0.0 126.4 jit_solution(14966771253193086333)
XLA Ops:
  0.0 11.4 %all-to-all-start = ((f32[32,16,512]{2,1,0:T(8,128)}), f32[32,16,512]{2,1,0:T(8,128)S(1)}, u32[]{:S(2)}, u32[]{:S(2)}) async-start(f32[32,16,512]{2,1,0:T(8,128)} %bitcast.120), calls=%async_computation | async-start | bytes 2097152 | tf_op jit(solution)/shard_map/all_to_all | solution.py:343
  11.5 0.1 pad_add_fusion.2
  11.6 0.7 copy-done.6
  12.2 0.7 fusion.59
  13.0 1.4 %and_select_fusion.4 = (s32[1,128]{1,0:T(1,128)S(1)}, s32[1,128]{1,0:T(1,128)S(1)}) fusion(s32[]{:T(128)} %get-tuple-element.20, s32[]{:T(128)S(6)} %mul.354, s32[]{:T(128)} %get-tuple-element.19), kind=kLoop, calls=%fused_computation.179 | loop fusion | flops 7040 | bytes 1036 | tf_op jit(solution)/shard_map/jit(remainder)/select_n | solution.py:314
  14.3 0.1 pad_add_fusion.3
  14.4 1.3 and_select_fusion
  15.7 0.3 select_multiply_fusion.1
  16.1 0.3 fusion.52
  16.4 0.1 broadcast_multiply_fusion.1
  16.5 1.5 %fusion.20 = (f32[2,128,128]{2,1,0:T(8,128)S(1)}, f32[2,128,128]{2,1,0:T(8,128)S(1)}, f32[2,128,128]{2,1,0:T(8,128)S(1)}) fusion(s32[128,128]{1,0:T(8,128)S(1)} %slice_bitcast_fusion, s32[2]{0:T(128)S(1)} %iota_multiply_fusion.1, s32[128,128]{1,0:T(8,128)S(1)} %slice_bitcast_fusion.1, s32[128,128]{1,0:T(8,128)S(1)} %iota_multiply_fusion), kind=kLoop, calls=%fused_computation.58 | loop fusion | flops 1376256 | bytes 589832 | tf_op jit(solution)/shard_map/cos | solution.py:24
  18.0 20.6 %all-to-all-done = f32[32,16,512]{2,1,0:T(8,128)S(1)} async-done(((f32[32,16,512]{2,1,0:T(8,128)}), f32[32,16,512]{2,1,0:T(8,128)S(1)}, u32[]{:S(2)}, u32[]{:S(2)}) %all-to-all-start) | async-done | bytes 1048608 | tf_op jit(solution)/shard_map/all_to_all | solution.py:343
  38.6 3.0 %transform.1 = f32[2048,128]{1,0:T(8,128)} custom-call(f32[512,512]{1,0:T(8,128)S(1)} %bitcast.117, f32[256,128]{1,0:T(8,128)S(1)} %pad_maximum_fusion.1.first_ref, f32[2,128,128]{2,1,0:T(8,128)S(1)} %get-tuple-element.59.twist_ref, f32[128,256]{1,0:T(8,128)S(1)} %pad_maximum_fusion.2.second_ref), custom_call_target="tpu_custom_call" | custom-call | tf_op jit(solution)/shard_map/transform/pallas_call | solution.py:344
  41.6 6.4 %all-to-all-start.1 = ((f32[32,64,128]{2,1,0:T(8,128)}), f32[32,64,128]{2,1,0:T(8,128)S(1)}, u32[]{:S(2)}, u32[]{:S(2)}) async-start(f32[32,64,128]{2,1,0:T(8,128)} %bitcast.2), calls=%async_computation.1 | async-start | bytes 2097152 | tf_op jit(solution)/shard_map/all_to_all | solution.py:354
  48.0 0.7 slice.209
  48.7 0.7 slice.207
  49.4 0.1 copy.16
  49.5 0.6 copy-done.4
  50.1 0.1 copy.17
  50.2 0.1 copy.15
  50.3 0.2 select_reduce_fusion.profile_ref
  50.5 0.8 toeplitz.1.band_ref
  51.4 0.1 pad_add_fusion.4
  51.4 0.1 broadcast_multiply_fusion
  51.6 2.9 %fusion.2.tab_ref = f32[3,2,256,128]{3,2,1,0:T(8,128)S(1)} fusion(s32[2]{0:T(128)S(1)} %iota_multiply_fusion.2, s32[3,256,128]{2,1,0:T(8,128)S(1)} %broadcast_multiply_fusion), kind=kLoop, calls=%fused_computation.7 | loop fusion | flops 2752512 | bytes 1179656 | tf_op jit(solution)/shard_map/cos | solution.py:24
  54.5 3.7 %fusion.9 = (f32[3,2,128,128]{3,2,1,0:T(8,128)S(1)}, f32[3,2,128,128]{3,2,1,0:T(8,128)}) fusion(s32[3,128,128]{2,1,0:T(8,128)S(1)} %copy-done.1, s32[2]{0:T(128)S(1)} %iota_multiply_fusion.1, s32[3,128,128]{2,1,0:T(8,128)S(1)} %copy-done.2), kind=kLoop, calls=%fused_computation.24 | loop fusion | flops 2752512 | bytes 1179656 | tf_op jit(solution)/shard_map/cos | solution.py:24
  58.2 16.3 %all-to-all-done.1 = f32[32,64,128]{2,1,0:T(8,128)S(1)} async-done(((f32[32,64,128]{2,1,0:T(8,128)}), f32[32,64,128]{2,1,0:T(8,128)S(1)}, u32[]{:S(2)}, u32[]{:S(2)}) %all-to-all-start.1) | async-done | bytes 1048608 | tf_op jit(solution)/shard_map/all_to_all | solution.py:354
  74.5 10.8 %subband.2 = f32[2,128,128]{2,1,0:T(8,128)S(1)} custom-call(f32[32,4,16,128]{3,2,1,0:T(8,128)S(1)} %bitcast.118, f32[3,2,256,128]{3,2,1,0:T(8,128)S(1)} %fusion.2.tab_ref, f32[2,128,128]{2,1,0:T(8,128)S(1)} %get-tuple-element.14.tw_ref), custom_call_target="tpu_custom_call" | custom-call | flops 10000000000 | bytes 8388608 | tf_op jit(solution)/shard_map/subband/pallas_call | solution.py:361
  85.3 0.2 collective-permute-start
  85.5 10.8 %subband.3 = f32[2,128,128]{2,1,0:T(8,128)S(1)} custom-call(f32[32,4,16,128]{3,2,1,0:T(8,128)S(1)} %bitcast.119, f32[3,2,256,128]{3,2,1,0:T(8,128)S(1)} %fusion.2.tab_ref, f32[2,128,128]{2,1,0:T(8,128)S(1)} %get-tuple-element.16.tw_ref), custom_call_target="tpu_custom_call" | custom-call | flops 10000000000 | bytes 8388608 | tf_op jit(solution)/shard_map/subband/pallas_call | solution.py:361
  96.3 0.5 collective-permute-start.5
  96.8 0.0 collective-permute-done
  96.9 0.4 copy-done
  97.3 1.6 %collective-permute-start.1 = (f32[2,128,128]{2,1,0:T(8,128)S(1)}, f32[2,128,128]{2,1,0:T(8,128)S(1)}, u32[]{:S(2)}, u32[]{:S(2)}) collective-permute-start(f32[2,128,128]{2,1,0:T(8,128)S(1)} %pad_maximum_fusion.3), channel_id=1, source_target_pairs={{0,64},{32,96},{64,0},{96,32},{128,192},{160,224},{192,128},{224,1... | collective-permute-start | bytes 393224 | tf_op jit(solution)/shard_map/ppermute | solution.py:385
  98.9 0.0 collective-permute-done.5
  99.0 0.6 collective-permute-start.6
  99.6 4.1 %collective-permute-done.1 = f32[2,128,128]{2,1,0:T(8,128)S(1)} collective-permute-done((f32[2,128,128]{2,1,0:T(8,128)S(1)}, f32[2,128,128]{2,1,0:T(8,128)S(1)}, u32[]{:S(2)}, u32[]{:S(2)}) %collective-permute-start.1) | collective-permute-done | bytes 131104 | tf_op jit(solution)/shard_map/ppermute | solution.py:385
  103.8 3.1 %collective-permute-start.2 = (f32[2,128,128]{2,1,0:T(8,128)S(1)}, f32[2,128,128]{2,1,0:T(8,128)S(1)}, u32[]{:S(2)}, u32[]{:S(2)}) collective-permute-start(f32[2,128,128]{2,1,0:T(8,128)S(1)} %pad_maximum_fusion.4), channel_id=1, source_target_pairs={{0,128},{32,160},{64,192},{96,224},{128,0},{160,32},{192,64},{224,... | collective-permute-start | bytes 393224 | tf_op jit(solution)/shard_map/ppermute | solution.py:385
  106.9 0.0 collective-permute-done.6
  107.0 2.3 %collective-permute-start.7 = (f32[2,128,128]{2,1,0:T(8,128)S(1)}, f32[2,128,128]{2,1,0:T(8,128)S(1)}, u32[]{:S(2)}, u32[]{:S(2)}) collective-permute-start(f32[2,128,128]{2,1,0:T(8,128)S(1)} %pad_maximum_fusion.6), channel_id=1, source_target_pairs={{0,128},{32,160},{64,192},{96,224},{128,0},{160,32},{192,64},{224,... | collective-permute-start | bytes 393224 | tf_op jit(solution)/shard_map/ppermute | solution.py:385
  109.3 2.5 %collective-permute-done.2 = f32[2,128,128]{2,1,0:T(8,128)S(1)} collective-permute-done((f32[2,128,128]{2,1,0:T(8,128)S(1)}, f32[2,128,128]{2,1,0:T(8,128)S(1)}, u32[]{:S(2)}, u32[]{:S(2)}) %collective-permute-start.2) | collective-permute-done | bytes 131104 | tf_op jit(solution)/shard_map/ppermute | solution.py:385
  111.9 5.1 %collective-permute-start.4 = (f32[2,32,128]{2,1,0:T(8,128)S(1)}, f32[2,32,128]{2,1,0:T(8,128)S(1)}, u32[]{:S(2)}, u32[]{:S(2)}) collective-permute-start(f32[2,32,128]{2,1,0:T(8,128)S(1)} %get-tuple-element.47), channel_id=1, source_target_pairs={{1,0},{2,1},{3,2},{4,3},{5,4},{6,5},{7,6},{8,7},{9,8},{10,9},{11,1... | collective-permute-start | bytes 98312 | tf_op jit(solution)/shard_map/ppermute | solution.py:398
  117.0 1.9 %collective-permute-start.3 = (f32[2,32,128]{2,1,0:T(8,128)S(1)}, f32[2,32,128]{2,1,0:T(8,128)S(1)}, u32[]{:S(2)}, u32[]{:S(2)}) collective-permute-start(f32[2,32,128]{2,1,0:T(8,128)S(1)} %get-tuple-element.48), channel_id=1, source_target_pairs={{0,1},{1,2},{2,3},{3,4},{4,5},{5,6},{6,7},{7,8},{8,9},{9,10},{10,1... | collective-permute-start | bytes 98312 | tf_op jit(solution)/shard_map/ppermute | solution.py:395
  119.0 0.0 collective-permute-done.7
  119.0 1.8 %inner_bins.1.inner_ref = f32[192,128]{1,0:T(8,128)S(1)} custom-call(f32[2,128,128]{2,1,0:T(8,128)S(1)} %pad_maximum_fusion.outer_ref, f32[2,128,128]{2,1,0:T(8,128)S(1)} %pad_maximum_fusion.7.mid_ref, bf16[2048,256]{1,0:T(8,128)(2,1)S(1)} %toeplitz.1.band_ref), custom_call_target="tpu_custom_call" | custom-call | flops 2000000000 | bytes 2097152 | tf_op jit(solution)/shard_map/inner_bins/pallas_call | solution.py:399
  120.9 0.0 collective-permute-done.4.right_ref
  120.9 4.1 %collective-permute-done.3.left_ref = f32[2,32,128]{2,1,0:T(8,128)S(1)} collective-permute-done((f32[2,32,128]{2,1,0:T(8,128)S(1)}, f32[2,32,128]{2,1,0:T(8,128)S(1)}, u32[]{:S(2)}, u32[]{:S(2)}) %collective-permute-start.3) | collective-permute-done | bytes 32800 | tf_op jit(solution)/shard_map/ppermute | solution.py:395
  124.9 1.5 %edge_bins.1 = f32[128,256]{1,0:T(8,128)} custom-call(f32[2,32,128]{2,1,0:T(8,128)S(1)} %collective-permute-done.3.left_ref, f32[2,128,128]{2,1,0:T(8,128)S(1)} %pad_maximum_fusion.outer_ref, f32[2,32,128]{2,1,0:T(8,128)S(1)} %collective-permute-done.4.right_ref, f32[192,128]{1,0:T(8,128)S(1)} %inner_bins.1.inner_ref, bf16[2048,256]{1,0:T(8,128)(2,1)S(1)} %toeplitz.1.band_ref), custom_call_target="tpu_custom_call" | custom-call | tf_op jit(solution)/shard_map/edge_bins/pallas_call | solution.py:408
  (46 shorter events, 0.5 us)
Async XLA Ops:
  0.0 38.6 %all-to-all-start = ((f32[32,16,512]{2,1,0:T(8,128)}), f32[32,16,512]{2,1,0:T(8,128)S(1)}, u32[]{:S(2)}, u32[]{:S(2)}) async-start(f32[32,16,512]{2,1,0:T(8,128)} %bitcast.120), calls=%async_computation | async-start | bytes 2097152 | tf_op jit(solution)/shard_map/all_to_all | solution.py:343
  11.6 0.7 copy-start.6
  41.6 32.8 %all-to-all-start.1 = ((f32[32,64,128]{2,1,0:T(8,128)}), f32[32,64,128]{2,1,0:T(8,128)S(1)}, u32[]{:S(2)}, u32[]{:S(2)}) async-start(f32[32,64,128]{2,1,0:T(8,128)} %bitcast.2), calls=%async_computation.1 | async-start | bytes 2097152 | tf_op jit(solution)/shard_map/all_to_all | solution.py:354
  48.7 0.7 copy-start.5
  48.7 1.5 %copy-start.3 = (s32[512,64]{0,1:T(8,128)S(1)}, s32[512,64]{0,1:T(8,128)}, u32[]{:S(2)}) copy-start(s32[512,64]{0,1:T(8,128)} %param.12) | copy-start | bytes 393220
  49.4 0.7 copy-start.4
  51.5 2.9 %copy-start.1 = (s32[3,128,128]{2,1,0:T(8,128)S(1)}, s32[3,128,128]{2,1,0:T(8,128)}, u32[]{:S(2)}) copy-start(s32[3,128,128]{2,1,0:T(8,128)} %slice.209) | copy-start | bytes 589828
  51.6 2.9 %copy-start.2 = (s32[3,128,128]{2,1,0:T(8,128)S(1)}, s32[3,128,128]{2,1,0:T(8,128)}, u32[]{:S(2)}) copy-start(s32[3,128,128]{2,1,0:T(8,128)} %slice.207) | copy-start | bytes 589828
  85.3 11.6 %collective-permute-start = (f32[2,128,128]{2,1,0:T(8,128)S(1)}, f32[2,128,128]{2,1,0:T(8,128)S(1)}, u32[]{:S(2)}, u32[]{:S(2)}) collective-permute-start(f32[2,128,128]{2,1,0:T(8,128)S(1)} %subband.2), channel_id=1, source_target_pairs={{0,32},{32,0},{64,96},{96,64},{128,160},{160,128},{192,224},{224,1... | collective-permute-start | bytes 393224 | tf_op jit(solution)/shard_map/ppermute | solution.py:385
  96.3 1.0 copy-start
  96.3 2.6 %collective-permute-start.5 = (f32[2,128,128]{2,1,0:T(8,128)S(1)}, f32[2,128,128]{2,1,0:T(8,128)S(1)}, u32[]{:S(2)}, u32[]{:S(2)}) collective-permute-start(f32[2,128,128]{2,1,0:T(8,128)S(1)} %subband.3), channel_id=1, source_target_pairs={{0,32},{32,0},{64,96},{96,64},{128,160},{160,128},{192,224},{224,1... | collective-permute-start | bytes 393224 | tf_op jit(solution)/shard_map/ppermute | solution.py:385
  97.3 6.4 %collective-permute-start.1 = (f32[2,128,128]{2,1,0:T(8,128)S(1)}, f32[2,128,128]{2,1,0:T(8,128)S(1)}, u32[]{:S(2)}, u32[]{:S(2)}) collective-permute-start(f32[2,128,128]{2,1,0:T(8,128)S(1)} %pad_maximum_fusion.3), channel_id=1, source_target_pairs={{0,64},{32,96},{64,0},{96,32},{128,192},{160,224},{192,128},{224,1... | collective-permute-start | bytes 393224 | tf_op jit(solution)/shard_map/ppermute | solution.py:385
  99.0 7.9 %collective-permute-start.6 = (f32[2,128,128]{2,1,0:T(8,128)S(1)}, f32[2,128,128]{2,1,0:T(8,128)S(1)}, u32[]{:S(2)}, u32[]{:S(2)}) collective-permute-start(f32[2,128,128]{2,1,0:T(8,128)S(1)} %pad_maximum_fusion.5), channel_id=1, source_target_pairs={{0,64},{32,96},{64,0},{96,32},{128,192},{160,224},{192,128},{224,1... | collective-permute-start | bytes 393224 | tf_op jit(solution)/shard_map/ppermute | solution.py:385
  103.8 8.0 %collective-permute-start.2 = (f32[2,128,128]{2,1,0:T(8,128)S(1)}, f32[2,128,128]{2,1,0:T(8,128)S(1)}, u32[]{:S(2)}, u32[]{:S(2)}) collective-permute-start(f32[2,128,128]{2,1,0:T(8,128)S(1)} %pad_maximum_fusion.4), channel_id=1, source_target_pairs={{0,128},{32,160},{64,192},{96,224},{128,0},{160,32},{192,64},{224,... | collective-permute-start | bytes 393224 | tf_op jit(solution)/shard_map/ppermute | solution.py:385
  107.0 12.0 %collective-permute-start.7 = (f32[2,128,128]{2,1,0:T(8,128)S(1)}, f32[2,128,128]{2,1,0:T(8,128)S(1)}, u32[]{:S(2)}, u32[]{:S(2)}) collective-permute-start(f32[2,128,128]{2,1,0:T(8,128)S(1)} %pad_maximum_fusion.6), channel_id=1, source_target_pairs={{0,128},{32,160},{64,192},{96,224},{128,0},{160,32},{192,64},{224,... | collective-permute-start | bytes 393224 | tf_op jit(solution)/shard_map/ppermute | solution.py:385
  111.9 9.0 %collective-permute-start.4 = (f32[2,32,128]{2,1,0:T(8,128)S(1)}, f32[2,32,128]{2,1,0:T(8,128)S(1)}, u32[]{:S(2)}, u32[]{:S(2)}) collective-permute-start(f32[2,32,128]{2,1,0:T(8,128)S(1)} %get-tuple-element.47), channel_id=1, source_target_pairs={{1,0},{2,1},{3,2},{4,3},{5,4},{6,5},{7,6},{8,7},{9,8},{10,9},{11,1... | collective-permute-start | bytes 98312 | tf_op jit(solution)/shard_map/ppermute | solution.py:398
  117.0 7.9 %collective-permute-start.3 = (f32[2,32,128]{2,1,0:T(8,128)S(1)}, f32[2,32,128]{2,1,0:T(8,128)S(1)}, u32[]{:S(2)}, u32[]{:S(2)}) collective-permute-start(f32[2,32,128]{2,1,0:T(8,128)S(1)} %get-tuple-element.48), channel_id=1, source_target_pairs={{0,1},{1,2},{2,3},{3,4},{4,5},{5,6},{6,7},{7,8},{8,9},{9,10},{10,1... | collective-permute-start | bytes 98312 | tf_op jit(solution)/shard_map/ppermute | solution.py:395

commit v8 on v7

--- a/solution.py
+++ b/solution.py
@@ -126,7 +126,7 @@
                 parts[slot, to, LANES:] = low
         first, step, unit = ((tab_ref[i, 0, at, :], tab_ref[i, 1, at, :]) for i in range(3))
         bin_turn = add_angles(unit, unit)
-        for b in range(GROUP // 2):
+        for b in range(2):
             offset[b, 0, at, :], offset[b, 1, at, :] = unit
             unit = add_angles(unit, bin_turn)
         for _ in range(3):
@@ -171,9 +171,11 @@
             advance = (tab_ref[1, 0, at, :], tab_ref[1, 1, at, :])
             mids = [(centre[slot, 0, at, :], centre[slot, 1, at, :])]
             mids.append(add_angles(mids[0], advance))
-            for b in range(GROUP // 2):
-                off_cos = offset[b, 0, at, :]
-                off_sin = offset[b, 1, at, :]
+            offs = [(offset[b, 0, at, :], offset[b, 1, at, :]) for b in range(2)]
+            bin_turn = add_angles(offs[1], (offs[0][0], -offs[0][1]))
+            for b in range(2, GROUP // 2):
+                offs.append(add_angles(offs[-1], bin_turn))
+            for b, (off_cos, off_sin) in enumerate(offs):
                 for h, (mid_cos, mid_sin) in enumerate(mids):
                     cc, ss = mid_cos * off_cos, mid_sin * off_sin
                     sc, cs = mid_sin * off_cos, mid_cos * off_sin
@@ -367,7 +369,7 @@
                     pltpu.VMEM((2, chan_dev, 2 * LANES), bf16),
                     pltpu.VMEM((2, 2, chan_dev // 2, LANES), f32),
                     pltpu.VMEM((GROUP, chan_dev, 2 * LANES), f32),
-                    pltpu.VMEM((GROUP // 2, 2, chan_dev // 2, LANES), f32),
+                    pltpu.VMEM((2, 2, chan_dev // 2, LANES), f32),
                     pltpu.VMEM((LANES // 4, LANES, 2 * LANES), bf16),
                 ],
                 cost_estimate=pl.CostEstimate(

time: 127 us -> 128 us (level)
  no operation moved by 1% of the time
where the time goes in v8:
time: 128 us; the launch traced here: 127 us
  waiting for transfers between devices  47.6 us (37%)
  starting transfers between devices  33.1 us (26%)
  Pallas kernels  29.7 us (23%)
  other arithmetic  13.2 us (10%)
  local copies, waits for them, and re-layouts  3.37 us (3%)
    pallas_call x2, Pallas kernels, per_device(): pl.pallas_call(functools.partial(sub_kernel, pair), out_shape=jax.ShapeDt...  22.6 us
    all_to_all x1, waiting for transfers between devices, per_device(): lax.all_to_all(blocks, 'freq', split_axis=0, concat_axis=0, tiled=True)  20.6 us
    all_to_all x1, waiting for transfers between devices, per_device(): spec = lax.all_to_all(spec, 'freq', split_axis=0, concat_axis=0, tiled=True)  16.3 us
    all_to_all x1, starting transfers between devices, per_device(): lax.all_to_all(blocks, 'freq', split_axis=0, concat_axis=0, tiled=True)  11.4 us
    ppermute x6, starting transfers between devices, per_device(): lax.ppermute(mine, 'band', [(j, j ^ half) for j in range(band_count)])  8.39 us
    cos x4, other arithmetic, turning(): return (jnp.cos(angle), jnp.sin(angle))  8.38 us
    ppermute x6, waiting for transfers between devices, per_device(): lax.ppermute(mine, 'band', [(j, j ^ half) for j in range(band_count)])  6.61 us
    all_to_all x1, starting transfers between devices, per_device(): spec = lax.all_to_all(spec, 'freq', split_axis=0, concat_axis=0, tiled=True)  6.37 us
  transfers between devices with their start and end apart: 10, of which 5 were waited for; matrix products, arithmetic and copies ran while one was open for 12% of the time, Pallas kernels for 11%

profile of v8, /device:TPU:32, one launch (start us, length us, event | category | flops | bytes accessed | tf_op | source)
XLA Modules:
  0.0 127.4 jit_solution(7965403394759422135)
XLA Ops:
  0.0 11.4 %all-to-all-start = ((f32[32,16,512]{2,1,0:T(8,128)}), f32[32,16,512]{2,1,0:T(8,128)S(1)}, u32[]{:S(2)}, u32[]{:S(2)}) async-start(f32[32,16,512]{2,1,0:T(8,128)} %bitcast.120), calls=%async_computation | async-start | bytes 2097152 | tf_op jit(solution)/shard_map/all_to_all | solution.py:345
  11.5 0.1 pad_add_fusion.2
  11.6 0.7 copy-done.6
  12.2 0.7 fusion.59
  13.0 1.4 %and_select_fusion.4 = (s32[1,128]{1,0:T(1,128)S(1)}, s32[1,128]{1,0:T(1,128)S(1)}) fusion(s32[]{:T(128)} %get-tuple-element.20, s32[]{:T(128)S(6)} %mul.354, s32[]{:T(128)} %get-tuple-element.19), kind=kLoop, calls=%fused_computation.179 | loop fusion | flops 7040 | bytes 1036 | tf_op jit(solution)/shard_map/jit(remainder)/select_n | solution.py:316
  14.3 0.1 pad_add_fusion.3
  14.4 1.3 and_select_fusion
  15.7 0.3 select_multiply_fusion.1
  16.1 0.3 fusion.52
  16.4 0.1 broadcast_multiply_fusion.1
  16.5 1.5 %fusion.20 = (f32[2,128,128]{2,1,0:T(8,128)S(1)}, f32[2,128,128]{2,1,0:T(8,128)S(1)}, f32[2,128,128]{2,1,0:T(8,128)S(1)}) fusion(s32[128,128]{1,0:T(8,128)S(1)} %slice_bitcast_fusion, s32[2]{0:T(128)S(1)} %iota_multiply_fusion.1, s32[128,128]{1,0:T(8,128)S(1)} %slice_bitcast_fusion.1, s32[128,128]{1,0:T(8,128)S(1)} %iota_multiply_fusion), kind=kLoop, calls=%fused_computation.58 | loop fusion | flops 1376256 | bytes 589832 | tf_op jit(solution)/shard_map/cos | solution.py:24
  18.0 20.6 %all-to-all-done = f32[32,16,512]{2,1,0:T(8,128)S(1)} async-done(((f32[32,16,512]{2,1,0:T(8,128)}), f32[32,16,512]{2,1,0:T(8,128)S(1)}, u32[]{:S(2)}, u32[]{:S(2)}) %all-to-all-start) | async-done | bytes 1048608 | tf_op jit(solution)/shard_map/all_to_all | solution.py:345
  38.6 3.0 %transform.1 = f32[2048,128]{1,0:T(8,128)} custom-call(f32[512,512]{1,0:T(8,128)S(1)} %bitcast.117, f32[256,128]{1,0:T(8,128)S(1)} %pad_maximum_fusion.1.first_ref, f32[2,128,128]{2,1,0:T(8,128)S(1)} %get-tuple-element.59.twist_ref, f32[128,256]{1,0:T(8,128)S(1)} %pad_maximum_fusion.2.second_ref), custom_call_target="tpu_custom_call" | custom-call | tf_op jit(solution)/shard_map/transform/pallas_call | solution.py:346
  41.6 6.4 %all-to-all-start.1 = ((f32[32,64,128]{2,1,0:T(8,128)}), f32[32,64,128]{2,1,0:T(8,128)S(1)}, u32[]{:S(2)}, u32[]{:S(2)}) async-start(f32[32,64,128]{2,1,0:T(8,128)} %bitcast.2), calls=%async_computation.1 | async-start | bytes 2097152 | tf_op jit(solution)/shard_map/all_to_all | solution.py:356
  48.0 0.7 slice.209
  48.7 0.7 slice.207
  49.4 0.1 copy.16
  49.5 0.6 copy-done.4
  50.1 0.1 copy.17
  50.2 0.1 copy.15
  50.3 0.2 select_reduce_fusion.profile_ref
  50.5 0.8 toeplitz.1.band_ref
  51.4 0.1 pad_add_fusion.4
  51.4 0.1 broadcast_multiply_fusion
  51.6 2.9 %fusion.2.tab_ref = f32[3,2,256,128]{3,2,1,0:T(8,128)S(1)} fusion(s32[2]{0:T(128)S(1)} %iota_multiply_fusion.2, s32[3,256,128]{2,1,0:T(8,128)S(1)} %broadcast_multiply_fusion), kind=kLoop, calls=%fused_computation.7 | loop fusion | flops 2752512 | bytes 1179656 | tf_op jit(solution)/shard_map/cos | solution.py:24
  54.5 3.7 %fusion.9 = (f32[3,2,128,128]{3,2,1,0:T(8,128)S(1)}, f32[3,2,128,128]{3,2,1,0:T(8,128)}) fusion(s32[3,128,128]{2,1,0:T(8,128)S(1)} %copy-done.1, s32[2]{0:T(128)S(1)} %iota_multiply_fusion.1, s32[3,128,128]{2,1,0:T(8,128)S(1)} %copy-done.2), kind=kLoop, calls=%fused_computation.24 | loop fusion | flops 2752512 | bytes 1179656 | tf_op jit(solution)/shard_map/cos | solution.py:24
  58.2 16.3 %all-to-all-done.1 = f32[32,64,128]{2,1,0:T(8,128)S(1)} async-done(((f32[32,64,128]{2,1,0:T(8,128)}), f32[32,64,128]{2,1,0:T(8,128)S(1)}, u32[]{:S(2)}, u32[]{:S(2)}) %all-to-all-start.1) | async-done | bytes 1048608 | tf_op jit(solution)/shard_map/all_to_all | solution.py:356
  74.5 11.3 %subband.2 = f32[2,128,128]{2,1,0:T(8,128)S(1)} custom-call(f32[32,4,16,128]{3,2,1,0:T(8,128)S(1)} %bitcast.118, f32[3,2,256,128]{3,2,1,0:T(8,128)S(1)} %fusion.2.tab_ref, f32[2,128,128]{2,1,0:T(8,128)S(1)} %get-tuple-element.14.tw_ref), custom_call_target="tpu_custom_call" | custom-call | flops 10000000000 | bytes 8388608 | tf_op jit(solution)/shard_map/subband/pallas_call | solution.py:363
  85.8 0.2 collective-permute-start
  86.0 11.3 %subband.3 = f32[2,128,128]{2,1,0:T(8,128)S(1)} custom-call(f32[32,4,16,128]{3,2,1,0:T(8,128)S(1)} %bitcast.119, f32[3,2,256,128]{3,2,1,0:T(8,128)S(1)} %fusion.2.tab_ref, f32[2,128,128]{2,1,0:T(8,128)S(1)} %get-tuple-element.16.tw_ref), custom_call_target="tpu_custom_call" | custom-call | flops 10000000000 | bytes 8388608 | tf_op jit(solution)/shard_map/subband/pallas_call | solution.py:363
  97.3 0.5 collective-permute-start.5
  97.9 0.0 collective-permute-done
  97.9 0.4 copy-done
  98.4 1.6 %collective-permute-start.1 = (f32[2,128,128]{2,1,0:T(8,128)S(1)}, f32[2,128,128]{2,1,0:T(8,128)S(1)}, u32[]{:S(2)}, u32[]{:S(2)}) collective-permute-start(f32[2,128,128]{2,1,0:T(8,128)S(1)} %pad_maximum_fusion.3), channel_id=1, source_target_pairs={{0,64},{32,96},{64,0},{96,32},{128,192},{160,224},{192,128},{224,1... | collective-permute-start | bytes 393224 | tf_op jit(solution)/shard_map/ppermute | solution.py:387
  99.9 0.0 collective-permute-done.5
  100.0 0.6 collective-permute-start.6
  100.7 4.1 %collective-permute-done.1 = f32[2,128,128]{2,1,0:T(8,128)S(1)} collective-permute-done((f32[2,128,128]{2,1,0:T(8,128)S(1)}, f32[2,128,128]{2,1,0:T(8,128)S(1)}, u32[]{:S(2)}, u32[]{:S(2)}) %collective-permute-start.1) | collective-permute-done | bytes 131104 | tf_op jit(solution)/shard_map/ppermute | solution.py:387
  104.8 3.1 %collective-permute-start.2 = (f32[2,128,128]{2,1,0:T(8,128)S(1)}, f32[2,128,128]{2,1,0:T(8,128)S(1)}, u32[]{:S(2)}, u32[]{:S(2)}) collective-permute-start(f32[2,128,128]{2,1,0:T(8,128)S(1)} %pad_maximum_fusion.4), channel_id=1, source_target_pairs={{0,128},{32,160},{64,192},{96,224},{128,0},{160,32},{192,64},{224,... | collective-permute-start | bytes 393224 | tf_op jit(solution)/shard_map/ppermute | solution.py:387
  107.9 0.0 collective-permute-done.6
  108.0 2.3 %collective-permute-start.7 = (f32[2,128,128]{2,1,0:T(8,128)S(1)}, f32[2,128,128]{2,1,0:T(8,128)S(1)}, u32[]{:S(2)}, u32[]{:S(2)}) collective-permute-start(f32[2,128,128]{2,1,0:T(8,128)S(1)} %pad_maximum_fusion.6), channel_id=1, source_target_pairs={{0,128},{32,160},{64,192},{96,224},{128,0},{160,32},{192,64},{224,... | collective-permute-start | bytes 393224 | tf_op jit(solution)/shard_map/ppermute | solution.py:387
  110.3 2.5 %collective-permute-done.2 = f32[2,128,128]{2,1,0:T(8,128)S(1)} collective-permute-done((f32[2,128,128]{2,1,0:T(8,128)S(1)}, f32[2,128,128]{2,1,0:T(8,128)S(1)}, u32[]{:S(2)}, u32[]{:S(2)}) %collective-permute-start.2) | collective-permute-done | bytes 131104 | tf_op jit(solution)/shard_map/ppermute | solution.py:387
  112.9 5.1 %collective-permute-start.4 = (f32[2,32,128]{2,1,0:T(8,128)S(1)}, f32[2,32,128]{2,1,0:T(8,128)S(1)}, u32[]{:S(2)}, u32[]{:S(2)}) collective-permute-start(f32[2,32,128]{2,1,0:T(8,128)S(1)} %get-tuple-element.47), channel_id=1, source_target_pairs={{1,0},{2,1},{3,2},{4,3},{5,4},{6,5},{7,6},{8,7},{9,8},{10,9},{11,1... | collective-permute-start | bytes 98312 | tf_op jit(solution)/shard_map/ppermute | solution.py:400
  118.0 1.9 %collective-permute-start.3 = (f32[2,32,128]{2,1,0:T(8,128)S(1)}, f32[2,32,128]{2,1,0:T(8,128)S(1)}, u32[]{:S(2)}, u32[]{:S(2)}) collective-permute-start(f32[2,32,128]{2,1,0:T(8,128)S(1)} %get-tuple-element.48), channel_id=1, source_target_pairs={{0,1},{1,2},{2,3},{3,4},{4,5},{5,6},{6,7},{7,8},{8,9},{9,10},{10,1... | collective-permute-start | bytes 98312 | tf_op jit(solution)/shard_map/ppermute | solution.py:397
  120.0 0.0 collective-permute-done.7
  120.1 1.8 %inner_bins.1.inner_ref = f32[192,128]{1,0:T(8,128)S(1)} custom-call(f32[2,128,128]{2,1,0:T(8,128)S(1)} %pad_maximum_fusion.outer_ref, f32[2,128,128]{2,1,0:T(8,128)S(1)} %pad_maximum_fusion.7.mid_ref, bf16[2048,256]{1,0:T(8,128)(2,1)S(1)} %toeplitz.1.band_ref), custom_call_target="tpu_custom_call" | custom-call | flops 2000000000 | bytes 2097152 | tf_op jit(solution)/shard_map/inner_bins/pallas_call | solution.py:401
  121.9 0.0 collective-permute-done.4.right_ref
  121.9 4.1 %collective-permute-done.3.left_ref = f32[2,32,128]{2,1,0:T(8,128)S(1)} collective-permute-done((f32[2,32,128]{2,1,0:T(8,128)S(1)}, f32[2,32,128]{2,1,0:T(8,128)S(1)}, u32[]{:S(2)}, u32[]{:S(2)}) %collective-permute-start.3) | collective-permute-done | bytes 32800 | tf_op jit(solution)/shard_map/ppermute | solution.py:397
  126.0 1.5 %edge_bins.1 = f32[128,256]{1,0:T(8,128)} custom-call(f32[2,32,128]{2,1,0:T(8,128)S(1)} %collective-permute-done.3.left_ref, f32[2,128,128]{2,1,0:T(8,128)S(1)} %pad_maximum_fusion.outer_ref, f32[2,32,128]{2,1,0:T(8,128)S(1)} %collective-permute-done.4.right_ref, f32[192,128]{1,0:T(8,128)S(1)} %inner_bins.1.inner_ref, bf16[2048,256]{1,0:T(8,128)(2,1)S(1)} %toeplitz.1.band_ref), custom_call_target="tpu_custom_call" | custom-call | tf_op jit(solution)/shard_map/edge_bins/pallas_call | solution.py:410
  (46 shorter events, 0.5 us)
Async XLA Ops:
  0.0 38.6 %all-to-all-start = ((f32[32,16,512]{2,1,0:T(8,128)}), f32[32,16,512]{2,1,0:T(8,128)S(1)}, u32[]{:S(2)}, u32[]{:S(2)}) async-start(f32[32,16,512]{2,1,0:T(8,128)} %bitcast.120), calls=%async_computation | async-start | bytes 2097152 | tf_op jit(solution)/shard_map/all_to_all | solution.py:345
  11.6 0.7 copy-start.6
  41.6 32.8 %all-to-all-start.1 = ((f32[32,64,128]{2,1,0:T(8,128)}), f32[32,64,128]{2,1,0:T(8,128)S(1)}, u32[]{:S(2)}, u32[]{:S(2)}) async-start(f32[32,64,128]{2,1,0:T(8,128)} %bitcast.2), calls=%async_computation.1 | async-start | bytes 2097152 | tf_op jit(solution)/shard_map/all_to_all | solution.py:356
  48.7 0.7 copy-start.5
  48.7 1.5 %copy-start.3 = (s32[512,64]{0,1:T(8,128)S(1)}, s32[512,64]{0,1:T(8,128)}, u32[]{:S(2)}) copy-start(s32[512,64]{0,1:T(8,128)} %param.12) | copy-start | bytes 393220
  49.4 0.7 copy-start.4
  51.5 2.9 %copy-start.1 = (s32[3,128,128]{2,1,0:T(8,128)S(1)}, s32[3,128,128]{2,1,0:T(8,128)}, u32[]{:S(2)}) copy-start(s32[3,128,128]{2,1,0:T(8,128)} %slice.209) | copy-start | bytes 589828
  51.6 2.9 %copy-start.2 = (s32[3,128,128]{2,1,0:T(8,128)S(1)}, s32[3,128,128]{2,1,0:T(8,128)}, u32[]{:S(2)}) copy-start(s32[3,128,128]{2,1,0:T(8,128)} %slice.207) | copy-start | bytes 589828
  85.8 12.1 %collective-permute-start = (f32[2,128,128]{2,1,0:T(8,128)S(1)}, f32[2,128,128]{2,1,0:T(8,128)S(1)}, u32[]{:S(2)}, u32[]{:S(2)}) collective-permute-start(f32[2,128,128]{2,1,0:T(8,128)S(1)} %subband.2), channel_id=1, source_target_pairs={{0,32},{32,0},{64,96},{96,64},{128,160},{160,128},{192,224},{224,1... | collective-permute-start | bytes 393224 | tf_op jit(solution)/shard_map/ppermute | solution.py:387
  97.3 1.0 copy-start
  97.3 2.6 %collective-permute-start.5 = (f32[2,128,128]{2,1,0:T(8,128)S(1)}, f32[2,128,128]{2,1,0:T(8,128)S(1)}, u32[]{:S(2)}, u32[]{:S(2)}) collective-permute-start(f32[2,128,128]{2,1,0:T(8,128)S(1)} %subband.3), channel_id=1, source_target_pairs={{0,32},{32,0},{64,96},{96,64},{128,160},{160,128},{192,224},{224,1... | collective-permute-start | bytes 393224 | tf_op jit(solution)/shard_map/ppermute | solution.py:387
  98.4 6.4 %collective-permute-start.1 = (f32[2,128,128]{2,1,0:T(8,128)S(1)}, f32[2,128,128]{2,1,0:T(8,128)S(1)}, u32[]{:S(2)}, u32[]{:S(2)}) collective-permute-start(f32[2,128,128]{2,1,0:T(8,128)S(1)} %pad_maximum_fusion.3), channel_id=1, source_target_pairs={{0,64},{32,96},{64,0},{96,32},{128,192},{160,224},{192,128},{224,1... | collective-permute-start | bytes 393224 | tf_op jit(solution)/shard_map/ppermute | solution.py:387
  100.0 7.9 %collective-permute-start.6 = (f32[2,128,128]{2,1,0:T(8,128)S(1)}, f32[2,128,128]{2,1,0:T(8,128)S(1)}, u32[]{:S(2)}, u32[]{:S(2)}) collective-permute-start(f32[2,128,128]{2,1,0:T(8,128)S(1)} %pad_maximum_fusion.5), channel_id=1, source_target_pairs={{0,64},{32,96},{64,0},{96,32},{128,192},{160,224},{192,128},{224,1... | collective-permute-start | bytes 393224 | tf_op jit(solution)/shard_map/ppermute | solution.py:387
  104.8 8.0 %collective-permute-start.2 = (f32[2,128,128]{2,1,0:T(8,128)S(1)}, f32[2,128,128]{2,1,0:T(8,128)S(1)}, u32[]{:S(2)}, u32[]{:S(2)}) collective-permute-start(f32[2,128,128]{2,1,0:T(8,128)S(1)} %pad_maximum_fusion.4), channel_id=1, source_target_pairs={{0,128},{32,160},{64,192},{96,224},{128,0},{160,32},{192,64},{224,... | collective-permute-start | bytes 393224 | tf_op jit(solution)/shard_map/ppermute | solution.py:387
  108.0 12.0 %collective-permute-start.7 = (f32[2,128,128]{2,1,0:T(8,128)S(1)}, f32[2,128,128]{2,1,0:T(8,128)S(1)}, u32[]{:S(2)}, u32[]{:S(2)}) collective-permute-start(f32[2,128,128]{2,1,0:T(8,128)S(1)} %pad_maximum_fusion.6), channel_id=1, source_target_pairs={{0,128},{32,160},{64,192},{96,224},{128,0},{160,32},{192,64},{224,... | collective-permute-start | bytes 393224 | tf_op jit(solution)/shard_map/ppermute | solution.py:387
  112.9 9.0 %collective-permute-start.4 = (f32[2,32,128]{2,1,0:T(8,128)S(1)}, f32[2,32,128]{2,1,0:T(8,128)S(1)}, u32[]{:S(2)}, u32[]{:S(2)}) collective-permute-start(f32[2,32,128]{2,1,0:T(8,128)S(1)} %get-tuple-element.47), channel_id=1, source_target_pairs={{1,0},{2,1},{3,2},{4,3},{5,4},{6,5},{7,6},{8,7},{9,8},{10,9},{11,1... | collective-permute-start | bytes 98312 | tf_op jit(solution)/shard_map/ppermute | solution.py:400
  118.0 7.9 %collective-permute-start.3 = (f32[2,32,128]{2,1,0:T(8,128)S(1)}, f32[2,32,128]{2,1,0:T(8,128)S(1)}, u32[]{:S(2)}, u32[]{:S(2)}) collective-permute-start(f32[2,32,128]{2,1,0:T(8,128)S(1)} %get-tuple-element.48), channel_id=1, source_target_pairs={{0,1},{1,2},{2,3},{3,4},{4,5},{5,6},{6,7},{7,8},{8,9},{9,10},{10,1... | collective-permute-start | bytes 98312 | tf_op jit(solution)/shard_map/ppermute | solution.py:397
